TPU v7x, 32 devices: a whole 2x2x4 slice. The times are simulated.
32 devices in a mesh: blk: 16 (over z, y, core), rows: 2 (over x).
Axes of the slice: x: 2, y: 2, z: 4, core: 2. Of those that a mesh axis runs over, the one named last changes fastest.
Arguments:
- q_panel: bfloat16 [2, 512, 256], P('rows', 'blk'), may hold values from -6 to 6
- tiles: bfloat16 [16, 2, 20, 128, 128], P('blk', 'rows'), may hold values from -0.15625 to 0.15625
- tile_rows: int32 [16, 2, 20], P('blk', 'rows'), may hold values from 0 to 3
- tile_cols: int32 [16, 2, 20, 1], P('blk', 'rows'), may hold values from 0 to 3; in each aligned block of 20 rows (0 to 19, 20 to 39, ..., all dimensions but the last counted through in order) at most 7 rows name the same one
- tile_count: int32 [16, 2], P('blk', 'rows'), may hold values from 10 to 20, as said below
- owner_map: int32 [16, 4], P('blk'), may hold values from 0 to 3, each once within a row
Outputs:
- y_basis: bfloat16 [16, 512, 256], P('blk', 'rows')
- z_basis: float32 [2, 512, 256], P('rows', 'blk')
Inputs may be any that keep to these rules, and one draw needn't show every extreme that they name: The live tiles of a device are its first tile_count slots; some device has all 20 live and some has 10. `tile_cols`: among the 20 slots of one device no column block appears more than 7 times. Each row of owner_map is a permutation; slot s belongs to the device with rows index s // 2.
All inputs are finite; a program needn't handle non-finite values.
Results may differ from a plain program's by a relative error of at most 0.0013.
Values may be sent and summed in bfloat16 or wider, within the bound.
No kernel may reach another device: no remote copies, remote signals or barrier semaphores. Data moves between devices by JAX's collectives and lax.ppermute only.
A program may use at most 64 MiB of HBM per device.

v0:
```python
import jax
import jax.numpy as jnp
from jax import lax
from jax.sharding import PartitionSpec as P


def shards(q_panel, tiles, tile_rows, tile_cols, tile_count, owner_map):
    panel_rows = q_panel.shape[1]
    tile_stack = tiles[0, 0]
    tile_total = tile_stack.shape[0]
    tile_size = tile_stack.shape[1]
    group_blocks = owner_map.shape[1]
    class_blocks = panel_rows * lax.axis_size("blk") // tile_size
    column_ids = tile_cols[0, 0, :, 0]
    active = jnp.arange(tile_total, dtype=jnp.int32) < tile_count[0, 0]
    slot_of_tile = owner_map[0][tile_rows[0, 0]]
    slot_hit = slot_of_tile[:, None] == jnp.arange(group_blocks, dtype=jnp.int32)[None, :]
    column_hit = column_ids[:, None] == jnp.arange(class_blocks, dtype=jnp.int32)[None, :]
    placing = (slot_hit[:, :, None] & column_hit[:, None, :] & active[:, None, None]).astype(
        tile_stack.dtype
    )
    local_matrix = jnp.einsum(
        "tsc,tik->sick", placing, tile_stack, preferred_element_type=jnp.float32
    )
    local_matrix = local_matrix.reshape(group_blocks * tile_size, class_blocks * tile_size)
    rows_in = lax.all_gather(q_panel, "blk", axis=1, tiled=True)[0]
    flat_partial = jnp.dot(
        local_matrix, rows_in.astype(jnp.float32), precision=lax.Precision.HIGHEST
    )
    owned = lax.psum_scatter(flat_partial, "rows", scatter_dimension=0, tiled=True)
    y_owned = owned.astype(jnp.bfloat16)
    y_group = lax.all_gather(y_owned, "rows", axis=0, tiled=True)
    column_term = lax.dot_general(
        local_matrix,
        y_group.astype(jnp.float32),
        (((0,), (0,)), ((), ())),
        precision=lax.Precision.HIGHEST,
    )
    z_share = lax.psum_scatter(column_term, "blk", scatter_dimension=0, tiled=True)
    return (y_owned[None], z_share[None])


def solution(mesh):
    placed = (
        P("rows", "blk", None),
        P("blk", "rows", None, None, None),
        P("blk", "rows", None),
        P("blk", "rows", None, None),
        P("blk", "rows"),
        P("blk", None),
    )
    return jax.shard_map(
        shards,
        mesh=mesh,
        in_specs=placed,
        out_specs=(P("blk", "rows", None), P("rows", "blk", None)),
        check_vma=False,
    )
```

profile of v0, /device:TPU:0, one launch (start us, length us, event | category | flops | bytes accessed | tf_op | source)
XLA Modules:
  0.0 123.7 jit_solution(16841095776658529970)
XLA Ops:
  7.2 0.0 reduce-scatter.3.cloned.1.call-start
  7.9 0.0 copy-start.1
  7.9 0.6 copy-done.1
  8.5 0.7 fusion.17
  9.2 24.0 %all_gather.6 = bf16[1,512,256]{2,1,0:T(8,128)(2,1)S(1)} all-gather(bf16[1,32,256]{2,1,0:T(8,128)(2,1)} %param.6), channel_id=1, replica_groups=mesh['blk'=16,'rows'=2] {'blk'}, dimensions={1}, use_global_device_ids=true | all-gather | bytes 278528 | tf_op jit(solution)/shard_map/all_gather | solution.py:26
  33.2 0.0 copy-start.2
  33.2 0.7 copy-done.2
  33.9 2.5 %fusion.16 = s32[20]{0:T(128)S(1)} fusion(s32[1,1,20]{2,1,0:T(1,128)S(1)} %copy-done.2, s32[]{:T(128)} %bitcast.1, s32[]{:T(128)} %bitcast.2, s32[]{:T(128)} %bitcast.4, s32[]{:T(128)} %bitcast.3), kind=kLoop, calls=%fused_computation.22 | loop fusion | flops 180 | bytes 176 | tf_op jit(solution)/shard_map/gather | solution.py:16
  36.4 0.0 copy-start.3
  36.4 0.6 copy-done.3
  37.1 1.7 %fusion.6 = f32[4,4,128,128]{3,1,2,0:T(4,128)S(1)} fusion(bf16[20,128,128]{2,1,0:T(8,128)(2,1)} %bitcast.37, pred[20]{0:T(512)(128)(4,1)S(1)} %iota_compare_fusion.2, pred[20,4]{0,1:T(4,128)(4,1)S(1)} %get-tuple-element.6, pred[20,4]{0,1:T(4,128)(4,1)S(1)} %get-tuple-element.7), kind=kOutput, calls=%fused_computation.6 | convolution fusion | flops 10486400 | bytes 1704116 | tf_op jit(solution)/shard_map/tsc,tik->sick/dot_general | solution.py:22
  38.8 1.4 %fusion.2 = f32[512,256]{1,0:T(8,128)} fusion(f32[64,8,4,128]{3,2,1,0:T(4,128)S(1)} %bitcast.35, bf16[1,512,256]{2,1,0:T(8,128)(2,1)S(1)} %all_gather.6), kind=kOutput, calls=%fused_computation.2 | convolution fusion | flops 805306368 | bytes 1835008 | tf_op jit(solution)/shard_map/dot_general | solution.py:27
  40.2 0.0 reduce-scatter.3.cloned.1.call-update
  40.2 0.0 reduce-scatter.5.cloned.1.call-start
  40.3 11.9 %reduce-scatter.3.cloned.1.call-done = f32[256,256]{1,0:T(8,128)} async-done(((f32[512,256]{1,0:T(8,128)}), f32[256,256]{1,0:T(8,128)}) %reduce-scatter.3.cloned.1.call-update) | async-done | bytes 262160 | tf_op jit(solution)/shard_map/reduce_scatter | solution.py:30
  52.2 1.0 convert_element_type.2
  53.2 5.9 %all_gather.7 = bf16[512,256]{1,0:T(8,128)(2,1)S(1)} all-gather(bf16[256,256]{1,0:T(8,128)(2,1)S(1)} %convert_element_type.2), channel_id=1, replica_groups=mesh['blk'=16,'rows'=2] {'rows'}, dimensions={0}, use_global_device_ids=true | all-gather | bytes 393216 | tf_op jit(solution)/shard_map/all_gather | solution.py:32
  59.1 1.8 %fusion = f32[512,256]{1,0:T(8,128)} fusion(bf16[512,256]{1,0:T(8,128)(2,1)S(1)} %all_gather.7, f32[64,8,4,128]{3,2,1,0:T(4,128)S(1)} %bitcast.36), kind=kOutput, calls=%fused_computation | convolution fusion | flops 805306368 | bytes 1835008 | tf_op jit(solution)/shard_map/dot_general | solution.py:33
  60.9 0.0 copy-start
  60.9 0.0 reduce-scatter.5.cloned.1.call-update
  60.9 0.9 copy-done
  61.9 0.7 convert_bitcast_fusion
  62.5 54.3 %reduce-scatter.5.cloned.1.call-done = f32[32,256]{1,0:T(8,128)} async-done(((f32[512,256]{1,0:T(8,128)}), f32[32,256]{1,0:T(8,128)}) %reduce-scatter.5.cloned.1.call-update) | async-done | bytes 32784 | tf_op jit(solution)/shard_map/reduce_scatter | solution.py:39
  (2 shorter events, 0.0 us)
Async XLA Ops:
  7.2 45.1 %reduce-scatter.3.cloned.1.call-start = ((), (), s32[]{:S(2)}) async-start(), calls=%async_computation.2 | async-start | bytes 786432 | tf_op jit(solution)/shard_map/reduce_scatter | solution.py:30
  7.9 0.7 copy-start.1
  33.2 0.7 copy-start.2
  36.4 0.7 copy-start.3
  40.2 76.6 %reduce-scatter.5.cloned.1.call-start = ((), (), s32[]{:S(2)}) async-start(), calls=%async_computation.3 | async-start | bytes 557056 | tf_op jit(solution)/shard_map/reduce_scatter | solution.py:39
  60.9 0.9 copy-start
Sparse Core Ops, SparseCore 0:
  40.4 11.8 reduce-scatter.2
  61.1 55.7 reduce-scatter.4
where the time goes:
time: 124 us
  waiting for transfers between devices  66.3 us (53%)
  blocking collectives  29.9 us (24%)
  between operations  14.7 us (12%)
  matrix products  4.93 us (4%)
  other arithmetic  4.19 us (3%)
  local copies, waits for them, and re-layouts  3.53 us (3%)
    reduce_scatter x1, waiting for transfers between devices, shards(): lax.psum_scatter(column_term, 'blk', scatter_dimension=0, tiled=True)  54.3 us
    all_gather x1, blocking collectives, shards(): rows_in = lax.all_gather(q_panel, 'blk', axis=1, tiled=True)[0]  24 us
    reduce_scatter x1, waiting for transfers between devices, shards(): lax.psum_scatter(flat_partial, 'rows', scatter_dimension=0, tiled=True)  11.9 us
    all_gather x1, blocking collectives, shards(): y_group = lax.all_gather(y_owned, 'rows', axis=0, tiled=True)  5.92 us
    unnamed x8, local copies, waits for them, and re-layouts  2.87 us
    gather x1, other arithmetic, shards(): slot_of_tile = owner_map[0][tile_rows[0, 0]]  2.55 us
  transfers between devices with their start and end apart: 2, of which 2 were waited for; matrix products, arithmetic and copies ran while one was open for 1% of the time, Pallas kernels for 0%

commit v1 on v0

--- a/solution.py
+++ b/solution.py
@@ -1,10 +1,193 @@
 import jax
 import jax.numpy as jnp
 from jax import lax
+from jax.experimental import pallas as pl
+from jax.experimental.pallas import tpu as pltpu
 from jax.sharding import PartitionSpec as P
 
 
-def shards(q_panel, tiles, tile_rows, tile_cols, tile_count, owner_map):
+def sides_of(chips):
+    sides = ([], [])
+    load = [0, 0]
+    for k in sorted(range(chips), key=lambda k: -(k // 2 + k % 2)):
+        open_sides = [c for c in range(2) if len(sides[c]) < chips // 2]
+        c = min(open_sides, key=lambda c: load[c])
+        sides[c].append(k)
+        load[c] += k // 2 + k % 2
+    return sides
+
+
+def block_kernel(rounds, sides, *refs):
+    direct, relayed = refs[:rounds], refs[rounds : 2 * rounds]
+    (own_tiles, far_tiles, own_rows, own_cols, own_count, owners, far_meta) = refs[
+        2 * rounds : 2 * rounds + 7
+    ]
+    outs = refs[2 * rounds + 7 :]
+    y_out, keep, give = outs[0], outs[1 : 1 + rounds], outs[1 + rounds : 1 + 2 * rounds]
+    near, far, own_a, far_a, y_all, z_all = outs[1 + 2 * rounds :]
+    total, size = own_tiles.shape[0], own_tiles.shape[1]
+    group = owners.shape[1]
+    shard = direct[0].shape[0] // 4
+    place = lax.axis_index("blk")
+    core, chip = lax.rem(place, 2), lax.div(place, 2)
+    half = lax.axis_index("rows")
+
+    def rows_of(which, side):
+        return pl.ds(pl.multiple_of(which * (2 * shard) + side * shard, shard), shard)
+
+    def chip_of(step, side):
+        return lax.bitwise_xor(chip, jnp.where(side == 0, sides[0][step], sides[1][step]))
+
+    for step in range(rounds):
+        for ref, side, first in (
+            (direct[step], core, core),
+            (relayed[step], 1 - core, 1 - core),
+        ):
+            which = chip_of(step, side)
+            near[rows_of(which, first), :] = ref[0:shard, :]
+            far[rows_of(which, first), :] = ref[shard : 2 * shard, :]
+            near[rows_of(which, 1 - first), :] = ref[2 * shard : 3 * shard, :]
+            far[rows_of(which, 1 - first), :] = ref[3 * shard : 4 * shard, :]
+
+    def place_tiles(a, tiles, row_at, col_at, count):
+        a[...] = jnp.zeros_like(a)
+
+        def add(t, carry):
+            rows = pl.ds(pl.multiple_of(row_at(t) * size, size), size)
+            cols = pl.ds(pl.multiple_of(col_at(t) * size, size), size)
+            a[rows, cols] = a[rows, cols] + tiles[t].astype(jnp.float32)
+            return carry
+
+        lax.fori_loop(0, count, add, 0)
+        high = a[...].astype(jnp.bfloat16)
+        low = (a[...] - high.astype(jnp.float32)).astype(jnp.bfloat16)
+        return high, low
+
+    own_high, own_low = place_tiles(
+        own_a, own_tiles, lambda t: own_rows[0, 0, t], lambda t: own_cols[0, t], own_count[0, 0]
+    )
+    far_high, far_low = place_tiles(
+        far_a,
+        far_tiles,
+        lambda t: far_meta[0, t],
+        lambda t: far_meta[0, total + t],
+        far_meta[0, 2 * total],
+    )
+
+    def dot(a, b):
+        return jnp.dot(a, b, preferred_element_type=jnp.float32)
+
+    q_near, q_far = near[...], far[...]
+    y = (dot(own_high, q_near) + dot(far_high, q_far)) + (
+        dot(own_low, q_near) + dot(far_low, q_far)
+    )
+    y16 = y.astype(jnp.bfloat16)
+    y_all[...] = y16
+    mine = group // 2
+    for k in range(group):
+        slot = owners[0, k]
+
+        @pl.when(lax.div(slot, mine) == half)
+        def _():
+            at = pl.multiple_of(lax.rem(slot, mine) * size, size)
+            y_out[pl.ds(at, size), :] = y_all[k * size : (k + 1) * size, :]
+
+    def turned(a, b):
+        return lax.dot_general(
+            a, b, (((0,), (0,)), ((), ())), preferred_element_type=jnp.float32
+        )
+
+    z_all[...] = turned(own_high, y16) + turned(own_low, y16)
+    for step in range(rounds):
+        for ref, side, first in (
+            (keep[step], core, core),
+            (give[step], 1 - core, 1 - core),
+        ):
+            which = chip_of(step, side)
+            ref[0:shard, :] = z_all[rows_of(which, first), :]
+            ref[shard : 2 * shard, :] = z_all[rows_of(which, 1 - first), :]
+
+
+def paired(q_panel, tiles, tile_rows, tile_cols, tile_count, owner_map):
+    devices = lax.axis_size("blk")
+    chips = devices // 2
+    rounds = chips // 2
+    sides = sides_of(chips)
+    shard, rank = q_panel.shape[1:]
+    stack = tiles[0, 0]
+    total, size = stack.shape[:2]
+    group = owner_map.shape[1]
+    cols = tile_cols.reshape(1, total)
+
+    across = [(0, 1), (1, 0)]
+    sibling = [(i, i ^ 1) for i in range(devices)]
+
+    def to_chips(step):
+        return [
+            (2 * m + c, 2 * (m ^ sides[c][step]) + c)
+            for m in range(chips)
+            for c in range(2)
+        ]
+
+    order = tuple(range(rounds))
+
+    q_own = q_panel[0]
+    q_far = lax.ppermute(q_own, "rows", across)
+    stack, q_far = lax.optimization_barrier((stack, q_far))
+    far_tiles = lax.ppermute(stack, "rows", across)
+    meta = jnp.concatenate(
+        [tile_rows.reshape(1, total), cols, tile_count.reshape(1, 1)], axis=1
+    )
+    far_meta = lax.ppermute(meta, "rows", across)
+    pair = jnp.concatenate([q_own, q_far], axis=0)
+    block = jnp.concatenate([pair, lax.ppermute(pair, "blk", sibling)], axis=0)
+    direct, relayed = [None] * rounds, [None] * rounds
+    for step in order:
+        direct[step] = lax.ppermute(block, "blk", to_chips(step))
+    for step in order:
+        relayed[step] = lax.ppermute(direct[step], "blk", sibling)
+
+    vmem = pl.BlockSpec(memory_space=pltpu.VMEM)
+    smem = pl.BlockSpec(memory_space=pltpu.SMEM)
+    width = devices * shard
+    height = group * size
+    piece = jax.ShapeDtypeStruct((2 * shard, rank), jnp.float32)
+
+    def body(*refs):
+        block_kernel(rounds, sides, *refs)
+
+    made = pl.pallas_call(
+        body,
+        out_shape=[jax.ShapeDtypeStruct((height // 2, rank), jnp.bfloat16)]
+        + [piece] * (2 * rounds),
+        in_specs=[vmem] * (2 * rounds + 2) + [smem] * 5,
+        out_specs=[vmem] * (1 + 2 * rounds),
+        scratch_shapes=[
+            pltpu.VMEM((width, rank), jnp.bfloat16),
+            pltpu.VMEM((width, rank), jnp.bfloat16),
+            pltpu.VMEM((height, width), jnp.float32),
+            pltpu.VMEM((height, width), jnp.float32),
+            pltpu.VMEM((height, rank), jnp.bfloat16),
+            pltpu.VMEM((width, rank), jnp.float32),
+        ],
+        compiler_params=pltpu.CompilerParams(vmem_limit_bytes=24 << 20),
+        name="block_products",
+    )(*direct, *relayed, stack, far_tiles, tile_rows, cols, tile_count, owner_map, far_meta)
+    y_owned, keep, give = made[0], made[1 : 1 + rounds], made[1 + rounds :]
+    came = [None] * rounds
+    for step in order:
+        came[step] = lax.ppermute(give[step], "blk", sibling)
+    arrived = [None] * rounds
+    for step in order:
+        arrived[step] = lax.ppermute(keep[step] + came[step], "blk", to_chips(step))
+    summed = arrived[0]
+    for step in range(1, rounds):
+        summed = summed + arrived[step]
+    z_share = summed[:shard] + lax.ppermute(summed[shard:], "blk", sibling)
+    return (y_owned[None], z_share[None])
+
+
+def general(q_panel, tiles, tile_rows, tile_cols, tile_count, owner_map):
     panel_rows = q_panel.shape[1]
     tile_stack = tiles[0, 0]
     tile_total = tile_stack.shape[0]
@@ -49,8 +232,10 @@
         P("blk", "rows"),
         P("blk", None),
     )
+    devices = mesh.shape["blk"]
+    fits = mesh.shape["rows"] == 2 and devices >= 4 and devices & (devices - 1) == 0
     return jax.shard_map(
-        shards,
+        paired if fits else general,
         mesh=mesh,
         in_specs=placed,
         out_specs=(P("blk", "rows", None), P("rows", "blk", None)),

time: 124 us -> 48.9 us (0.39)
  waiting for transfers between devices: 66.3 us -> 16.7 us
  blocking collectives: 29.9 us -> 0 us
  starting transfers between devices: 0.08 us -> 24.2 us
  between operations: 14.7 us -> 1.42 us
  matrix products: 4.93 us -> 0 us
  Pallas kernels: 0 us -> 3.08 us
  other arithmetic: 4.19 us -> 1.54 us
  local copies, waits for them, and re-layouts: 3.53 us -> 1.76 us
    reduce_scatter x2 -> x0, waiting for transfers between devices: 66.2 us -> none  [the longest x1 54.3 us: shards(): lax.psum_scatter(column_term, 'blk', scatter_dimension=0, tiled=True)]
    all_gather x2 -> x0, blocking collectives: 29.9 us -> none  [the longest x1 24 us: shards(): rows_in = lax.all_gather(q_panel, 'blk', axis=1, tiled=True)[0]]
    ppermute x0 -> x21, starting transfers between devices: none -> 24.2 us  [the longest x4 11.1 us: paired(): direct[step] = lax.ppermute(block, 'blk', to_chips(step))]
    ppermute x0 -> x21, waiting for transfers between devices: none -> 16.7 us  [the longest x4 5.08 us: paired(): arrived[step] = lax.ppermute(keep[step] + came[step], 'blk', to_chips(step))]
    dot_general x3 -> x0, matrix products: 4.93 us -> none  [the longest x1 1.79 us: shards(): lax.dot_general(local_matrix, y_group.astype(jnp.float32), (((0,), (0,)),...]
    pallas_call x0 -> x1, Pallas kernels: none -> 3.08 us  [paired(): pl.pallas_call(body, out_shape=[jax.ShapeDtypeStruct((height // 2, rank),...]
    gather x1 -> x0, other arithmetic: 2.55 us -> none  [shards(): slot_of_tile = owner_map[0][tile_rows[0, 0]]]
    unnamed x8 -> x10, local copies, waits for them, and re-layouts: 2.87 us -> 1.76 us
  transfers between devices with their start and end apart: 2 -> 21, of which waited for: 2 -> 9; matrix products, arithmetic and copies ran while one was open for 1% -> 2% of each run, Pallas kernels for 0% -> 0%
where the time goes in v1:
time: 48.9 us; the launch traced here: 48.7 us
  starting transfers between devices  24.2 us (49%)
  waiting for transfers between devices  16.7 us (34%)
  Pallas kernels  3.08 us (6%)
  local copies, waits for them, and re-layouts  1.76 us (4%)
  other arithmetic  1.54 us (3%)
  between operations  1.42 us (3%)
    ppermute x4, starting transfers between devices, paired(): direct[step] = lax.ppermute(block, 'blk', to_chips(step))  11.1 us
    ppermute x4, starting transfers between devices, paired(): arrived[step] = lax.ppermute(keep[step] + came[step], 'blk', to_chips(step))  6.25 us
    ppermute x4, waiting for transfers between devices, paired(): arrived[step] = lax.ppermute(keep[step] + came[step], 'blk', to_chips(step))  5.08 us
    ppermute x1, waiting for transfers between devices, paired(): far_meta = lax.ppermute(meta, 'rows', across)  4.8 us
    pallas_call x1, Pallas kernels, paired(): pl.pallas_call(body, out_shape=[jax.ShapeDtypeStruct((height // 2, rank),...  3.08 us
    ppermute x1, starting transfers between devices, paired(): q_far = lax.ppermute(q_own, 'rows', across)  3 us
    ppermute x1, starting transfers between devices, paired(): far_tiles = lax.ppermute(stack, 'rows', across)  2.02 us
    ppermute x1, waiting for transfers between devices, paired(): q_far = lax.ppermute(q_own, 'rows', across)  1.93 us
  transfers between devices with their start and end apart: 21, of which 9 were waited for; matrix products, arithmetic and copies ran while one was open for 2% of the time, Pallas kernels for 0%

profile of v1, /device:TPU:0, one launch (start us, length us, event | category | flops | bytes accessed | tf_op | source)
XLA Modules:
  0.0 48.7 jit_solution(15117538788861416936)
XLA Ops:
  0.6 3.0 %collective-permute-start = (bf16[32,256]{1,0:T(8,128)(2,1)}, bf16[32,256]{1,0:T(8,128)(2,1)S(1)}, u32[]{:S(2)}, u32[]{:S(2)}) collective-permute-start(bf16[32,256]{1,0:T(8,128)(2,1)} %bitcast.12), channel_id=1, source_target_pairs={{0,1},{1,0},{2,3},{3,2},{4,5},{5,4},{6,7},{7,6},{8,9},{9,8},{10,11... | collective-permute-start | bytes 49160 | tf_op jit(solution)/shard_map/ppermute | solution.py:135
  3.6 1.9 %collective-permute-done = bf16[32,256]{1,0:T(8,128)(2,1)S(1)} collective-permute-done((bf16[32,256]{1,0:T(8,128)(2,1)}, bf16[32,256]{1,0:T(8,128)(2,1)S(1)}, u32[]{:S(2)}, u32[]{:S(2)}) %collective-permute-start) | collective-permute-done | bytes 16416 | tf_op jit(solution)/shard_map/ppermute | solution.py:135
  5.6 2.0 %collective-permute-start.10 = (bf16[20,128,128]{2,1,0:T(8,128)(2,1)}, bf16[20,128,128]{2,1,0:T(8,128)(2,1)S(1)}, u32[]{:S(2)}, u32[]{:S(2)}) collective-permute-start(bf16[20,128,128]{2,1,0:T(8,128)(2,1)} %bitcast.7), channel_id=1, source_target_pairs={{0,1},{1,0},{2,3},{3,2},{4,5},{5,4},{6,7},{7,6},{8,9},{9,8},{10,11... | collective-permute-start | bytes 1966088 | tf_op jit(solution)/shard_map/ppermute | solution.py:137
  8.2 0.8 %pad_maximum_fusion.1 = bf16[64,256]{1,0:T(8,128)(2,1)S(1)} fusion(bf16[32,256]{1,0:T(8,128)(2,1)S(1)} %collective-permute-done, bf16[32,256]{1,0:T(8,128)(2,1)} %bitcast.13), kind=kLoop, calls=%fused_computation.4 | loop fusion | flops 65536 | bytes 65536 | tf_op jit(solution)/shard_map/concatenate | solution.py:142
  9.0 0.0 collective-permute-start.1
  9.0 0.6 %copy-done.1 = s32[1,1,20]{2,1,0:T(1,128)S(1)} copy-done((s32[1,1,20]{2,1,0:T(1,128)S(1)}, s32[1,1,20]{2,1,0:T(1,128)}, u32[]{:S(2)}) %copy-start.1) | copy-done | bytes 104
  9.7 0.0 copy-done.2
  9.7 0.1 pad_add_fusion
  9.8 0.5 collective-permute-done.1
  10.2 0.7 %collective-permute-start.5 = (bf16[128,256]{1,0:T(8,128)(2,1)S(1)}, bf16[128,256]{1,0:T(8,128)(2,1)S(1)}, u32[]{:S(2)}, u32[]{:S(2)}) collective-permute-start(bf16[128,256]{1,0:T(8,128)(2,1)S(1)} %pad_maximum_fusion), channel_id=1, source_target_pairs={{0,0},{2,10},{4,4},{6,14},{8,8},{10,2},{12,12},{14,6},{16,16},{18,... | collective-permute-start | bytes 196616 | tf_op jit(solution)/shard_map/ppermute | solution.py:146
  10.9 0.1 collective-permute-start.11
  11.0 3.1 %collective-permute-start.4 = (bf16[128,256]{1,0:T(8,128)(2,1)S(1)}, bf16[128,256]{1,0:T(8,128)(2,1)S(1)}, u32[]{:S(2)}, u32[]{:S(2)}) collective-permute-start(bf16[128,256]{1,0:T(8,128)(2,1)S(1)} %pad_maximum_fusion), channel_id=1, source_target_pairs={{0,16},{2,6},{4,20},{6,2},{8,24},{10,14},{12,28},{14,10},{16,0},{1... | collective-permute-start | bytes 196616 | tf_op jit(solution)/shard_map/ppermute | solution.py:146
  14.1 2.5 %collective-permute-start.3 = (bf16[128,256]{1,0:T(8,128)(2,1)S(1)}, bf16[128,256]{1,0:T(8,128)(2,1)S(1)}, u32[]{:S(2)}, u32[]{:S(2)}) collective-permute-start(bf16[128,256]{1,0:T(8,128)(2,1)S(1)} %pad_maximum_fusion), channel_id=1, source_target_pairs={{0,12},{2,26},{4,8},{6,30},{8,4},{10,18},{12,0},{14,22},{16,28},{1... | collective-permute-start | bytes 196616 | tf_op jit(solution)/shard_map/ppermute | solution.py:146
  16.6 4.8 %collective-permute-done.11.refs_14_ = s32[1,41]{1,0:T(1,128)S(1)} collective-permute-done((s32[1,41]{1,0:T(1,128)S(1)}, s32[1,41]{1,0:T(1,128)S(1)}, u32[]{:S(2)}, u32[]{:S(2)}) %collective-permute-start.11) | collective-permute-done | bytes 196 | tf_op jit(solution)/shard_map/ppermute | solution.py:141
  21.4 4.8 %collective-permute-start.2 = (bf16[128,256]{1,0:T(8,128)(2,1)S(1)}, bf16[128,256]{1,0:T(8,128)(2,1)S(1)}, u32[]{:S(2)}, u32[]{:S(2)}) collective-permute-start(bf16[128,256]{1,0:T(8,128)(2,1)S(1)} %pad_maximum_fusion), channel_id=1, source_target_pairs={{0,28},{2,22},{4,24},{6,18},{8,20},{10,30},{12,16},{14,26},{16,12}... | collective-permute-start | bytes 196616 | tf_op jit(solution)/shard_map/ppermute | solution.py:146
  26.2 0.0 collective-permute-done.5.refs_3_
  26.3 0.0 collective-permute-start.9
  26.3 0.0 collective-permute-done.4.refs_2_
  26.3 0.5 %collective-permute-start.8 = (bf16[128,256]{1,0:T(8,128)(2,1)S(1)}, bf16[128,256]{1,0:T(8,128)(2,1)S(1)}, u32[]{:S(2)}, u32[]{:S(2)}) collective-permute-start(bf16[128,256]{1,0:T(8,128)(2,1)S(1)} %collective-permute-done.4.refs_2_), channel_id=1, source_target_pairs={{0,2},{2,0},{4,6},{6,4},{8,10},{10,8},{12,14},{14,12},{16,18},{18,... | collective-permute-start | bytes 196616 | tf_op jit(solution)/shard_map/ppermute | solution.py:148
  26.8 0.0 collective-permute-done.3.refs_1_
  26.8 0.1 collective-permute-start.7
  26.8 1.7 %collective-permute-done.2.refs_0_ = bf16[128,256]{1,0:T(8,128)(2,1)S(1)} collective-permute-done((bf16[128,256]{1,0:T(8,128)(2,1)S(1)}, bf16[128,256]{1,0:T(8,128)(2,1)S(1)}, u32[]{:S(2)}, u32[]{:S(2)}) %collective-permute-start.2) | collective-permute-done | bytes 65568 | tf_op jit(solution)/shard_map/ppermute | solution.py:146
  28.6 0.0 collective-permute-start.6
  28.6 0.0 collective-permute-done.9.refs_7_
  28.6 0.0 collective-permute-done.8.refs_6_
  28.6 0.0 collective-permute-done.7.refs_5_
  28.6 1.2 %collective-permute-done.6.refs_4_ = bf16[128,256]{1,0:T(8,128)(2,1)S(1)} collective-permute-done((bf16[128,256]{1,0:T(8,128)(2,1)S(1)}, bf16[128,256]{1,0:T(8,128)(2,1)S(1)}, u32[]{:S(2)}, u32[]{:S(2)}) %collective-permute-start.6) | collective-permute-done | bytes 65568 | tf_op jit(solution)/shard_map/ppermute | solution.py:148
  29.8 0.0 collective-permute-done.10.refs_9_
  29.8 1.1 %copy-done = bf16[1,1,20,128,128]{4,3,2,1,0:T(8,128)(2,1)S(1)} copy-done((bf16[1,1,20,128,128]{4,3,2,1,0:T(8,128)(2,1)S(1)}, bf16[1,1,20,128,128]{4,3,2,1,0:T(8,128)(2,1)}, u32[]{:S(2)}) %copy-start) | copy-done | bytes 655384
  30.9 3.1 %block_products.1 = (bf16[256,256]{1,0:T(8,128)(2,1)}, f32[64,256]{1,0:T(8,128)S(1)}, f32[64,256]{1,0:T(8,128)S(1)}, f32[64,256]{1,0:T(8,128)S(1)}, f32[64,256]{...) custom-call(bf16[128,256]{1,0:T(8,128)(2,1)S(1)} %collective-permute, ...), custom_call_target="tpu_custom_call" | custom-call | tf_op jit(solution)/shard_map/block_products/pallas_call | solution.py:159
  34.0 0.4 collective-permute-start.12
  34.4 0.2 collective-permute-start.14
  34.6 0.4 collective-permute-start.16
  34.9 0.2 collective-permute-start.18
  35.1 0.2 collective-permute-done.12
  35.3 4.8 %collective-permute-start.13 = (f32[64,256]{1,0:T(8,128)S(1)}, f32[64,256]{1,0:T(8,128)S(1)}, u32[]{:S(2)}, u32[]{:S(2)}) collective-permute-start(f32[64,256]{1,0:T(8,128)S(1)} %add.24), channel_id=1, source_target_pairs={{0,28},{2,22},{4,24},{6,18},{8,20},{10,30},{12,16},{14,26},{16,12}... | collective-permute-start | bytes 196616 | tf_op jit(solution)/shard_map/ppermute | solution.py:182
  40.2 0.0 collective-permute-done.14
  40.2 0.1 collective-permute-start.15
  40.3 0.0 collective-permute-done.16
  40.3 0.7 %collective-permute-start.17 = (f32[64,256]{1,0:T(8,128)S(1)}, f32[64,256]{1,0:T(8,128)S(1)}, u32[]{:S(2)}, u32[]{:S(2)}) collective-permute-start(f32[64,256]{1,0:T(8,128)S(1)} %add.27), channel_id=1, source_target_pairs={{0,16},{2,6},{4,20},{6,2},{8,24},{10,14},{12,28},{14,10},{16,0},{1... | collective-permute-start | bytes 196616 | tf_op jit(solution)/shard_map/ppermute | solution.py:182
  41.0 0.0 collective-permute-done.18
  41.0 0.7 %collective-permute-start.19 = (f32[64,256]{1,0:T(8,128)S(1)}, f32[64,256]{1,0:T(8,128)S(1)}, u32[]{:S(2)}, u32[]{:S(2)}) collective-permute-start(f32[64,256]{1,0:T(8,128)S(1)} %add.29), channel_id=1, source_target_pairs={{0,0},{2,10},{4,4},{6,14},{8,8},{10,2},{12,12},{14,6},{16,16},{18,... | collective-permute-start | bytes 196616 | tf_op jit(solution)/shard_map/ppermute | solution.py:182
  41.7 1.4 %collective-permute-done.13 = f32[64,256]{1,0:T(8,128)S(1)} collective-permute-done((f32[64,256]{1,0:T(8,128)S(1)}, f32[64,256]{1,0:T(8,128)S(1)}, u32[]{:S(2)}, u32[]{:S(2)}) %collective-permute-start.13) | collective-permute-done | bytes 65568 | tf_op jit(solution)/shard_map/ppermute | solution.py:182
  43.1 3.7 %collective-permute-done.15 = f32[64,256]{1,0:T(8,128)S(1)} collective-permute-done((f32[64,256]{1,0:T(8,128)S(1)}, f32[64,256]{1,0:T(8,128)S(1)}, u32[]{:S(2)}, u32[]{:S(2)}) %collective-permute-start.15) | collective-permute-done | bytes 65568 | tf_op jit(solution)/shard_map/ppermute | solution.py:182
  46.7 0.0 collective-permute-done.17
  46.8 0.1 collective-permute-start.20
  46.9 1.2 %collective-permute-done.20 = f32[32,256]{1,0:T(8,128)S(1)} collective-permute-done((f32[32,256]{1,0:T(8,128)S(1)}, f32[32,256]{1,0:T(8,128)S(1)}, u32[]{:S(2)}, u32[]{:S(2)}) %collective-permute-start.20) | collective-permute-done | bytes 32800 | tf_op jit(solution)/shard_map/ppermute | solution.py:186
  48.1 0.6 %fusion = f32[1,32,256]{2,1,0:T(8,128)} fusion(f32[32,256]{1,0:T(8,128)S(1)} %collective-permute-done.20, f32[64,256]{1,0:T(8,128)S(1)} %add_add_fusion), kind=kLoop, calls=%fused_computation.3 | loop fusion | flops 8192 | bytes 98304 | tf_op jit(solution)/shard_map/broadcast_in_dim | solution.py:187
  (15 shorter events, 0.1 us)
Async XLA Ops:
  0.6 4.9 %collective-permute-start = (bf16[32,256]{1,0:T(8,128)(2,1)}, bf16[32,256]{1,0:T(8,128)(2,1)S(1)}, u32[]{:S(2)}, u32[]{:S(2)}) collective-permute-start(bf16[32,256]{1,0:T(8,128)(2,1)} %bitcast.12), channel_id=1, source_target_pairs={{0,1},{1,0},{2,3},{3,2},{4,5},{5,4},{6,7},{7,6},{8,9},{9,8},{10,11... | collective-permute-start | bytes 49160 | tf_op jit(solution)/shard_map/ppermute | solution.py:135
  5.6 24.3 %collective-permute-start.10 = (bf16[20,128,128]{2,1,0:T(8,128)(2,1)}, bf16[20,128,128]{2,1,0:T(8,128)(2,1)S(1)}, u32[]{:S(2)}, u32[]{:S(2)}) collective-permute-start(bf16[20,128,128]{2,1,0:T(8,128)(2,1)} %bitcast.7), channel_id=1, source_target_pairs={{0,1},{1,0},{2,3},{3,2},{4,5},{5,4},{6,7},{7,6},{8,9},{9,8},{10,11... | collective-permute-start | bytes 1966088 | tf_op jit(solution)/shard_map/ppermute | solution.py:137
  8.2 2.0 %copy-start.4 = (bf16[1,32,256]{2,1,0:T(8,128)(2,1)S(1)}, bf16[1,32,256]{2,1,0:T(8,128)(2,1)}, u32[]{:S(2)}) copy-start(bf16[1,32,256]{2,1,0:T(8,128)(2,1)} %param.6) | copy-start | bytes 49156
  9.0 1.2 %collective-permute-start.1 = (bf16[64,256]{1,0:T(8,128)(2,1)S(1)}, bf16[64,256]{1,0:T(8,128)(2,1)S(1)}, u32[]{:S(2)}, u32[]{:S(2)}) collective-permute-start(bf16[64,256]{1,0:T(8,128)(2,1)S(1)} %pad_maximum_fusion.1), channel_id=1, source_target_pairs={{0,2},{2,0},{4,6},{6,4},{8,10},{10,8},{12,14},{14,12},{16,18},{18,... | collective-permute-start | bytes 98312 | tf_op jit(solution)/shard_map/ppermute | solution.py:143
  9.0 0.7 %copy-start.1 = (s32[1,1,20]{2,1,0:T(1,128)S(1)}, s32[1,1,20]{2,1,0:T(1,128)}, u32[]{:S(2)}) copy-start(s32[1,1,20]{2,1,0:T(1,128)} %refs_10_.1) | copy-start | bytes 244
  9.0 0.7 %copy-start.2 = (s32[1,1,20,1]{2,3,1,0:T(1,128)S(1)}, s32[1,1,20,1]{2,3,1,0:T(1,128)}, u32[]{:S(2)}) copy-start(s32[1,1,20,1]{2,3,1,0:T(1,128)} %param.9) | copy-start | bytes 244
  9.8 20.1 %copy-start.3 = (s32[1,4]{1,0:T(1,128)S(1)}, s32[1,4]{1,0:T(1,128)}, u32[]{:S(2)}) copy-start(s32[1,4]{1,0:T(1,128)} %refs_13_.1) | copy-start | bytes 52
  10.2 16.0 %collective-permute-start.5 = (bf16[128,256]{1,0:T(8,128)(2,1)S(1)}, bf16[128,256]{1,0:T(8,128)(2,1)S(1)}, u32[]{:S(2)}, u32[]{:S(2)}) collective-permute-start(bf16[128,256]{1,0:T(8,128)(2,1)S(1)} %pad_maximum_fusion), channel_id=1, source_target_pairs={{0,0},{2,10},{4,4},{6,14},{8,8},{10,2},{12,12},{14,6},{16,16},{18,... | collective-permute-start | bytes 196616 | tf_op jit(solution)/shard_map/ppermute | solution.py:146
  10.9 10.5 %collective-permute-start.11 = (s32[1,41]{1,0:T(1,128)S(1)}, s32[1,41]{1,0:T(1,128)S(1)}, u32[]{:S(2)}, u32[]{:S(2)}) collective-permute-start(s32[1,41]{1,0:T(1,128)S(1)} %pad_add_fusion), channel_id=1, source_target_pairs={{0,1},{1,0},{2,3},{3,2},{4,5},{5,4},{6,7},{7,6},{8,9},{9,8},{10,11... | collective-permute-start | bytes 500 | tf_op jit(solution)/shard_map/ppermute | solution.py:141
  11.0 15.3 %collective-permute-start.4 = (bf16[128,256]{1,0:T(8,128)(2,1)S(1)}, bf16[128,256]{1,0:T(8,128)(2,1)S(1)}, u32[]{:S(2)}, u32[]{:S(2)}) collective-permute-start(bf16[128,256]{1,0:T(8,128)(2,1)S(1)} %pad_maximum_fusion), channel_id=1, source_target_pairs={{0,16},{2,6},{4,20},{6,2},{8,24},{10,14},{12,28},{14,10},{16,0},{1... | collective-permute-start | bytes 196616 | tf_op jit(solution)/shard_map/ppermute | solution.py:146
  14.1 12.7 %collective-permute-start.3 = (bf16[128,256]{1,0:T(8,128)(2,1)S(1)}, bf16[128,256]{1,0:T(8,128)(2,1)S(1)}, u32[]{:S(2)}, u32[]{:S(2)}) collective-permute-start(bf16[128,256]{1,0:T(8,128)(2,1)S(1)} %pad_maximum_fusion), channel_id=1, source_target_pairs={{0,12},{2,26},{4,8},{6,30},{8,4},{10,18},{12,0},{14,22},{16,28},{1... | collective-permute-start | bytes 196616 | tf_op jit(solution)/shard_map/ppermute | solution.py:146
  21.4 7.1 %collective-permute-start.2 = (bf16[128,256]{1,0:T(8,128)(2,1)S(1)}, bf16[128,256]{1,0:T(8,128)(2,1)S(1)}, u32[]{:S(2)}, u32[]{:S(2)}) collective-permute-start(bf16[128,256]{1,0:T(8,128)(2,1)S(1)} %pad_maximum_fusion), channel_id=1, source_target_pairs={{0,28},{2,22},{4,24},{6,18},{8,20},{10,30},{12,16},{14,26},{16,12}... | collective-permute-start | bytes 196616 | tf_op jit(solution)/shard_map/ppermute | solution.py:146
  26.3 2.3 %collective-permute-start.9 = (bf16[128,256]{1,0:T(8,128)(2,1)S(1)}, bf16[128,256]{1,0:T(8,128)(2,1)S(1)}, u32[]{:S(2)}, u32[]{:S(2)}) collective-permute-start(bf16[128,256]{1,0:T(8,128)(2,1)S(1)} %collective-permute-done.5.refs_3_), channel_id=1, source_target_pairs={{0,2},{2,0},{4,6},{6,4},{8,10},{10,8},{12,14},{14,12},{16,18},{18,... | collective-permute-start | bytes 196616 | tf_op jit(solution)/shard_map/ppermute | solution.py:148
  26.3 2.3 %collective-permute-start.8 = (bf16[128,256]{1,0:T(8,128)(2,1)S(1)}, bf16[128,256]{1,0:T(8,128)(2,1)S(1)}, u32[]{:S(2)}, u32[]{:S(2)}) collective-permute-start(bf16[128,256]{1,0:T(8,128)(2,1)S(1)} %collective-permute-done.4.refs_2_), channel_id=1, source_target_pairs={{0,2},{2,0},{4,6},{6,4},{8,10},{10,8},{12,14},{14,12},{16,18},{18,... | collective-permute-start | bytes 196616 | tf_op jit(solution)/shard_map/ppermute | solution.py:148
  26.8 1.8 %collective-permute-start.7 = (bf16[128,256]{1,0:T(8,128)(2,1)S(1)}, bf16[128,256]{1,0:T(8,128)(2,1)S(1)}, u32[]{:S(2)}, u32[]{:S(2)}) collective-permute-start(bf16[128,256]{1,0:T(8,128)(2,1)S(1)} %collective-permute-done.3.refs_1_), channel_id=1, source_target_pairs={{0,2},{2,0},{4,6},{6,4},{8,10},{10,8},{12,14},{14,12},{16,18},{18,... | collective-permute-start | bytes 196616 | tf_op jit(solution)/shard_map/ppermute | solution.py:148
  28.6 1.3 %collective-permute-start.6 = (bf16[128,256]{1,0:T(8,128)(2,1)S(1)}, bf16[128,256]{1,0:T(8,128)(2,1)S(1)}, u32[]{:S(2)}, u32[]{:S(2)}) collective-permute-start(bf16[128,256]{1,0:T(8,128)(2,1)S(1)} %collective-permute-done.2.refs_0_), channel_id=1, source_target_pairs={{0,2},{2,0},{4,6},{6,4},{8,10},{10,8},{12,14},{14,12},{16,18},{18,... | collective-permute-start | bytes 196616 | tf_op jit(solution)/shard_map/ppermute | solution.py:148
  29.8 1.1 %copy-start = (bf16[1,1,20,128,128]{4,3,2,1,0:T(8,128)(2,1)S(1)}, bf16[1,1,20,128,128]{4,3,2,1,0:T(8,128)(2,1)}, u32[]{:S(2)}) copy-start(bf16[1,1,20,128,128]{4,3,2,1,0:T(8,128)(2,1)} %param.7) | copy-start | bytes 1966084
  34.0 1.3 %collective-permute-start.12 = (f32[64,256]{1,0:T(8,128)S(1)}, f32[64,256]{1,0:T(8,128)S(1)}, u32[]{:S(2)}, u32[]{:S(2)}) collective-permute-start(f32[64,256]{1,0:T(8,128)S(1)} %get-tuple-element.17), channel_id=1, source_target_pairs={{0,2},{2,0},{4,6},{6,4},{8,10},{10,8},{12,14},{14,12},{16,18},{18,... | collective-permute-start | bytes 196616 | tf_op jit(solution)/shard_map/ppermute | solution.py:179
  34.4 5.7 %collective-permute-start.14 = (f32[64,256]{1,0:T(8,128)S(1)}, f32[64,256]{1,0:T(8,128)S(1)}, u32[]{:S(2)}, u32[]{:S(2)}) collective-permute-start(f32[64,256]{1,0:T(8,128)S(1)} %get-tuple-element.19), channel_id=1, source_target_pairs={{0,2},{2,0},{4,6},{6,4},{8,10},{10,8},{12,14},{14,12},{16,18},{18,... | collective-permute-start | bytes 196616 | tf_op jit(solution)/shard_map/ppermute | solution.py:179
  34.6 5.7 %collective-permute-start.16 = (f32[64,256]{1,0:T(8,128)S(1)}, f32[64,256]{1,0:T(8,128)S(1)}, u32[]{:S(2)}, u32[]{:S(2)}) collective-permute-start(f32[64,256]{1,0:T(8,128)S(1)} %get-tuple-element.21), channel_id=1, source_target_pairs={{0,2},{2,0},{4,6},{6,4},{8,10},{10,8},{12,14},{14,12},{16,18},{18,... | collective-permute-start | bytes 196616 | tf_op jit(solution)/shard_map/ppermute | solution.py:179
  34.9 6.0 %collective-permute-start.18 = (f32[64,256]{1,0:T(8,128)S(1)}, f32[64,256]{1,0:T(8,128)S(1)}, u32[]{:S(2)}, u32[]{:S(2)}) collective-permute-start(f32[64,256]{1,0:T(8,128)S(1)} %get-tuple-element.23), channel_id=1, source_target_pairs={{0,2},{2,0},{4,6},{6,4},{8,10},{10,8},{12,14},{14,12},{16,18},{18,... | collective-permute-start | bytes 196616 | tf_op jit(solution)/shard_map/ppermute | solution.py:179
  35.3 7.7 %collective-permute-start.13 = (f32[64,256]{1,0:T(8,128)S(1)}, f32[64,256]{1,0:T(8,128)S(1)}, u32[]{:S(2)}, u32[]{:S(2)}) collective-permute-start(f32[64,256]{1,0:T(8,128)S(1)} %add.24), channel_id=1, source_target_pairs={{0,28},{2,22},{4,24},{6,18},{8,20},{10,30},{12,16},{14,26},{16,12}... | collective-permute-start | bytes 196616 | tf_op jit(solution)/shard_map/ppermute | solution.py:182
  40.2 6.6 %collective-permute-start.15 = (f32[64,256]{1,0:T(8,128)S(1)}, f32[64,256]{1,0:T(8,128)S(1)}, u32[]{:S(2)}, u32[]{:S(2)}) collective-permute-start(f32[64,256]{1,0:T(8,128)S(1)} %add.25), channel_id=1, source_target_pairs={{0,12},{2,26},{4,8},{6,30},{8,4},{10,18},{12,0},{14,22},{16,28},{1... | collective-permute-start | bytes 196616 | tf_op jit(solution)/shard_map/ppermute | solution.py:182
  40.3 6.5 %collective-permute-start.17 = (f32[64,256]{1,0:T(8,128)S(1)}, f32[64,256]{1,0:T(8,128)S(1)}, u32[]{:S(2)}, u32[]{:S(2)}) collective-permute-start(f32[64,256]{1,0:T(8,128)S(1)} %add.27), channel_id=1, source_target_pairs={{0,16},{2,6},{4,20},{6,2},{8,24},{10,14},{12,28},{14,10},{16,0},{1... | collective-permute-start | bytes 196616 | tf_op jit(solution)/shard_map/ppermute | solution.py:182
  41.0 5.7 %collective-permute-start.19 = (f32[64,256]{1,0:T(8,128)S(1)}, f32[64,256]{1,0:T(8,128)S(1)}, u32[]{:S(2)}, u32[]{:S(2)}) collective-permute-start(f32[64,256]{1,0:T(8,128)S(1)} %add.29), channel_id=1, source_target_pairs={{0,0},{2,10},{4,4},{6,14},{8,8},{10,2},{12,12},{14,6},{16,16},{18,... | collective-permute-start | bytes 196616 | tf_op jit(solution)/shard_map/ppermute | solution.py:182
  46.8 1.3 %collective-permute-start.20 = (f32[32,256]{1,0:T(8,128)S(1)}, f32[32,256]{1,0:T(8,128)S(1)}, u32[]{:S(2)}, u32[]{:S(2)}) collective-permute-start(f32[32,256]{1,0:T(8,128)S(1)} %slice.9), channel_id=1, source_target_pairs={{0,2},{2,0},{4,6},{6,4},{8,10},{10,8},{12,14},{14,12},{16,18},{18,... | collective-permute-start | bytes 98312 | tf_op jit(solution)/shard_map/ppermute | solution.py:186

commit v2 on v1

--- a/solution.py
+++ b/solution.py
@@ -4,6 +4,8 @@
 from jax.experimental import pallas as pl
 from jax.experimental.pallas import tpu as pltpu
 from jax.sharding import PartitionSpec as P
+
+NOTES, LANES = 16, 128
 
 
 def sides_of(chips):
@@ -17,21 +19,56 @@
     return sides
 
 
+def parcel_kernel(tiles_hbm, rows_hbm, cols_hbm, count_hbm, owners_hbm, parcel, notes, *scratch):
+    rows, cols, count, owners, sems = scratch
+    height = tiles_hbm.shape[0]
+    copies = [
+        pltpu.make_async_copy(source, target, sems.at[i])
+        for i, (source, target) in enumerate(
+            (
+                (rows_hbm, rows),
+                (cols_hbm, cols),
+                (count_hbm, count),
+                (owners_hbm, owners),
+                (tiles_hbm, parcel.at[0:height, :]),
+            )
+        )
+    ]
+    for copy in copies:
+        copy.start()
+    notes[...] = jnp.zeros_like(notes)
+    for copy in copies[:4]:
+        copy.wait()
+    notes[0:1, 0 : rows.shape[1]] = rows[...]
+    notes[1:2, 0 : cols.shape[1]] = cols[...]
+    notes[2:3, 0:1] = count[...]
+    notes[3:4, 0 : owners.shape[1]] = owners[...]
+    parcel[height:, :] = notes[...].astype(jnp.float32).astype(parcel.dtype)
+    copies[4].wait()
+
+
 def block_kernel(rounds, sides, *refs):
-    direct, relayed = refs[:rounds], refs[rounds : 2 * rounds]
-    (own_tiles, far_tiles, own_rows, own_cols, own_count, owners, far_meta) = refs[
-        2 * rounds : 2 * rounds + 7
-    ]
-    outs = refs[2 * rounds + 7 :]
+    direct, relayed = refs[:rounds][::-1], refs[rounds : 2 * rounds][::-1]
+    own_notes, own_parcel, far_parcel = refs[2 * rounds : 2 * rounds + 3]
+    outs = refs[2 * rounds + 3 :]
     y_out, keep, give = outs[0], outs[1 : 1 + rounds], outs[1 + rounds : 1 + 2 * rounds]
-    near, far, own_a, far_a, y_all, z_all = outs[1 + 2 * rounds :]
-    total, size = own_tiles.shape[0], own_tiles.shape[1]
-    group = owners.shape[1]
+    near, far, own_a, far_a, y_all, z_all, far_notes, scalars, sems = outs[1 + 2 * rounds :]
+    size = own_parcel.shape[1]
+    height = own_parcel.shape[0] - NOTES
     shard = direct[0].shape[0] // 4
+    group = own_a.shape[0] // size
     place = lax.axis_index("blk")
     core, chip = lax.rem(place, 2), lax.div(place, 2)
     half = lax.axis_index("rows")
 
+    far_notes[...] = far_parcel[height:, :].astype(jnp.float32).astype(jnp.int32)
+    tells = [
+        pltpu.make_async_copy(own_notes, scalars.at[0], sems.at[0]),
+        pltpu.make_async_copy(far_notes, scalars.at[1], sems.at[1]),
+    ]
+    for tell in tells:
+        tell.start()
+
     def rows_of(which, side):
         return pl.ds(pl.multiple_of(which * (2 * shard) + side * shard, shard), shard)
 
@@ -39,40 +76,31 @@
         return lax.bitwise_xor(chip, jnp.where(side == 0, sides[0][step], sides[1][step]))
 
     for step in range(rounds):
-        for ref, side, first in (
-            (direct[step], core, core),
-            (relayed[step], 1 - core, 1 - core),
-        ):
+        for ref, side in ((direct[step], core), (relayed[step], 1 - core)):
             which = chip_of(step, side)
-            near[rows_of(which, first), :] = ref[0:shard, :]
-            far[rows_of(which, first), :] = ref[shard : 2 * shard, :]
-            near[rows_of(which, 1 - first), :] = ref[2 * shard : 3 * shard, :]
-            far[rows_of(which, 1 - first), :] = ref[3 * shard : 4 * shard, :]
-
-    def place_tiles(a, tiles, row_at, col_at, count):
+            near[rows_of(which, side), :] = ref[0:shard, :]
+            far[rows_of(which, side), :] = ref[shard : 2 * shard, :]
+            near[rows_of(which, 1 - side), :] = ref[2 * shard : 3 * shard, :]
+            far[rows_of(which, 1 - side), :] = ref[3 * shard : 4 * shard, :]
+
+    def place_tiles(a, tiles, at):
         a[...] = jnp.zeros_like(a)
 
         def add(t, carry):
-            rows = pl.ds(pl.multiple_of(row_at(t) * size, size), size)
-            cols = pl.ds(pl.multiple_of(col_at(t) * size, size), size)
-            a[rows, cols] = a[rows, cols] + tiles[t].astype(jnp.float32)
+            rows = pl.ds(pl.multiple_of(scalars[at, 0, t] * size, size), size)
+            cols = pl.ds(pl.multiple_of(scalars[at, 1, t] * size, size), size)
+            a[rows, cols] = a[rows, cols] + tiles[pl.ds(pl.multiple_of(t * size, size), size), :].astype(jnp.float32)
             return carry
 
-        lax.fori_loop(0, count, add, 0)
+        lax.fori_loop(0, scalars[at, 2, 0], add, 0)
         high = a[...].astype(jnp.bfloat16)
         low = (a[...] - high.astype(jnp.float32)).astype(jnp.bfloat16)
         return high, low
 
-    own_high, own_low = place_tiles(
-        own_a, own_tiles, lambda t: own_rows[0, 0, t], lambda t: own_cols[0, t], own_count[0, 0]
-    )
-    far_high, far_low = place_tiles(
-        far_a,
-        far_tiles,
-        lambda t: far_meta[0, t],
-        lambda t: far_meta[0, total + t],
-        far_meta[0, 2 * total],
-    )
+    for tell in tells:
+        tell.wait()
+    own_high, own_low = place_tiles(own_a, own_parcel, 0)
+    far_high, far_low = place_tiles(far_a, far_parcel, 1)
 
     def dot(a, b):
         return jnp.dot(a, b, preferred_element_type=jnp.float32)
@@ -85,7 +113,7 @@
     y_all[...] = y16
     mine = group // 2
     for k in range(group):
-        slot = owners[0, k]
+        slot = scalars[0, 3, k]
 
         @pl.when(lax.div(slot, mine) == half)
         def _():
@@ -99,13 +127,10 @@
 
     z_all[...] = turned(own_high, y16) + turned(own_low, y16)
     for step in range(rounds):
-        for ref, side, first in (
-            (keep[step], core, core),
-            (give[step], 1 - core, 1 - core),
-        ):
+        for ref, side in ((keep[step], core), (give[step], 1 - core)):
             which = chip_of(step, side)
-            ref[0:shard, :] = z_all[rows_of(which, first), :]
-            ref[shard : 2 * shard, :] = z_all[rows_of(which, 1 - first), :]
+            ref[0:shard, :] = z_all[rows_of(which, side), :]
+            ref[shard : 2 * shard, :] = z_all[rows_of(which, 1 - side), :]
 
 
 def paired(q_panel, tiles, tile_rows, tile_cols, tile_count, owner_map):
@@ -117,7 +142,6 @@
     stack = tiles[0, 0]
     total, size = stack.shape[:2]
     group = owner_map.shape[1]
-    cols = tile_cols.reshape(1, total)
 
     across = [(0, 1), (1, 0)]
     sibling = [(i, i ^ 1) for i in range(devices)]
@@ -130,25 +154,45 @@
         ]
 
     order = tuple(range(rounds))
+    vmem = pl.BlockSpec(memory_space=pltpu.VMEM)
 
     q_own = q_panel[0]
     q_far = lax.ppermute(q_own, "rows", across)
-    stack, q_far = lax.optimization_barrier((stack, q_far))
-    far_tiles = lax.ppermute(stack, "rows", across)
-    meta = jnp.concatenate(
-        [tile_rows.reshape(1, total), cols, tile_count.reshape(1, 1)], axis=1
-    )
-    far_meta = lax.ppermute(meta, "rows", across)
-    pair = jnp.concatenate([q_own, q_far], axis=0)
-    block = jnp.concatenate([pair, lax.ppermute(pair, "blk", sibling)], axis=0)
+    q_sibling = lax.ppermute(q_own, "blk", sibling)
+    parcel, notes = pl.pallas_call(
+        parcel_kernel,
+        out_shape=[
+            jax.ShapeDtypeStruct((total * size + NOTES, size), stack.dtype),
+            jax.ShapeDtypeStruct((NOTES, LANES), jnp.int32),
+        ],
+        in_specs=[pl.BlockSpec(memory_space=pl.ANY)] * 5,
+        out_specs=[vmem] * 2,
+        scratch_shapes=[
+            pltpu.VMEM((1, total), jnp.int32),
+            pltpu.VMEM((1, total), jnp.int32),
+            pltpu.VMEM((1, 1), jnp.int32),
+            pltpu.VMEM((1, group), jnp.int32),
+            pltpu.SemaphoreType.DMA((5,)),
+        ],
+        compiler_params=pltpu.CompilerParams(vmem_limit_bytes=24 << 20),
+        name="parcel",
+    )(
+        stack.reshape(total * size, size),
+        tile_rows.reshape(1, total),
+        tile_cols.reshape(1, total),
+        tile_count,
+        owner_map,
+    )
+    late_parcel, q_far = lax.optimization_barrier((parcel, q_far))
+    far_parcel = lax.ppermute(late_parcel, "rows", across)
+    q_diagonal = lax.ppermute(q_far, "blk", sibling)
+    block = jnp.concatenate([q_own, q_far, q_sibling, q_diagonal], axis=0)
     direct, relayed = [None] * rounds, [None] * rounds
-    for step in order:
+    for step in reversed(order):
         direct[step] = lax.ppermute(block, "blk", to_chips(step))
-    for step in order:
+    for step in reversed(order):
         relayed[step] = lax.ppermute(direct[step], "blk", sibling)
 
-    vmem = pl.BlockSpec(memory_space=pltpu.VMEM)
-    smem = pl.BlockSpec(memory_space=pltpu.SMEM)
     width = devices * shard
     height = group * size
     piece = jax.ShapeDtypeStruct((2 * shard, rank), jnp.float32)
@@ -160,7 +204,7 @@
         body,
         out_shape=[jax.ShapeDtypeStruct((height // 2, rank), jnp.bfloat16)]
         + [piece] * (2 * rounds),
-        in_specs=[vmem] * (2 * rounds + 2) + [smem] * 5,
+        in_specs=[vmem] * (2 * rounds + 3),
         out_specs=[vmem] * (1 + 2 * rounds),
         scratch_shapes=[
             pltpu.VMEM((width, rank), jnp.bfloat16),
@@ -169,10 +213,13 @@
             pltpu.VMEM((height, width), jnp.float32),
             pltpu.VMEM((height, rank), jnp.bfloat16),
             pltpu.VMEM((width, rank), jnp.float32),
+            pltpu.VMEM((NOTES, LANES), jnp.int32),
+            pltpu.SMEM((2, NOTES, LANES), jnp.int32),
+            pltpu.SemaphoreType.DMA((2,)),
         ],
         compiler_params=pltpu.CompilerParams(vmem_limit_bytes=24 << 20),
         name="block_products",
-    )(*direct, *relayed, stack, far_tiles, tile_rows, cols, tile_count, owner_map, far_meta)
+    )(*direct[::-1], *relayed[::-1], notes, parcel, far_parcel)
     y_owned, keep, give = made[0], made[1 : 1 + rounds], made[1 + rounds :]
     came = [None] * rounds
     for step in order:

time: 48.9 us -> 40.5 us (0.83)
  starting transfers between devices: 24.2 us -> 18.6 us
  waiting for transfers between devices: 16.7 us -> 14.2 us
  other arithmetic: 1.54 us -> 0.68 us
  Pallas kernels: 3.08 us -> 3.71 us
    ppermute x4, starting transfers between devices: 11.1 us -> 5.94 us  [paired(): direct[step] = lax.ppermute(block, 'blk', to_chips(step))]
    ppermute x3, waiting for transfers between devices: 5.26 us -> 2.02 us  [the longest x1 1.18 us: paired(): far_parcel = lax.ppermute(late_parcel, 'rows', across)]
    ppermute x4, waiting for transfers between devices: 1.74 us -> 4.85 us  [paired(): direct[step] = lax.ppermute(block, 'blk', to_chips(step))]
    ppermute x1, waiting for transfers between devices: 1.93 us -> 0.01 us  [paired(): q_far = lax.ppermute(q_own, 'rows', across)]
    concatenate x3 -> x1, other arithmetic: 0.86 us -> 0.01 us  [paired(): block = jnp.concatenate([q_own, q_far, q_sibling, q_diagonal], axis=0)]
  transfers between devices with their start and end apart: 21 -> 21, of which waited for: 9 -> 12; matrix products, arithmetic and copies ran while one was open for 2% -> 0% of each run, Pallas kernels for 0% -> 1%
where the time goes in v2:
time: 40.5 us; the launch traced here: 40.4 us
  starting transfers between devices  18.6 us (46%)
  waiting for transfers between devices  14.2 us (35%)
  Pallas kernels  3.71 us (9%)
  local copies, waits for them, and re-layouts  1.76 us (4%)
  between operations  1.43 us (4%)
  other arithmetic  0.68 us (2%)
    ppermute x4, starting transfers between devices, paired(): arrived[step] = lax.ppermute(keep[step] + came[step], 'blk', to_chips(step))  6.22 us
    ppermute x4, starting transfers between devices, paired(): direct[step] = lax.ppermute(block, 'blk', to_chips(step))  5.94 us
    ppermute x4, waiting for transfers between devices, paired(): direct[step] = lax.ppermute(block, 'blk', to_chips(step))  4.85 us
    ppermute x4, waiting for transfers between devices, paired(): arrived[step] = lax.ppermute(keep[step] + came[step], 'blk', to_chips(step))  4.75 us
    pallas_call x1, Pallas kernels, paired(): pl.pallas_call(body, out_shape=[jax.ShapeDtypeStruct((height // 2, rank),...  3.44 us
    ppermute x1, starting transfers between devices, paired(): q_far = lax.ppermute(q_own, 'rows', across)  3 us
    unnamed x10, local copies, waits for them, and re-layouts  1.75 us
    ppermute x1, starting transfers between devices, paired(): far_parcel = lax.ppermute(late_parcel, 'rows', across)  1.23 us
  transfers between devices with their start and end apart: 21, of which 12 were waited for; matrix products, arithmetic and copies ran while one was open for 0% of the time, Pallas kernels for 1%

profile of v2, /device:TPU:0, one launch (start us, length us, event | category | flops | bytes accessed | tf_op | source)
XLA Modules:
  0.0 40.4 jit_solution(13559327095305800152)
XLA Ops:
  0.6 3.0 %collective-permute-start = (bf16[32,256]{1,0:T(8,128)(2,1)}, bf16[32,256]{1,0:T(8,128)(2,1)S(1)}, u32[]{:S(2)}, u32[]{:S(2)}) collective-permute-start(bf16[32,256]{1,0:T(8,128)(2,1)} %bitcast.10), channel_id=1, source_target_pairs={{0,1},{1,0},{2,3},{3,2},{4,5},{5,4},{6,7},{7,6},{8,9},{9,8},{10,11... | collective-permute-start | bytes 49160 | tf_op jit(solution)/shard_map/ppermute | solution.py:160
  4.3 0.6 %copy-done.1 = s32[1,1,20]{2,1,0:T(1,128)S(1)} copy-done((s32[1,1,20]{2,1,0:T(1,128)S(1)}, s32[1,1,20]{2,1,0:T(1,128)}, u32[]{:S(2)}) %copy-start.1) | copy-done | bytes 104
  4.9 0.0 copy-done.2
  5.0 0.0 copy-done.3
  5.0 1.1 %copy-done = bf16[1,1,20,128,128]{4,3,2,1,0:T(8,128)(2,1)S(1)} copy-done((bf16[1,1,20,128,128]{4,3,2,1,0:T(8,128)(2,1)S(1)}, bf16[1,1,20,128,128]{4,3,2,1,0:T(8,128)(2,1)}, u32[]{:S(2)}) %copy-start) | copy-done | bytes 655384
  6.1 0.3 parcel.1
  6.3 0.0 collective-permute-done
  6.4 1.2 %collective-permute-start.11 = (bf16[2576,128]{1,0:T(8,128)(2,1)S(1)}, bf16[2576,128]{1,0:T(8,128)(2,1)S(1)}, u32[]{:S(2)}, u32[]{:S(2)}) collective-permute-start(bf16[2576,128]{1,0:T(8,128)(2,1)S(1)} %get-tuple-element.18.refs_9_), channel_id=1, source_target_pairs={{0,1},{1,0},{2,3},{3,2},{4,5},{5,4},{6,7},{7,6},{8,9},{9,8},{10,11... | collective-permute-start | bytes 1978376 | tf_op jit(solution)/shard_map/ppermute | solution.py:187
  7.6 0.0 collective-permute-start.1
  7.6 0.5 %collective-permute-start.2 = (bf16[32,256]{1,0:T(8,128)(2,1)S(1)}, bf16[32,256]{1,0:T(8,128)(2,1)S(1)}, u32[]{:S(2)}, u32[]{:S(2)}) collective-permute-start(bf16[32,256]{1,0:T(8,128)(2,1)S(1)} %collective-permute-done), channel_id=1, source_target_pairs={{0,2},{2,0},{4,6},{6,4},{8,10},{10,8},{12,14},{14,12},{16,18},{18,... | collective-permute-start | bytes 49160 | tf_op jit(solution)/shard_map/ppermute | solution.py:188
  8.1 0.7 %collective-permute-done.1 = bf16[32,256]{1,0:T(8,128)(2,1)S(1)} collective-permute-done((bf16[32,256]{1,0:T(8,128)(2,1)S(1)}, bf16[32,256]{1,0:T(8,128)(2,1)S(1)}, u32[]{:S(2)}, u32[]{:S(2)}) %collective-permute-start.1) | collective-permute-done | bytes 16416 | tf_op jit(solution)/shard_map/ppermute | solution.py:161
  8.8 0.2 collective-permute-done.2
  8.9 4.6 %collective-permute-start.6 = (bf16[128,256]{1,0:T(8,128)(2,1)S(1)}, bf16[128,256]{1,0:T(8,128)(2,1)S(1)}, u32[]{:S(2)}, u32[]{:S(2)}) collective-permute-start(bf16[128,256]{1,0:T(8,128)(2,1)S(1)} %pad_maximum_fusion), channel_id=1, source_target_pairs={{0,28},{2,22},{4,24},{6,18},{8,20},{10,30},{12,16},{14,26},{16,12}... | collective-permute-start | bytes 196616 | tf_op jit(solution)/shard_map/ppermute | solution.py:192
  13.5 0.0 collective-permute-start.5
  13.5 0.7 %collective-permute-start.4 = (bf16[128,256]{1,0:T(8,128)(2,1)S(1)}, bf16[128,256]{1,0:T(8,128)(2,1)S(1)}, u32[]{:S(2)}, u32[]{:S(2)}) collective-permute-start(bf16[128,256]{1,0:T(8,128)(2,1)S(1)} %pad_maximum_fusion), channel_id=1, source_target_pairs={{0,16},{2,6},{4,20},{6,2},{8,24},{10,14},{12,28},{14,10},{16,0},{1... | collective-permute-start | bytes 196616 | tf_op jit(solution)/shard_map/ppermute | solution.py:192
  14.2 0.7 %collective-permute-start.3 = (bf16[128,256]{1,0:T(8,128)(2,1)S(1)}, bf16[128,256]{1,0:T(8,128)(2,1)S(1)}, u32[]{:S(2)}, u32[]{:S(2)}) collective-permute-start(bf16[128,256]{1,0:T(8,128)(2,1)S(1)} %pad_maximum_fusion), channel_id=1, source_target_pairs={{0,0},{2,10},{4,4},{6,14},{8,8},{10,2},{12,12},{14,6},{16,16},{18,... | collective-permute-start | bytes 196616 | tf_op jit(solution)/shard_map/ppermute | solution.py:192
  14.9 1.3 %collective-permute-done.6.refs_3_ = bf16[128,256]{1,0:T(8,128)(2,1)S(1)} collective-permute-done((bf16[128,256]{1,0:T(8,128)(2,1)S(1)}, bf16[128,256]{1,0:T(8,128)(2,1)S(1)}, u32[]{:S(2)}, u32[]{:S(2)}) %collective-permute-start.6) | collective-permute-done | bytes 65568 | tf_op jit(solution)/shard_map/ppermute | solution.py:192
  16.2 0.0 collective-permute-start.10
  16.2 3.5 %collective-permute-done.5.refs_2_ = bf16[128,256]{1,0:T(8,128)(2,1)S(1)} collective-permute-done((bf16[128,256]{1,0:T(8,128)(2,1)S(1)}, bf16[128,256]{1,0:T(8,128)(2,1)S(1)}, u32[]{:S(2)}, u32[]{:S(2)}) %collective-permute-start.5) | collective-permute-done | bytes 65568 | tf_op jit(solution)/shard_map/ppermute | solution.py:192
  19.7 0.0 collective-permute-start.9
  19.7 0.0 collective-permute-done.4.refs_1_
  19.7 0.5 %collective-permute-start.8 = (bf16[128,256]{1,0:T(8,128)(2,1)S(1)}, bf16[128,256]{1,0:T(8,128)(2,1)S(1)}, u32[]{:S(2)}, u32[]{:S(2)}) collective-permute-start(bf16[128,256]{1,0:T(8,128)(2,1)S(1)} %collective-permute-done.4.refs_1_), channel_id=1, source_target_pairs={{0,2},{2,0},{4,6},{6,4},{8,10},{10,8},{12,14},{14,12},{16,18},{18,... | collective-permute-start | bytes 196616 | tf_op jit(solution)/shard_map/ppermute | solution.py:194
  20.3 0.0 collective-permute-done.3.refs_0_
  20.3 0.1 collective-permute-start.7
  20.3 0.0 collective-permute-done.10.refs_7_
  20.3 0.7 %collective-permute-done.9.refs_6_ = bf16[128,256]{1,0:T(8,128)(2,1)S(1)} collective-permute-done((bf16[128,256]{1,0:T(8,128)(2,1)S(1)}, bf16[128,256]{1,0:T(8,128)(2,1)S(1)}, u32[]{:S(2)}, u32[]{:S(2)}) %collective-permute-start.9) | collective-permute-done | bytes 65568 | tf_op jit(solution)/shard_map/ppermute | solution.py:194
  21.0 0.2 collective-permute-done.8.refs_5_
  21.2 0.4 collective-permute-done.7.refs_4_
  21.5 1.2 %collective-permute-done.11.refs_10_ = bf16[2576,128]{1,0:T(8,128)(2,1)S(1)} collective-permute-done((bf16[2576,128]{1,0:T(8,128)(2,1)S(1)}, bf16[2576,128]{1,0:T(8,128)(2,1)S(1)}, u32[]{:S(2)}, u32[]{:S(2)}) %collective-permute-start.11) | collective-permute-done | bytes 659488 | tf_op jit(solution)/shard_map/ppermute | solution.py:187
  22.7 3.4 %block_products.1 = (bf16[256,256]{1,0:T(8,128)(2,1)}, f32[64,256]{1,0:T(8,128)S(1)}, f32[64,256]{1,0:T(8,128)S(1)}, f32[64,256]{1,0:T(8,128)S(1)}, f32[64,256]{...) custom-call(bf16[128,256]{1,0:T(8,128)(2,1)S(1)} %collective-permute, ...), custom_call_target="tpu_custom_call" | custom-call | tf_op jit(solution)/shard_map/block_products/pallas_call | solution.py:203
  26.1 0.1 collective-permute-start.12
  26.2 0.5 %collective-permute-start.14 = (f32[64,256]{1,0:T(8,128)S(1)}, f32[64,256]{1,0:T(8,128)S(1)}, u32[]{:S(2)}, u32[]{:S(2)}) collective-permute-start(f32[64,256]{1,0:T(8,128)S(1)} %get-tuple-element.23), channel_id=1, source_target_pairs={{0,2},{2,0},{4,6},{6,4},{8,10},{10,8},{12,14},{14,12},{16,18},{18,... | collective-permute-start | bytes 196616 | tf_op jit(solution)/shard_map/ppermute | solution.py:226
  26.7 0.1 collective-permute-start.16
  26.8 0.4 %collective-permute-start.18 = (f32[64,256]{1,0:T(8,128)S(1)}, f32[64,256]{1,0:T(8,128)S(1)}, u32[]{:S(2)}, u32[]{:S(2)}) collective-permute-start(f32[64,256]{1,0:T(8,128)S(1)} %get-tuple-element.27), channel_id=1, source_target_pairs={{0,2},{2,0},{4,6},{6,4},{8,10},{10,8},{12,14},{14,12},{16,18},{18,... | collective-permute-start | bytes 196616 | tf_op jit(solution)/shard_map/ppermute | solution.py:226
  27.2 0.2 collective-permute-done.12
  27.5 4.8 %collective-permute-start.13 = (f32[64,256]{1,0:T(8,128)S(1)}, f32[64,256]{1,0:T(8,128)S(1)}, u32[]{:S(2)}, u32[]{:S(2)}) collective-permute-start(f32[64,256]{1,0:T(8,128)S(1)} %add.24), channel_id=1, source_target_pairs={{0,28},{2,22},{4,24},{6,18},{8,20},{10,30},{12,16},{14,26},{16,12}... | collective-permute-start | bytes 196616 | tf_op jit(solution)/shard_map/ppermute | solution.py:229
  32.3 0.0 collective-permute-done.14
  32.3 0.1 collective-permute-start.15
  32.4 0.0 collective-permute-done.16
  32.4 0.7 %collective-permute-start.17 = (f32[64,256]{1,0:T(8,128)S(1)}, f32[64,256]{1,0:T(8,128)S(1)}, u32[]{:S(2)}, u32[]{:S(2)}) collective-permute-start(f32[64,256]{1,0:T(8,128)S(1)} %add.27), channel_id=1, source_target_pairs={{0,16},{2,6},{4,20},{6,2},{8,24},{10,14},{12,28},{14,10},{16,0},{1... | collective-permute-start | bytes 196616 | tf_op jit(solution)/shard_map/ppermute | solution.py:229
  33.1 0.0 collective-permute-done.18
  33.1 0.7 %collective-permute-start.19 = (f32[64,256]{1,0:T(8,128)S(1)}, f32[64,256]{1,0:T(8,128)S(1)}, u32[]{:S(2)}, u32[]{:S(2)}) collective-permute-start(f32[64,256]{1,0:T(8,128)S(1)} %add.29), channel_id=1, source_target_pairs={{0,0},{2,10},{4,4},{6,14},{8,8},{10,2},{12,12},{14,6},{16,16},{18,... | collective-permute-start | bytes 196616 | tf_op jit(solution)/shard_map/ppermute | solution.py:229
  33.8 1.0 %collective-permute-done.13 = f32[64,256]{1,0:T(8,128)S(1)} collective-permute-done((f32[64,256]{1,0:T(8,128)S(1)}, f32[64,256]{1,0:T(8,128)S(1)}, u32[]{:S(2)}, u32[]{:S(2)}) %collective-permute-start.13) | collective-permute-done | bytes 65568 | tf_op jit(solution)/shard_map/ppermute | solution.py:229
  34.8 3.7 %collective-permute-done.15 = f32[64,256]{1,0:T(8,128)S(1)} collective-permute-done((f32[64,256]{1,0:T(8,128)S(1)}, f32[64,256]{1,0:T(8,128)S(1)}, u32[]{:S(2)}, u32[]{:S(2)}) %collective-permute-start.15) | collective-permute-done | bytes 65568 | tf_op jit(solution)/shard_map/ppermute | solution.py:229
  38.5 0.0 collective-permute-done.17
  38.6 0.1 collective-permute-start.20
  38.6 1.2 %collective-permute-done.20 = f32[32,256]{1,0:T(8,128)S(1)} collective-permute-done((f32[32,256]{1,0:T(8,128)S(1)}, f32[32,256]{1,0:T(8,128)S(1)}, u32[]{:S(2)}, u32[]{:S(2)}) %collective-permute-start.20) | collective-permute-done | bytes 32800 | tf_op jit(solution)/shard_map/ppermute | solution.py:233
  39.8 0.6 %fusion = f32[1,32,256]{2,1,0:T(8,128)} fusion(f32[32,256]{1,0:T(8,128)S(1)} %collective-permute-done.20, f32[64,256]{1,0:T(8,128)S(1)} %add_add_fusion), kind=kLoop, calls=%fused_computation.3 | loop fusion | flops 8192 | bytes 98304 | tf_op jit(solution)/shard_map/broadcast_in_dim | solution.py:234
  (14 shorter events, 0.1 us)
Async XLA Ops:
  0.6 5.7 %collective-permute-start = (bf16[32,256]{1,0:T(8,128)(2,1)}, bf16[32,256]{1,0:T(8,128)(2,1)S(1)}, u32[]{:S(2)}, u32[]{:S(2)}) collective-permute-start(bf16[32,256]{1,0:T(8,128)(2,1)} %bitcast.10), channel_id=1, source_target_pairs={{0,1},{1,0},{2,3},{3,2},{4,5},{5,4},{6,7},{7,6},{8,9},{9,8},{10,11... | collective-permute-start | bytes 49160 | tf_op jit(solution)/shard_map/ppermute | solution.py:160
  4.3 0.7 %copy-start.1 = (s32[1,1,20]{2,1,0:T(1,128)S(1)}, s32[1,1,20]{2,1,0:T(1,128)}, u32[]{:S(2)}) copy-start(s32[1,1,20]{2,1,0:T(1,128)} %param.8) | copy-start | bytes 244
  4.3 0.7 %copy-start.2 = (s32[1,1,20,1]{2,3,1,0:T(1,128)S(1)}, s32[1,1,20,1]{2,3,1,0:T(1,128)}, u32[]{:S(2)}) copy-start(s32[1,1,20,1]{2,3,1,0:T(1,128)} %param.9) | copy-start | bytes 244
  4.3 0.7 %copy-start.3 = (s32[1,4]{1,0:T(1,128)S(1)}, s32[1,4]{1,0:T(1,128)}, u32[]{:S(2)}) copy-start(s32[1,4]{1,0:T(1,128)} %owners_hbm.1) | copy-start | bytes 52
  5.0 1.1 %copy-start = (bf16[1,1,20,128,128]{4,3,2,1,0:T(8,128)(2,1)S(1)}, bf16[1,1,20,128,128]{4,3,2,1,0:T(8,128)(2,1)}, u32[]{:S(2)}) copy-start(bf16[1,1,20,128,128]{4,3,2,1,0:T(8,128)(2,1)} %param.7) | copy-start | bytes 1966084
  6.1 1.5 %copy-start.4 = (bf16[1,32,256]{2,1,0:T(8,128)(2,1)S(1)}, bf16[1,32,256]{2,1,0:T(8,128)(2,1)}, u32[]{:S(2)}) copy-start(bf16[1,32,256]{2,1,0:T(8,128)(2,1)} %param.6) | copy-start | bytes 49156
  6.4 16.3 %collective-permute-start.11 = (bf16[2576,128]{1,0:T(8,128)(2,1)S(1)}, bf16[2576,128]{1,0:T(8,128)(2,1)S(1)}, u32[]{:S(2)}, u32[]{:S(2)}) collective-permute-start(bf16[2576,128]{1,0:T(8,128)(2,1)S(1)} %get-tuple-element.18.refs_9_), channel_id=1, source_target_pairs={{0,1},{1,0},{2,3},{3,2},{4,5},{5,4},{6,7},{7,6},{8,9},{9,8},{10,11... | collective-permute-start | bytes 1978376 | tf_op jit(solution)/shard_map/ppermute | solution.py:187
  7.6 1.2 %collective-permute-start.1 = (bf16[32,256]{1,0:T(8,128)(2,1)S(1)}, bf16[32,256]{1,0:T(8,128)(2,1)S(1)}, u32[]{:S(2)}, u32[]{:S(2)}) collective-permute-start(bf16[32,256]{1,0:T(8,128)(2,1)S(1)} %bitcast.11), channel_id=1, source_target_pairs={{0,2},{2,0},{4,6},{6,4},{8,10},{10,8},{12,14},{14,12},{16,18},{18,... | collective-permute-start | bytes 49160 | tf_op jit(solution)/shard_map/ppermute | solution.py:161
  7.6 1.3 %collective-permute-start.2 = (bf16[32,256]{1,0:T(8,128)(2,1)S(1)}, bf16[32,256]{1,0:T(8,128)(2,1)S(1)}, u32[]{:S(2)}, u32[]{:S(2)}) collective-permute-start(bf16[32,256]{1,0:T(8,128)(2,1)S(1)} %collective-permute-done), channel_id=1, source_target_pairs={{0,2},{2,0},{4,6},{6,4},{8,10},{10,8},{12,14},{14,12},{16,18},{18,... | collective-permute-start | bytes 49160 | tf_op jit(solution)/shard_map/ppermute | solution.py:188
  8.9 7.3 %collective-permute-start.6 = (bf16[128,256]{1,0:T(8,128)(2,1)S(1)}, bf16[128,256]{1,0:T(8,128)(2,1)S(1)}, u32[]{:S(2)}, u32[]{:S(2)}) collective-permute-start(bf16[128,256]{1,0:T(8,128)(2,1)S(1)} %pad_maximum_fusion), channel_id=1, source_target_pairs={{0,28},{2,22},{4,24},{6,18},{8,20},{10,30},{12,16},{14,26},{16,12}... | collective-permute-start | bytes 196616 | tf_op jit(solution)/shard_map/ppermute | solution.py:192
  13.5 6.2 %collective-permute-start.5 = (bf16[128,256]{1,0:T(8,128)(2,1)S(1)}, bf16[128,256]{1,0:T(8,128)(2,1)S(1)}, u32[]{:S(2)}, u32[]{:S(2)}) collective-permute-start(bf16[128,256]{1,0:T(8,128)(2,1)S(1)} %pad_maximum_fusion), channel_id=1, source_target_pairs={{0,12},{2,26},{4,8},{6,30},{8,4},{10,18},{12,0},{14,22},{16,28},{1... | collective-permute-start | bytes 196616 | tf_op jit(solution)/shard_map/ppermute | solution.py:192
  13.5 6.2 %collective-permute-start.4 = (bf16[128,256]{1,0:T(8,128)(2,1)S(1)}, bf16[128,256]{1,0:T(8,128)(2,1)S(1)}, u32[]{:S(2)}, u32[]{:S(2)}) collective-permute-start(bf16[128,256]{1,0:T(8,128)(2,1)S(1)} %pad_maximum_fusion), channel_id=1, source_target_pairs={{0,16},{2,6},{4,20},{6,2},{8,24},{10,14},{12,28},{14,10},{16,0},{1... | collective-permute-start | bytes 196616 | tf_op jit(solution)/shard_map/ppermute | solution.py:192
  14.2 6.0 %collective-permute-start.3 = (bf16[128,256]{1,0:T(8,128)(2,1)S(1)}, bf16[128,256]{1,0:T(8,128)(2,1)S(1)}, u32[]{:S(2)}, u32[]{:S(2)}) collective-permute-start(bf16[128,256]{1,0:T(8,128)(2,1)S(1)} %pad_maximum_fusion), channel_id=1, source_target_pairs={{0,0},{2,10},{4,4},{6,14},{8,8},{10,2},{12,12},{14,6},{16,16},{18,... | collective-permute-start | bytes 196616 | tf_op jit(solution)/shard_map/ppermute | solution.py:192
  16.2 4.1 %collective-permute-start.10 = (bf16[128,256]{1,0:T(8,128)(2,1)S(1)}, bf16[128,256]{1,0:T(8,128)(2,1)S(1)}, u32[]{:S(2)}, u32[]{:S(2)}) collective-permute-start(bf16[128,256]{1,0:T(8,128)(2,1)S(1)} %collective-permute-done.6.refs_3_), channel_id=1, source_target_pairs={{0,2},{2,0},{4,6},{6,4},{8,10},{10,8},{12,14},{14,12},{16,18},{18,... | collective-permute-start | bytes 196616 | tf_op jit(solution)/shard_map/ppermute | solution.py:194
  19.7 1.3 %collective-permute-start.9 = (bf16[128,256]{1,0:T(8,128)(2,1)S(1)}, bf16[128,256]{1,0:T(8,128)(2,1)S(1)}, u32[]{:S(2)}, u32[]{:S(2)}) collective-permute-start(bf16[128,256]{1,0:T(8,128)(2,1)S(1)} %collective-permute-done.5.refs_2_), channel_id=1, source_target_pairs={{0,2},{2,0},{4,6},{6,4},{8,10},{10,8},{12,14},{14,12},{16,18},{18,... | collective-permute-start | bytes 196616 | tf_op jit(solution)/shard_map/ppermute | solution.py:194
  19.7 1.4 %collective-permute-start.8 = (bf16[128,256]{1,0:T(8,128)(2,1)S(1)}, bf16[128,256]{1,0:T(8,128)(2,1)S(1)}, u32[]{:S(2)}, u32[]{:S(2)}) collective-permute-start(bf16[128,256]{1,0:T(8,128)(2,1)S(1)} %collective-permute-done.4.refs_1_), channel_id=1, source_target_pairs={{0,2},{2,0},{4,6},{6,4},{8,10},{10,8},{12,14},{14,12},{16,18},{18,... | collective-permute-start | bytes 196616 | tf_op jit(solution)/shard_map/ppermute | solution.py:194
  20.3 1.3 %collective-permute-start.7 = (bf16[128,256]{1,0:T(8,128)(2,1)S(1)}, bf16[128,256]{1,0:T(8,128)(2,1)S(1)}, u32[]{:S(2)}, u32[]{:S(2)}) collective-permute-start(bf16[128,256]{1,0:T(8,128)(2,1)S(1)} %collective-permute-done.3.refs_0_), channel_id=1, source_target_pairs={{0,2},{2,0},{4,6},{6,4},{8,10},{10,8},{12,14},{14,12},{16,18},{18,... | collective-permute-start | bytes 196616 | tf_op jit(solution)/shard_map/ppermute | solution.py:194
  26.1 1.3 %collective-permute-start.12 = (f32[64,256]{1,0:T(8,128)S(1)}, f32[64,256]{1,0:T(8,128)S(1)}, u32[]{:S(2)}, u32[]{:S(2)}) collective-permute-start(f32[64,256]{1,0:T(8,128)S(1)} %get-tuple-element.21), channel_id=1, source_target_pairs={{0,2},{2,0},{4,6},{6,4},{8,10},{10,8},{12,14},{14,12},{16,18},{18,... | collective-permute-start | bytes 196616 | tf_op jit(solution)/shard_map/ppermute | solution.py:226
  26.2 6.1 %collective-permute-start.14 = (f32[64,256]{1,0:T(8,128)S(1)}, f32[64,256]{1,0:T(8,128)S(1)}, u32[]{:S(2)}, u32[]{:S(2)}) collective-permute-start(f32[64,256]{1,0:T(8,128)S(1)} %get-tuple-element.23), channel_id=1, source_target_pairs={{0,2},{2,0},{4,6},{6,4},{8,10},{10,8},{12,14},{14,12},{16,18},{18,... | collective-permute-start | bytes 196616 | tf_op jit(solution)/shard_map/ppermute | solution.py:226
  26.7 5.7 %collective-permute-start.16 = (f32[64,256]{1,0:T(8,128)S(1)}, f32[64,256]{1,0:T(8,128)S(1)}, u32[]{:S(2)}, u32[]{:S(2)}) collective-permute-start(f32[64,256]{1,0:T(8,128)S(1)} %get-tuple-element.25), channel_id=1, source_target_pairs={{0,2},{2,0},{4,6},{6,4},{8,10},{10,8},{12,14},{14,12},{16,18},{18,... | collective-permute-start | bytes 196616 | tf_op jit(solution)/shard_map/ppermute | solution.py:226
  26.8 6.3 %collective-permute-start.18 = (f32[64,256]{1,0:T(8,128)S(1)}, f32[64,256]{1,0:T(8,128)S(1)}, u32[]{:S(2)}, u32[]{:S(2)}) collective-permute-start(f32[64,256]{1,0:T(8,128)S(1)} %get-tuple-element.27), channel_id=1, source_target_pairs={{0,2},{2,0},{4,6},{6,4},{8,10},{10,8},{12,14},{14,12},{16,18},{18,... | collective-permute-start | bytes 196616 | tf_op jit(solution)/shard_map/ppermute | solution.py:226
  27.5 7.3 %collective-permute-start.13 = (f32[64,256]{1,0:T(8,128)S(1)}, f32[64,256]{1,0:T(8,128)S(1)}, u32[]{:S(2)}, u32[]{:S(2)}) collective-permute-start(f32[64,256]{1,0:T(8,128)S(1)} %add.24), channel_id=1, source_target_pairs={{0,28},{2,22},{4,24},{6,18},{8,20},{10,30},{12,16},{14,26},{16,12}... | collective-permute-start | bytes 196616 | tf_op jit(solution)/shard_map/ppermute | solution.py:229
  32.3 6.2 %collective-permute-start.15 = (f32[64,256]{1,0:T(8,128)S(1)}, f32[64,256]{1,0:T(8,128)S(1)}, u32[]{:S(2)}, u32[]{:S(2)}) collective-permute-start(f32[64,256]{1,0:T(8,128)S(1)} %add.25), channel_id=1, source_target_pairs={{0,12},{2,26},{4,8},{6,30},{8,4},{10,18},{12,0},{14,22},{16,28},{1... | collective-permute-start | bytes 196616 | tf_op jit(solution)/shard_map/ppermute | solution.py:229
  32.4 6.1 %collective-permute-start.17 = (f32[64,256]{1,0:T(8,128)S(1)}, f32[64,256]{1,0:T(8,128)S(1)}, u32[]{:S(2)}, u32[]{:S(2)}) collective-permute-start(f32[64,256]{1,0:T(8,128)S(1)} %add.27), channel_id=1, source_target_pairs={{0,16},{2,6},{4,20},{6,2},{8,24},{10,14},{12,28},{14,10},{16,0},{1... | collective-permute-start | bytes 196616 | tf_op jit(solution)/shard_map/ppermute | solution.py:229
  33.1 5.4 %collective-permute-start.19 = (f32[64,256]{1,0:T(8,128)S(1)}, f32[64,256]{1,0:T(8,128)S(1)}, u32[]{:S(2)}, u32[]{:S(2)}) collective-permute-start(f32[64,256]{1,0:T(8,128)S(1)} %add.29), channel_id=1, source_target_pairs={{0,0},{2,10},{4,4},{6,14},{8,8},{10,2},{12,12},{14,6},{16,16},{18,... | collective-permute-start | bytes 196616 | tf_op jit(solution)/shard_map/ppermute | solution.py:229
  38.6 1.3 %collective-permute-start.20 = (f32[32,256]{1,0:T(8,128)S(1)}, f32[32,256]{1,0:T(8,128)S(1)}, u32[]{:S(2)}, u32[]{:S(2)}) collective-permute-start(f32[32,256]{1,0:T(8,128)S(1)} %slice.9), channel_id=1, source_target_pairs={{0,2},{2,0},{4,6},{6,4},{8,10},{10,8},{12,14},{14,12},{16,18},{18,... | collective-permute-start | bytes 98312 | tf_op jit(solution)/shard_map/ppermute | solution.py:233

commit v3 on v0

--- a/solution.py
+++ b/solution.py
@@ -1,10 +1,240 @@
 import jax
 import jax.numpy as jnp
 from jax import lax
+from jax.experimental import pallas as pl
+from jax.experimental.pallas import tpu as pltpu
 from jax.sharding import PartitionSpec as P
 
 
-def shards(q_panel, tiles, tile_rows, tile_cols, tile_count, owner_map):
+LANES = 128
+SCALE_ROWS = 16
+VMEM_BYTES = 24 << 20
+
+
+def sides_of(chips):
+    sides = ([], [])
+    load = [0, 0]
+    for k in sorted(range(chips), key=lambda k: -(k // 2 + k % 2)):
+        open_sides = [c for c in range(2) if len(sides[c]) < chips // 2]
+        c = min(open_sides, key=lambda c: load[c])
+        sides[c].append(k)
+        load[c] += k // 2 + k % 2
+    return sides
+
+
+def own_place(sides, shard):
+    place = lax.axis_index("blk")
+    core, chip = lax.rem(place, 2), lax.div(place, 2)
+
+    def rows_of(step, side, owner):
+        which = lax.bitwise_xor(chip, jnp.where(side == 0, sides[0][step], sides[1][step]))
+        return pl.ds(pl.multiple_of(which * (2 * shard) + owner * shard, shard), shard)
+
+    return core, rows_of
+
+
+def coded(x):
+    top = jnp.max(jnp.abs(x), axis=0, keepdims=True)
+    power = jnp.ceil(jnp.log2(jnp.maximum(top, 1e-30)))
+    whole = jnp.round(x * jnp.exp2(15.0 - power))
+    whole = jnp.clip(whole, -32767.0, 32767.0)
+    return whole.astype(jnp.int32).astype(jnp.int16), power
+
+
+def decoded(whole, power):
+    return whole.astype(jnp.int32).astype(jnp.float32) * jnp.exp2(power - 15.0)
+
+
+def dot(a, b):
+    return jnp.dot(a, b, preferred_element_type=jnp.float32)
+
+
+def copy_kernel(source, target):
+    target[...] = source[...]
+
+
+def at_hand_kernel(rows, cols, count, owners, tiles, notes, tiles_copy):
+    notes[...] = jnp.zeros_like(notes)
+    notes[0:1, 0 : rows.shape[1]] = rows[...]
+    notes[1:2, 0 : cols.shape[1]] = cols[...]
+    notes[2:3, 0:1] = count[...]
+    notes[3:4, 0 : owners.shape[1]] = owners[...]
+    tiles_copy[...] = tiles[...]
+
+
+def each_tile(notes, tiles):
+    total, size = tiles.shape[:2]
+    for t in range(total):
+        tile = jnp.where(t < notes[2, 0], tiles[t], jnp.zeros_like(tiles[t]))
+        yield tile, *(
+            pl.ds(pl.multiple_of(notes[which, t] * size, size), size) for which in (0, 1)
+        )
+
+
+def partial_kernel(rounds, sides, group, *refs):
+    direct, relayed = refs[:rounds][::-1], refs[rounds : 2 * rounds][::-1]
+    notes, tiles, partial, sent, q = refs[2 * rounds :]
+    shard = direct[0].shape[0] // 2
+    core, rows_of = own_place(sides, shard)
+    for step in range(rounds):
+        for ref, side in ((direct[step], core), (relayed[step], 1 - core)):
+            q[rows_of(step, side, side), :] = ref[0:shard, :]
+            q[rows_of(step, side, 1 - side), :] = ref[shard : 2 * shard, :]
+    height = partial.shape[0]
+    size = height // group
+    partial[...] = jnp.zeros_like(partial)
+    for tile, rows, cols in each_tile(notes, tiles):
+        partial[rows, :] = partial[rows, :] + dot(tile, q[cols, :])
+    powers = []
+    for k in range(group):
+        rows = slice(k * size, (k + 1) * size)
+        sent[rows, :], power = coded(partial[rows, :])
+        powers.append(power)
+    powers.append(jnp.zeros((SCALE_ROWS - group, partial.shape[1]), jnp.float32))
+    sent[height:, :] = jnp.concatenate(powers, axis=0).astype(jnp.int32).astype(jnp.int16)
+
+
+def turned_kernel(notes, tiles, high, low, a):
+    a[...] = jnp.zeros_like(a)
+    for tile, rows, cols in each_tile(notes, tiles):
+        a[rows, cols] = a[rows, cols] + tile.astype(jnp.float32)
+    turned = a[...].T
+    high[...] = turned.astype(high.dtype)
+    low[...] = (turned - high[...].astype(jnp.float32)).astype(low.dtype)
+
+
+def product_kernel(rounds, sides, group, *refs):
+    partial, came, high, low, y = refs[:5]
+    keep, give = refs[5 : 5 + rounds], refs[5 + rounds : 5 + 2 * rounds]
+    z = refs[5 + 2 * rounds]
+    height = partial.shape[0]
+    size = height // group
+    powers = came[height:, :].astype(jnp.int32).astype(jnp.float32)
+    for k in range(group):
+        rows = slice(k * size, (k + 1) * size)
+        term = decoded(came[rows, :], powers[k : k + 1, :])
+        y[rows, :] = (partial[rows, :] + term).astype(y.dtype)
+    z[...] = dot(high[...], y[...]) + dot(low[...], y[...])
+    shard = keep[0].shape[0] // 2
+    core, rows_of = own_place(sides, shard)
+    for step in range(rounds):
+        for ref, side in ((keep[step], core), (give[step], 1 - core)):
+            ref[0:shard, :] = z[rows_of(step, side, side), :]
+            ref[shard : 2 * shard, :] = z[rows_of(step, side, 1 - side), :]
+
+
+def owned_kernel(group, y, notes, y_out):
+    size = y.shape[0] // group
+    mine = group // 2
+    for k in range(group):
+        slot = notes[3, k]
+
+        @pl.when(lax.div(slot, mine) == lax.axis_index("rows"))
+        def _():
+            at = pl.multiple_of(lax.rem(slot, mine) * size, size)
+            y_out[pl.ds(at, size), :] = y[k * size : (k + 1) * size, :]
+
+
+def paired(q_panel, tiles, tile_rows, tile_cols, tile_count, owner_map):
+    devices = lax.axis_size("blk")
+    chips = devices // 2
+    rounds = chips // 2
+    sides = sides_of(chips)
+    shard, rank = q_panel.shape[1:]
+    stack = tiles[0, 0]
+    total, size = stack.shape[:2]
+    group = owner_map.shape[1]
+    width = devices * shard
+    height = group * size
+    across = [(0, 1), (1, 0)]
+    sibling = [(i, i ^ 1) for i in range(devices)]
+    vmem = pl.BlockSpec(memory_space=pltpu.VMEM)
+
+    def to_chips(step):
+        return [
+            (2 * m + c, 2 * (m ^ sides[c][step]) + c)
+            for m in range(chips)
+            for c in range(2)
+        ]
+
+    def call(body, name, outs, args, scratch=()):
+        return pl.pallas_call(
+            body,
+            out_shape=[jax.ShapeDtypeStruct(*out) for out in outs],
+            in_specs=[vmem] * len(args),
+            out_specs=[vmem] * len(outs),
+            scratch_shapes=list(scratch),
+            compiler_params=pltpu.CompilerParams(vmem_limit_bytes=VMEM_BYTES),
+            name=name,
+        )(*args)
+
+    q_own = q_panel[0]
+    q_sibling = lax.ppermute(q_own, "blk", sibling)
+    (q_copy,) = call(copy_kernel, "own_rows", [(q_own.shape, q_own.dtype)], [q_own])
+    block = jnp.concatenate([q_copy, q_sibling], axis=0)
+    direct = [lax.ppermute(block, "blk", to_chips(step)) for step in range(rounds)]
+
+    stack, direct[0] = lax.optimization_barrier((stack, direct[0]))
+    notes, stack = call(
+        at_hand_kernel,
+        "at_hand",
+        [((8, LANES), jnp.int32), (stack.shape, stack.dtype)],
+        [
+            tile_rows.reshape(1, total),
+            tile_cols.reshape(1, total),
+            tile_count,
+            owner_map,
+            stack,
+        ],
+    )
+    direct[1], notes, stack = lax.optimization_barrier((direct[1], notes, stack))
+    relayed = [lax.ppermute(one, "blk", sibling) for one in direct]
+
+    partial, sent = call(
+        lambda *refs: partial_kernel(rounds, sides, group, *refs),
+        "partial",
+        [((height, rank), jnp.float32), ((height + SCALE_ROWS, rank), jnp.int16)],
+        [*direct[::-1], *relayed[::-1], notes, stack],
+        [pltpu.VMEM((width, rank), q_own.dtype)],
+    )
+    came = lax.ppermute(sent, "rows", across)
+    notes, stack, sent = lax.optimization_barrier((notes, stack, sent))
+    turned = call(
+        turned_kernel,
+        "turned",
+        [((width, height), stack.dtype)] * 2,
+        [notes, stack],
+        [pltpu.VMEM((height, width), jnp.float32)],
+    )
+    y, *pieces = call(
+        lambda *refs: product_kernel(rounds, sides, group, *refs),
+        "products",
+        [((height, rank), jnp.bfloat16)]
+        + [((2 * shard, rank), jnp.float32)] * (2 * rounds),
+        [partial, came, *turned],
+        [pltpu.VMEM((width, rank), jnp.float32)],
+    )
+    keep, give = pieces[:rounds], pieces[rounds:]
+    given = [lax.ppermute(one, "blk", sibling) for one in give]
+    arrived = [
+        lax.ppermute(keep[step] + given[step], "blk", to_chips(step)) for step in range(rounds)
+    ]
+    y, arrived[0] = lax.optimization_barrier((y, arrived[0]))
+    (y_owned,) = call(
+        lambda *refs: owned_kernel(group, *refs),
+        "owned",
+        [((height // 2, rank), jnp.bfloat16)],
+        [y, notes],
+    )
+    arrived[1], y_owned = lax.optimization_barrier((arrived[1], y_owned))
+    summed = arrived[0]
+    for step in range(1, rounds):
+        summed = summed + arrived[step]
+    z_share = summed[:shard] + lax.ppermute(summed[shard:], "blk", sibling)
+    return (y_owned[None], z_share[None])
+
+
+def general(q_panel, tiles, tile_rows, tile_cols, tile_count, owner_map):
     panel_rows = q_panel.shape[1]
     tile_stack = tiles[0, 0]
     tile_total = tile_stack.shape[0]
@@ -49,8 +279,10 @@
         P("blk", "rows"),
         P("blk", None),
     )
+    devices = mesh.shape["blk"]
+    fits = mesh.shape["rows"] == 2 and devices >= 8 and devices & (devices - 1) == 0
     return jax.shard_map(
-        shards,
+        paired if fits else general,
         mesh=mesh,
         in_specs=placed,
         out_specs=(P("blk", "rows", None), P("rows", "blk", None)),

time: 124 us -> 38.7 us (0.31)
  waiting for transfers between devices: 66.3 us -> 12.2 us
  blocking collectives: 29.9 us -> 0 us
  starting transfers between devices: 0.08 us -> 18.6 us
  between operations: 14.7 us -> 1.41 us
  matrix products: 4.93 us -> 0 us
  other arithmetic: 4.19 us -> 0.68 us
  Pallas kernels: 0 us -> 3.01 us
    reduce_scatter x2 -> x0, waiting for transfers between devices: 66.2 us -> none  [the longest x1 54.3 us: shards(): lax.psum_scatter(column_term, 'blk', scatter_dimension=0, tiled=True)]
    all_gather x2 -> x0, blocking collectives: 29.9 us -> none  [the longest x1 24 us: shards(): rows_in = lax.all_gather(q_panel, 'blk', axis=1, tiled=True)[0]]
    ppermute x0 -> x19, starting transfers between devices: none -> 18.6 us  [the longest x4 7.11 us: paired(): lax.ppermute(block, 'blk', to_chips(step))]
    ppermute x0 -> x19, waiting for transfers between devices: none -> 12.2 us  [the longest x1 6.37 us: paired(): came = lax.ppermute(sent, 'rows', across)]
    dot_general x3 -> x0, matrix products: 4.93 us -> none  [the longest x1 1.79 us: shards(): lax.dot_general(local_matrix, y_group.astype(jnp.float32), (((0,), (0,)),...]
    pallas_call x0 -> x6, Pallas kernels: none -> 3.01 us  [call(): pl.pallas_call(body, out_shape=[jax.ShapeDtypeStruct(*out) for out in out...]
    gather x1 -> x0, other arithmetic: 2.55 us -> none  [shards(): slot_of_tile = owner_map[0][tile_rows[0, 0]]]
    unnamed x8 -> x10, local copies, waits for them, and re-layouts: 2.87 us -> 2.49 us
  transfers between devices with their start and end apart: 2 -> 19, of which waited for: 2 -> 10; matrix products, arithmetic and copies ran while one was open for 1% -> 0% of each run, Pallas kernels for 0% -> 5%
where the time goes in v3:
time: 38.7 us; the launch traced here: 38.4 us
  starting transfers between devices  18.6 us (48%)
  waiting for transfers between devices  12.2 us (32%)
  Pallas kernels  3.01 us (8%)
  local copies, waits for them, and re-layouts  2.49 us (6%)
  between operations  1.41 us (4%)
  other arithmetic  0.68 us (2%)
    ppermute x4, starting transfers between devices, paired(): lax.ppermute(block, 'blk', to_chips(step))  7.11 us
    ppermute x1, waiting for transfers between devices, paired(): came = lax.ppermute(sent, 'rows', across)  6.37 us
    ppermute x4, starting transfers between devices, paired(): lax.ppermute(keep[step] + given[step], 'blk', to_chips(step))  6.13 us
    ppermute x4, waiting for transfers between devices, paired(): lax.ppermute(keep[step] + given[step], 'blk', to_chips(step))  3.28 us
    pallas_call x6, Pallas kernels, call(): pl.pallas_call(body, out_shape=[jax.ShapeDtypeStruct(*out) for out in out...  3.01 us
    unnamed x10, local copies, waits for them, and re-layouts  2.49 us
    ppermute x4, starting transfers between devices, paired(): relayed = [lax.ppermute(one, 'blk', sibling) for one in direct]  1.79 us
    ppermute x1, starting transfers between devices, paired(): came = lax.ppermute(sent, 'rows', across)  1.56 us
  transfers between devices with their start and end apart: 19, of which 10 were waited for; matrix products, arithmetic and copies ran while one was open for 0% of the time, Pallas kernels for 5%

profile of v3, /device:TPU:0, one launch (start us, length us, event | category | flops | bytes accessed | tf_op | source)
XLA Modules:
  0.0 38.4 jit_solution(10041260260538049659)
XLA Ops:
  0.6 0.5 %collective-permute-start = (bf16[32,256]{1,0:T(8,128)(2,1)}, bf16[32,256]{1,0:T(8,128)(2,1)S(1)}, u32[]{:S(2)}, u32[]{:S(2)}) collective-permute-start(bf16[32,256]{1,0:T(8,128)(2,1)} %bitcast.8), channel_id=1, source_target_pairs={{0,2},{2,0},{4,6},{6,4},{8,10},{10,8},{12,14},{14,12},{16,18},{18,... | collective-permute-start | bytes 49160 | tf_op jit(solution)/shard_map/ppermute | solution.py:172
  1.1 0.7 %copy-done.1 = bf16[1,32,256]{2,1,0:T(8,128)(2,1)S(1)} copy-done((bf16[1,32,256]{2,1,0:T(8,128)(2,1)S(1)}, bf16[1,32,256]{2,1,0:T(8,128)(2,1)}, u32[]{:S(2)}) %copy-start.1) | copy-done | bytes 16408
  1.9 0.3 collective-permute-done
  2.2 5.9 %collective-permute-start.4 = (bf16[64,256]{1,0:T(8,128)(2,1)S(1)}, bf16[64,256]{1,0:T(8,128)(2,1)S(1)}, u32[]{:S(2)}, u32[]{:S(2)}) collective-permute-start(bf16[64,256]{1,0:T(8,128)(2,1)S(1)} %pad_maximum_fusion), channel_id=1, source_target_pairs={{0,28},{2,22},{4,24},{6,18},{8,20},{10,30},{12,16},{14,26},{16,12}... | collective-permute-start | bytes 98312 | tf_op jit(solution)/shard_map/ppermute | solution.py:175
  8.1 0.0 collective-permute-start.3
  8.1 0.6 %collective-permute-start.2 = (bf16[64,256]{1,0:T(8,128)(2,1)S(1)}, bf16[64,256]{1,0:T(8,128)(2,1)S(1)}, u32[]{:S(2)}, u32[]{:S(2)}) collective-permute-start(bf16[64,256]{1,0:T(8,128)(2,1)S(1)} %pad_maximum_fusion), channel_id=1, source_target_pairs={{0,16},{2,6},{4,20},{6,2},{8,24},{10,14},{12,28},{14,10},{16,0},{1... | collective-permute-start | bytes 98312 | tf_op jit(solution)/shard_map/ppermute | solution.py:175
  8.7 0.7 %collective-permute-start.1 = (bf16[64,256]{1,0:T(8,128)(2,1)S(1)}, bf16[64,256]{1,0:T(8,128)(2,1)S(1)}, u32[]{:S(2)}, u32[]{:S(2)}) collective-permute-start(bf16[64,256]{1,0:T(8,128)(2,1)S(1)} %pad_maximum_fusion), channel_id=1, source_target_pairs={{0,0},{2,10},{4,4},{6,14},{8,8},{10,2},{12,12},{14,6},{16,16},{18,... | collective-permute-start | bytes 98312 | tf_op jit(solution)/shard_map/ppermute | solution.py:175
  10.0 0.0 collective-permute-done.4.refs_3_
  10.0 1.1 %collective-permute-start.8 = (bf16[64,256]{1,0:T(8,128)(2,1)S(1)}, bf16[64,256]{1,0:T(8,128)(2,1)S(1)}, u32[]{:S(2)}, u32[]{:S(2)}) collective-permute-start(bf16[64,256]{1,0:T(8,128)(2,1)S(1)} %collective-permute-done.4.refs_3_), channel_id=1, source_target_pairs={{0,2},{2,0},{4,6},{6,4},{8,10},{10,8},{12,14},{14,12},{16,18},{18,... | collective-permute-start | bytes 98312 | tf_op jit(solution)/shard_map/ppermute | solution.py:191
  11.1 0.6 %copy-done.2 = s32[1,1,20]{2,1,0:T(1,128)S(1)} copy-done((s32[1,1,20]{2,1,0:T(1,128)S(1)}, s32[1,1,20]{2,1,0:T(1,128)}, u32[]{:S(2)}) %copy-start.2) | copy-done | bytes 104
  11.8 0.0 copy-done.3
  11.8 0.0 copy-done.4
  11.8 1.1 %copy-done = bf16[1,1,20,128,128]{4,3,2,1,0:T(8,128)(2,1)S(1)} copy-done((bf16[1,1,20,128,128]{4,3,2,1,0:T(8,128)(2,1)S(1)}, bf16[1,1,20,128,128]{4,3,2,1,0:T(8,128)(2,1)}, u32[]{:S(2)}) %copy-start) | copy-done | bytes 655384
  12.9 0.0 collective-permute-done.3.refs_2_
  13.0 0.0 collective-permute-done.2.refs_1_
  13.0 0.1 collective-permute-start.6
  13.1 0.0 collective-permute-done.1.refs_0_
  13.1 0.5 %collective-permute-start.5 = (bf16[64,256]{1,0:T(8,128)(2,1)S(1)}, bf16[64,256]{1,0:T(8,128)(2,1)S(1)}, u32[]{:S(2)}, u32[]{:S(2)}) collective-permute-start(bf16[64,256]{1,0:T(8,128)(2,1)S(1)} %collective-permute-done.1.refs_0_), channel_id=1, source_target_pairs={{0,2},{2,0},{4,6},{6,4},{8,10},{10,8},{12,14},{14,12},{16,18},{18,... | collective-permute-start | bytes 98312 | tf_op jit(solution)/shard_map/ppermute | solution.py:191
  13.6 0.1 collective-permute-start.7
  13.6 0.0 collective-permute-done.8.refs_7_
  13.6 0.6 %collective-permute-done.6.refs_5_ = bf16[64,256]{1,0:T(8,128)(2,1)S(1)} collective-permute-done((bf16[64,256]{1,0:T(8,128)(2,1)S(1)}, bf16[64,256]{1,0:T(8,128)(2,1)S(1)}, u32[]{:S(2)}, u32[]{:S(2)}) %collective-permute-start.6) | collective-permute-done | bytes 32800 | tf_op jit(solution)/shard_map/ppermute | solution.py:191
  14.2 0.2 collective-permute-done.5.refs_4_
  14.4 0.3 collective-permute-done.7.refs_6_
  14.8 0.8 %partial.1 = (f32[512,256]{1,0:T(8,128)S(1)}, s16[528,256]{1,0:T(8,128)(2,1)S(1)}) custom-call(bf16[64,256]{1,0:T(8,128)(2,1)S(1)} %collective-permute-done.1.refs_0_, bf16[64,256]{1,0:T(8,128)(2,1)S(1)} %collective-permute-done.2.refs_1_, bf16[64,256]{1,0:T(8,128)(2,1)S(1)} %collective-permute-done.3.refs_2_, ...), custom_call_target="tpu_custom_call" | custom-call | tf_op jit(solution)/shard_map/partial/pallas_call | solution.py:161
  15.5 1.6 %collective-permute-start.9 = (s16[528,256]{1,0:T(8,128)(2,1)S(1)}, s16[528,256]{1,0:T(8,128)(2,1)S(1)}, u32[]{:S(2)}, u32[]{:S(2)}) collective-permute-start(s16[528,256]{1,0:T(8,128)(2,1)S(1)} %get-tuple-element.36), channel_id=1, source_target_pairs={{0,1},{1,0},{2,3},{3,2},{4,5},{5,4},{6,7},{7,6},{8,9},{9,8},{10,11... | collective-permute-start | bytes 811016 | tf_op jit(solution)/shard_map/ppermute | solution.py:200
  17.1 0.7 %turned.1 = (bf16[512,512]{1,0:T(8,128)(2,1)S(1)}, bf16[512,512]{1,0:T(8,128)(2,1)S(1)}) custom-call(s32[8,128]{1,0:T(8,128)S(1)} %get-tuple-element.37.refs_8_.notes.refs_1_, bf16[20,128,128]{2,1,0:T(8,128)(2,1)S(1)} %get-tuple-element.38.refs_9_.tiles), custom_call_target="tpu_custom_call" | custom-call | tf_op jit(solution)/shard_map/turned/pallas_call | solution.py:161
  17.8 6.4 %collective-permute-done.9.refs_1_ = s16[528,256]{1,0:T(8,128)(2,1)S(1)} collective-permute-done((s16[528,256]{1,0:T(8,128)(2,1)S(1)}, s16[528,256]{1,0:T(8,128)(2,1)S(1)}, u32[]{:S(2)}, u32[]{:S(2)}) %collective-permute-start.9) | collective-permute-done | bytes 270368 | tf_op jit(solution)/shard_map/ppermute | solution.py:200
  24.1 0.5 %products.1 = (bf16[512,256]{1,0:T(8,128)(2,1)S(1)}, f32[64,256]{1,0:T(8,128)S(1)}, f32[64,256]{1,0:T(8,128)S(1)}, f32[64,256]{1,0:T(8,128)S(1)}, f32[64,256]{1,...) custom-call(f32[512,256]{1,0:T(8,128)S(1)} %get-tuple-element.35.ref, ...), custom_call_target="tpu_custom_call" | custom-call | tf_op jit(solution)/shard_map/products/pallas_call | solution.py:161
  24.6 0.1 collective-permute-start.12
  24.7 0.5 %collective-permute-start.10 = (f32[64,256]{1,0:T(8,128)S(1)}, f32[64,256]{1,0:T(8,128)S(1)}, u32[]{:S(2)}, u32[]{:S(2)}) collective-permute-start(f32[64,256]{1,0:T(8,128)S(1)} %get-tuple-element.42), channel_id=1, source_target_pairs={{0,2},{2,0},{4,6},{6,4},{8,10},{10,8},{12,14},{14,12},{16,18},{18,... | collective-permute-start | bytes 196616 | tf_op jit(solution)/shard_map/ppermute | solution.py:218
  25.2 0.1 collective-permute-start.14
  25.3 0.4 %collective-permute-start.16 = (f32[64,256]{1,0:T(8,128)S(1)}, f32[64,256]{1,0:T(8,128)S(1)}, u32[]{:S(2)}, u32[]{:S(2)}) collective-permute-start(f32[64,256]{1,0:T(8,128)S(1)} %get-tuple-element.53), channel_id=1, source_target_pairs={{0,2},{2,0},{4,6},{6,4},{8,10},{10,8},{12,14},{14,12},{16,18},{18,... | collective-permute-start | bytes 196616 | tf_op jit(solution)/shard_map/ppermute | solution.py:218
  25.7 0.2 collective-permute-done.12
  26.0 4.1 %collective-permute-start.13 = (f32[64,256]{1,0:T(8,128)S(1)}, f32[64,256]{1,0:T(8,128)S(1)}, u32[]{:S(2)}, u32[]{:S(2)}) collective-permute-start(f32[64,256]{1,0:T(8,128)S(1)} %add.25), channel_id=1, source_target_pairs={{0,28},{2,22},{4,24},{6,18},{8,20},{10,30},{12,16},{14,26},{16,12}... | collective-permute-start | bytes 196616 | tf_op jit(solution)/shard_map/ppermute | solution.py:220
  30.0 0.0 collective-permute-done.10
  30.0 0.1 collective-permute-start.11
  30.1 0.0 collective-permute-done.14
  30.1 1.3 %collective-permute-start.15 = (f32[64,256]{1,0:T(8,128)S(1)}, f32[64,256]{1,0:T(8,128)S(1)}, u32[]{:S(2)}, u32[]{:S(2)}) collective-permute-start(f32[64,256]{1,0:T(8,128)S(1)} %add.27), channel_id=1, source_target_pairs={{0,16},{2,6},{4,20},{6,2},{8,24},{10,14},{12,28},{14,10},{16,0},{1... | collective-permute-start | bytes 196616 | tf_op jit(solution)/shard_map/ppermute | solution.py:220
  31.5 0.0 collective-permute-done.16
  31.5 0.7 %collective-permute-start.17 = (f32[64,256]{1,0:T(8,128)S(1)}, f32[64,256]{1,0:T(8,128)S(1)}, u32[]{:S(2)}, u32[]{:S(2)}) collective-permute-start(f32[64,256]{1,0:T(8,128)S(1)} %add.29), channel_id=1, source_target_pairs={{0,0},{2,10},{4,4},{6,14},{8,8},{10,2},{12,12},{14,6},{16,16},{18,... | collective-permute-start | bytes 196616 | tf_op jit(solution)/shard_map/ppermute | solution.py:220
  32.2 1.4 %collective-permute-done.13 = f32[64,256]{1,0:T(8,128)S(1)} collective-permute-done((f32[64,256]{1,0:T(8,128)S(1)}, f32[64,256]{1,0:T(8,128)S(1)}, u32[]{:S(2)}, u32[]{:S(2)}) %collective-permute-start.13) | collective-permute-done | bytes 65568 | tf_op jit(solution)/shard_map/ppermute | solution.py:220
  33.6 1.0 %owned.1 = bf16[256,256]{1,0:T(8,128)(2,1)} custom-call(bf16[512,256]{1,0:T(8,128)(2,1)S(1)} %get-tuple-element.46.refs_0_, s32[8,128]{1,0:T(8,128)S(1)} %get-tuple-element.37.refs_8_.notes.refs_1_), custom_call_target="tpu_custom_call" | custom-call | tf_op jit(solution)/shard_map/owned/pallas_call | solution.py:161
  34.7 0.6 %collective-permute-done.11 = f32[64,256]{1,0:T(8,128)S(1)} collective-permute-done((f32[64,256]{1,0:T(8,128)S(1)}, f32[64,256]{1,0:T(8,128)S(1)}, u32[]{:S(2)}, u32[]{:S(2)}) %collective-permute-start.11) | collective-permute-done | bytes 65568 | tf_op jit(solution)/shard_map/ppermute | solution.py:220
  35.3 1.2 %collective-permute-done.15 = f32[64,256]{1,0:T(8,128)S(1)} collective-permute-done((f32[64,256]{1,0:T(8,128)S(1)}, f32[64,256]{1,0:T(8,128)S(1)}, u32[]{:S(2)}, u32[]{:S(2)}) %collective-permute-start.15) | collective-permute-done | bytes 65568 | tf_op jit(solution)/shard_map/ppermute | solution.py:220
  36.5 0.0 collective-permute-done.17
  36.5 0.4 %collective-permute-start.18 = (f32[32,256]{1,0:T(8,128)S(1)}, f32[32,256]{1,0:T(8,128)S(1)}, u32[]{:S(2)}, u32[]{:S(2)}) collective-permute-start(f32[32,256]{1,0:T(8,128)S(1)} %slice.9), channel_id=1, source_target_pairs={{0,2},{2,0},{4,6},{6,4},{8,10},{10,8},{12,14},{14,12},{16,18},{18,... | collective-permute-start | bytes 98312 | tf_op jit(solution)/shard_map/ppermute | solution.py:233
  36.9 0.9 %collective-permute-done.18 = f32[32,256]{1,0:T(8,128)S(1)} collective-permute-done((f32[32,256]{1,0:T(8,128)S(1)}, f32[32,256]{1,0:T(8,128)S(1)}, u32[]{:S(2)}, u32[]{:S(2)}) %collective-permute-start.18) | collective-permute-done | bytes 32800 | tf_op jit(solution)/shard_map/ppermute | solution.py:233
  37.8 0.6 %fusion = f32[1,32,256]{2,1,0:T(8,128)} fusion(f32[32,256]{1,0:T(8,128)S(1)} %collective-permute-done.18, f32[64,256]{1,0:T(8,128)S(1)} %add_add_fusion), kind=kLoop, calls=%fused_computation.2 | loop fusion | flops 8192 | bytes 98304 | tf_op jit(solution)/shard_map/broadcast_in_dim | solution.py:234
  (14 shorter events, 0.1 us)
Async XLA Ops:
  0.6 1.6 %collective-permute-start = (bf16[32,256]{1,0:T(8,128)(2,1)}, bf16[32,256]{1,0:T(8,128)(2,1)S(1)}, u32[]{:S(2)}, u32[]{:S(2)}) collective-permute-start(bf16[32,256]{1,0:T(8,128)(2,1)} %bitcast.8), channel_id=1, source_target_pairs={{0,2},{2,0},{4,6},{6,4},{8,10},{10,8},{12,14},{14,12},{16,18},{18,... | collective-permute-start | bytes 49160 | tf_op jit(solution)/shard_map/ppermute | solution.py:172
  1.1 0.7 %copy-start.1 = (bf16[1,32,256]{2,1,0:T(8,128)(2,1)S(1)}, bf16[1,32,256]{2,1,0:T(8,128)(2,1)}, u32[]{:S(2)}) copy-start(bf16[1,32,256]{2,1,0:T(8,128)(2,1)} %param.6) | copy-start | bytes 49156
  2.2 7.8 %collective-permute-start.4 = (bf16[64,256]{1,0:T(8,128)(2,1)S(1)}, bf16[64,256]{1,0:T(8,128)(2,1)S(1)}, u32[]{:S(2)}, u32[]{:S(2)}) collective-permute-start(bf16[64,256]{1,0:T(8,128)(2,1)S(1)} %pad_maximum_fusion), channel_id=1, source_target_pairs={{0,28},{2,22},{4,24},{6,18},{8,20},{10,30},{12,16},{14,26},{16,12}... | collective-permute-start | bytes 98312 | tf_op jit(solution)/shard_map/ppermute | solution.py:175
  8.1 4.9 %collective-permute-start.3 = (bf16[64,256]{1,0:T(8,128)(2,1)S(1)}, bf16[64,256]{1,0:T(8,128)(2,1)S(1)}, u32[]{:S(2)}, u32[]{:S(2)}) collective-permute-start(bf16[64,256]{1,0:T(8,128)(2,1)S(1)} %pad_maximum_fusion), channel_id=1, source_target_pairs={{0,12},{2,26},{4,8},{6,30},{8,4},{10,18},{12,0},{14,22},{16,28},{1... | collective-permute-start | bytes 98312 | tf_op jit(solution)/shard_map/ppermute | solution.py:175
  8.1 4.9 %collective-permute-start.2 = (bf16[64,256]{1,0:T(8,128)(2,1)S(1)}, bf16[64,256]{1,0:T(8,128)(2,1)S(1)}, u32[]{:S(2)}, u32[]{:S(2)}) collective-permute-start(bf16[64,256]{1,0:T(8,128)(2,1)S(1)} %pad_maximum_fusion), channel_id=1, source_target_pairs={{0,16},{2,6},{4,20},{6,2},{8,24},{10,14},{12,28},{14,10},{16,0},{1... | collective-permute-start | bytes 98312 | tf_op jit(solution)/shard_map/ppermute | solution.py:175
  8.7 4.4 %collective-permute-start.1 = (bf16[64,256]{1,0:T(8,128)(2,1)S(1)}, bf16[64,256]{1,0:T(8,128)(2,1)S(1)}, u32[]{:S(2)}, u32[]{:S(2)}) collective-permute-start(bf16[64,256]{1,0:T(8,128)(2,1)S(1)} %pad_maximum_fusion), channel_id=1, source_target_pairs={{0,0},{2,10},{4,4},{6,14},{8,8},{10,2},{12,12},{14,6},{16,16},{18,... | collective-permute-start | bytes 98312 | tf_op jit(solution)/shard_map/ppermute | solution.py:175
  10.0 3.6 %collective-permute-start.8 = (bf16[64,256]{1,0:T(8,128)(2,1)S(1)}, bf16[64,256]{1,0:T(8,128)(2,1)S(1)}, u32[]{:S(2)}, u32[]{:S(2)}) collective-permute-start(bf16[64,256]{1,0:T(8,128)(2,1)S(1)} %collective-permute-done.4.refs_3_), channel_id=1, source_target_pairs={{0,2},{2,0},{4,6},{6,4},{8,10},{10,8},{12,14},{14,12},{16,18},{18,... | collective-permute-start | bytes 98312 | tf_op jit(solution)/shard_map/ppermute | solution.py:191
  11.1 0.7 %copy-start.2 = (s32[1,1,20]{2,1,0:T(1,128)S(1)}, s32[1,1,20]{2,1,0:T(1,128)}, u32[]{:S(2)}) copy-start(s32[1,1,20]{2,1,0:T(1,128)} %param.8) | copy-start | bytes 244
  11.1 0.7 %copy-start.3 = (s32[1,1,20,1]{2,3,1,0:T(1,128)S(1)}, s32[1,1,20,1]{2,3,1,0:T(1,128)}, u32[]{:S(2)}) copy-start(s32[1,1,20,1]{2,3,1,0:T(1,128)} %param.9) | copy-start | bytes 244
  11.1 0.7 %copy-start.4 = (s32[1,4]{1,0:T(1,128)S(1)}, s32[1,4]{1,0:T(1,128)}, u32[]{:S(2)}) copy-start(s32[1,4]{1,0:T(1,128)} %owners.1) | copy-start | bytes 52
  11.8 1.1 %copy-start = (bf16[1,1,20,128,128]{4,3,2,1,0:T(8,128)(2,1)S(1)}, bf16[1,1,20,128,128]{4,3,2,1,0:T(8,128)(2,1)}, u32[]{:S(2)}) copy-start(bf16[1,1,20,128,128]{4,3,2,1,0:T(8,128)(2,1)} %param.7) | copy-start | bytes 1966084
  13.0 1.3 %collective-permute-start.6 = (bf16[64,256]{1,0:T(8,128)(2,1)S(1)}, bf16[64,256]{1,0:T(8,128)(2,1)S(1)}, u32[]{:S(2)}, u32[]{:S(2)}) collective-permute-start(bf16[64,256]{1,0:T(8,128)(2,1)S(1)} %collective-permute-done.2.refs_1_), channel_id=1, source_target_pairs={{0,2},{2,0},{4,6},{6,4},{8,10},{10,8},{12,14},{14,12},{16,18},{18,... | collective-permute-start | bytes 98312 | tf_op jit(solution)/shard_map/ppermute | solution.py:191
  13.1 1.4 %collective-permute-start.5 = (bf16[64,256]{1,0:T(8,128)(2,1)S(1)}, bf16[64,256]{1,0:T(8,128)(2,1)S(1)}, u32[]{:S(2)}, u32[]{:S(2)}) collective-permute-start(bf16[64,256]{1,0:T(8,128)(2,1)S(1)} %collective-permute-done.1.refs_0_), channel_id=1, source_target_pairs={{0,2},{2,0},{4,6},{6,4},{8,10},{10,8},{12,14},{14,12},{16,18},{18,... | collective-permute-start | bytes 98312 | tf_op jit(solution)/shard_map/ppermute | solution.py:191
  13.6 1.2 %collective-permute-start.7 = (bf16[64,256]{1,0:T(8,128)(2,1)S(1)}, bf16[64,256]{1,0:T(8,128)(2,1)S(1)}, u32[]{:S(2)}, u32[]{:S(2)}) collective-permute-start(bf16[64,256]{1,0:T(8,128)(2,1)S(1)} %collective-permute-done.3.refs_2_), channel_id=1, source_target_pairs={{0,2},{2,0},{4,6},{6,4},{8,10},{10,8},{12,14},{14,12},{16,18},{18,... | collective-permute-start | bytes 98312 | tf_op jit(solution)/shard_map/ppermute | solution.py:191
  15.5 8.6 %collective-permute-start.9 = (s16[528,256]{1,0:T(8,128)(2,1)S(1)}, s16[528,256]{1,0:T(8,128)(2,1)S(1)}, u32[]{:S(2)}, u32[]{:S(2)}) collective-permute-start(s16[528,256]{1,0:T(8,128)(2,1)S(1)} %get-tuple-element.36), channel_id=1, source_target_pairs={{0,1},{1,0},{2,3},{3,2},{4,5},{5,4},{6,7},{7,6},{8,9},{9,8},{10,11... | collective-permute-start | bytes 811016 | tf_op jit(solution)/shard_map/ppermute | solution.py:200
  24.6 1.3 %collective-permute-start.12 = (f32[64,256]{1,0:T(8,128)S(1)}, f32[64,256]{1,0:T(8,128)S(1)}, u32[]{:S(2)}, u32[]{:S(2)}) collective-permute-start(f32[64,256]{1,0:T(8,128)S(1)} %get-tuple-element.45), channel_id=1, source_target_pairs={{0,2},{2,0},{4,6},{6,4},{8,10},{10,8},{12,14},{14,12},{16,18},{18,... | collective-permute-start | bytes 196616 | tf_op jit(solution)/shard_map/ppermute | solution.py:218
  24.7 5.3 %collective-permute-start.10 = (f32[64,256]{1,0:T(8,128)S(1)}, f32[64,256]{1,0:T(8,128)S(1)}, u32[]{:S(2)}, u32[]{:S(2)}) collective-permute-start(f32[64,256]{1,0:T(8,128)S(1)} %get-tuple-element.42), channel_id=1, source_target_pairs={{0,2},{2,0},{4,6},{6,4},{8,10},{10,8},{12,14},{14,12},{16,18},{18,... | collective-permute-start | bytes 196616 | tf_op jit(solution)/shard_map/ppermute | solution.py:218
  25.2 4.9 %collective-permute-start.14 = (f32[64,256]{1,0:T(8,128)S(1)}, f32[64,256]{1,0:T(8,128)S(1)}, u32[]{:S(2)}, u32[]{:S(2)}) collective-permute-start(f32[64,256]{1,0:T(8,128)S(1)} %get-tuple-element.51), channel_id=1, source_target_pairs={{0,2},{2,0},{4,6},{6,4},{8,10},{10,8},{12,14},{14,12},{16,18},{18,... | collective-permute-start | bytes 196616 | tf_op jit(solution)/shard_map/ppermute | solution.py:218
  25.3 6.2 %collective-permute-start.16 = (f32[64,256]{1,0:T(8,128)S(1)}, f32[64,256]{1,0:T(8,128)S(1)}, u32[]{:S(2)}, u32[]{:S(2)}) collective-permute-start(f32[64,256]{1,0:T(8,128)S(1)} %get-tuple-element.53), channel_id=1, source_target_pairs={{0,2},{2,0},{4,6},{6,4},{8,10},{10,8},{12,14},{14,12},{16,18},{18,... | collective-permute-start | bytes 196616 | tf_op jit(solution)/shard_map/ppermute | solution.py:218
  26.0 7.7 %collective-permute-start.13 = (f32[64,256]{1,0:T(8,128)S(1)}, f32[64,256]{1,0:T(8,128)S(1)}, u32[]{:S(2)}, u32[]{:S(2)}) collective-permute-start(f32[64,256]{1,0:T(8,128)S(1)} %add.25), channel_id=1, source_target_pairs={{0,28},{2,22},{4,24},{6,18},{8,20},{10,30},{12,16},{14,26},{16,12}... | collective-permute-start | bytes 196616 | tf_op jit(solution)/shard_map/ppermute | solution.py:220
  30.0 5.2 %collective-permute-start.11 = (f32[64,256]{1,0:T(8,128)S(1)}, f32[64,256]{1,0:T(8,128)S(1)}, u32[]{:S(2)}, u32[]{:S(2)}) collective-permute-start(f32[64,256]{1,0:T(8,128)S(1)} %add.24), channel_id=1, source_target_pairs={{0,12},{2,26},{4,8},{6,30},{8,4},{10,18},{12,0},{14,22},{16,28},{1... | collective-permute-start | bytes 196616 | tf_op jit(solution)/shard_map/ppermute | solution.py:220
  30.1 6.3 %collective-permute-start.15 = (f32[64,256]{1,0:T(8,128)S(1)}, f32[64,256]{1,0:T(8,128)S(1)}, u32[]{:S(2)}, u32[]{:S(2)}) collective-permute-start(f32[64,256]{1,0:T(8,128)S(1)} %add.27), channel_id=1, source_target_pairs={{0,16},{2,6},{4,20},{6,2},{8,24},{10,14},{12,28},{14,10},{16,0},{1... | collective-permute-start | bytes 196616 | tf_op jit(solution)/shard_map/ppermute | solution.py:220
  31.5 5.0 %collective-permute-start.17 = (f32[64,256]{1,0:T(8,128)S(1)}, f32[64,256]{1,0:T(8,128)S(1)}, u32[]{:S(2)}, u32[]{:S(2)}) collective-permute-start(f32[64,256]{1,0:T(8,128)S(1)} %add.29), channel_id=1, source_target_pairs={{0,0},{2,10},{4,4},{6,14},{8,8},{10,2},{12,12},{14,6},{16,16},{18,... | collective-permute-start | bytes 196616 | tf_op jit(solution)/shard_map/ppermute | solution.py:220
  36.5 1.3 %collective-permute-start.18 = (f32[32,256]{1,0:T(8,128)S(1)}, f32[32,256]{1,0:T(8,128)S(1)}, u32[]{:S(2)}, u32[]{:S(2)}) collective-permute-start(f32[32,256]{1,0:T(8,128)S(1)} %slice.9), channel_id=1, source_target_pairs={{0,2},{2,0},{4,6},{6,4},{8,10},{10,8},{12,14},{14,12},{16,18},{18,... | collective-permute-start | bytes 98312 | tf_op jit(solution)/shard_map/ppermute | solution.py:233

commit v4 on v3

v4 whole, which is shorter than its diff:
```python
import jax
import jax.numpy as jnp
from jax import lax
from jax.experimental import pallas as pl
from jax.experimental.pallas import tpu as pltpu
from jax.sharding import PartitionSpec as P


LANES = 128
VMEM_BYTES = 24 << 20
PAIR_COST, TURNED_COST = 1 << 35, 1 << 31


def sides_of(chips):
    sides = ([], [])
    load = [0, 0]
    for k in sorted(range(2, chips), key=lambda k: -(k // 2 + k % 2)):
        open_sides = [c for c in range(2) if len(sides[c]) < chips // 2 - 1]
        c = min(open_sides, key=lambda c: load[c])
        sides[c].append(k)
        load[c] += k // 2 + k % 2
    return sides


def own_place(sides, shard):
    place = lax.axis_index("blk")
    core, chip = lax.rem(place, 2), lax.div(place, 2)

    def rows_at(offset, owner):
        which = lax.bitwise_xor(chip, offset)
        return pl.ds(pl.multiple_of(which * (2 * shard) + owner * shard, shard), shard)

    def rows_of(step, side, owner):
        return rows_at(jnp.where(side == 0, sides[0][step], sides[1][step]), owner)

    return core, rows_at, rows_of


def dot(a, b):
    return jnp.dot(a, b, preferred_element_type=jnp.float32)


def pair_kernel(q_own, q_far, pair):
    shard = q_own.shape[0]
    pair[0:shard, :] = q_own[...]
    pair[shard:, :] = q_far[...]


def front_kernel(rows, cols, count, owners, q_own, notes, q_copy):
    notes[...] = jnp.zeros_like(notes)
    notes[0:1, 0 : rows.shape[1]] = rows[...]
    notes[1:2, 0 : cols.shape[1]] = cols[...]
    notes[2:3, 0:1] = count[...]
    notes[3:4, 0 : owners.shape[1]] = owners[...]
    q_copy[...] = q_own[...]


def each_tile(notes, tiles):
    total, size = tiles.shape[:2]
    for t in range(total):
        tile = jnp.where(t < notes[2, 0], tiles[t], jnp.zeros_like(tiles[t]))
        yield tile, *(
            pl.ds(pl.multiple_of(notes[which, t] * size, size), size) for which in (0, 1)
        )


def add_tiles(total, notes, tiles, q):
    for tile, rows, cols in each_tile(notes, tiles):
        total[rows, :] = total[rows, :] + dot(tile, q[cols, :])


def near_kernel(rounds, sides, *refs):
    block, beside, *refs = refs
    direct, relayed = refs[:rounds][::-1], refs[rounds : 2 * rounds][::-1]
    notes, tiles, y, q_far, q_near = refs[2 * rounds :]
    shard = block.shape[0] // 4
    core, rows_at, rows_of = own_place(sides, shard)

    def put(ref, rows, other):
        for part, at in enumerate((rows, other)):
            low = 2 * part * shard
            q_near[at, :] = ref[low : low + shard, :]
            q_far[at, :] = ref[low + shard : low + 2 * shard, :]

    for ref, offset in ((block, 0), (beside, 1)):
        put(ref, rows_at(offset, core), rows_at(offset, 1 - core))
    for step in range(rounds):
        for ref, side in ((direct[step], core), (relayed[step], 1 - core)):
            put(ref, rows_of(step, side, side), rows_of(step, side, 1 - side))
    y[...] = jnp.zeros_like(y)
    add_tiles(y, notes, tiles, q_near)


def turned_kernel(notes, tiles, high, low, a):
    a[...] = jnp.zeros_like(a)
    for tile, rows, cols in each_tile(notes, tiles):
        a[rows, cols] = a[rows, cols] + tile.astype(jnp.float32)
    turned = a[...].T
    high[...] = turned.astype(high.dtype)
    low[...] = (turned - high[...].astype(jnp.float32)).astype(low.dtype)


def product_kernel(rounds, sides, *refs):
    y_near, q_far, far_notes, far_tiles, high, low, y = refs[:7]
    keep, give = refs[7 : 8 + rounds], refs[8 + rounds : 9 + 2 * rounds]
    total, z = refs[9 + 2 * rounds :]
    total[...] = y_near[...]
    add_tiles(total, far_notes, far_tiles, q_far)
    y[...] = total[...].astype(y.dtype)
    z[...] = dot(high[...], y[...]) + dot(low[...], y[...])
    shard = keep[0].shape[0] // 2
    core, rows_at, rows_of = own_place(sides, shard)
    for step in range(rounds):
        for ref, side in ((keep[step], core), (give[step], 1 - core)):
            ref[0:shard, :] = z[rows_of(step, side, side), :]
            ref[shard : 2 * shard, :] = z[rows_of(step, side, 1 - side), :]
    for ref, side in ((keep[rounds], core), (give[rounds], 1 - core)):
        ref[0:shard, :] = z[rows_at(0, side), :]
        ref[shard : 2 * shard, :] = z[rows_at(1, side), :]


def owned_kernel(group, y, notes, y_out):
    size = y.shape[0] // group
    mine = group // 2
    for k in range(group):
        slot = notes[3, k]

        @pl.when(lax.div(slot, mine) == lax.axis_index("rows"))
        def _():
            at = pl.multiple_of(lax.rem(slot, mine) * size, size)
            y_out[pl.ds(at, size), :] = y[k * size : (k + 1) * size, :]


def paired(q_panel, tiles, tile_rows, tile_cols, tile_count, owner_map):
    devices = lax.axis_size("blk")
    chips = devices // 2
    rounds = chips // 2 - 1
    sides = sides_of(chips)
    shard, rank = q_panel.shape[1:]
    stack = tiles[0, 0]
    total, size = stack.shape[:2]
    group = owner_map.shape[1]
    width = devices * shard
    height = group * size
    across = [(0, 1), (1, 0)]
    sibling = [(i, i ^ 1) for i in range(devices)]
    neighbour = [(i, i ^ 2) for i in range(devices)]
    vmem = pl.BlockSpec(memory_space=pltpu.VMEM)

    def to_chips(step):
        return [
            (2 * m + c, 2 * (m ^ sides[c][step]) + c)
            for m in range(chips)
            for c in range(2)
        ]

    def call(body, name, outs, args, scratch=(), cost=0):
        return pl.pallas_call(
            body,
            out_shape=[jax.ShapeDtypeStruct(*out) for out in outs],
            in_specs=[vmem] * len(args),
            out_specs=[vmem] * len(outs),
            scratch_shapes=list(scratch),
            compiler_params=pltpu.CompilerParams(vmem_limit_bytes=VMEM_BYTES),
            cost_estimate=pl.CostEstimate(flops=cost, bytes_accessed=0, transcendentals=0)
            if cost
            else None,
            name=name,
        )(*args)

    q_own = q_panel[0]
    q_far = lax.ppermute(q_own, "rows", across)
    far_tiles = lax.ppermute(stack, "rows", across)
    notes, q_copy = call(
        front_kernel,
        "front",
        [((8, LANES), jnp.int32), (q_own.shape, q_own.dtype)],
        [
            tile_rows.reshape(1, total),
            tile_cols.reshape(1, total),
            tile_count,
            owner_map,
            q_own,
        ],
    )
    (pair,) = call(
        pair_kernel,
        "pair",
        [((2 * shard, rank), q_own.dtype)],
        [q_copy, q_far],
        cost=PAIR_COST,
    )
    block = jnp.concatenate([pair, lax.ppermute(pair, "blk", sibling)], axis=0)
    direct = [lax.ppermute(block, "blk", to_chips(step)) for step in range(rounds)]
    beside = lax.ppermute(block, "blk", neighbour)

    stack, notes, direct[0] = lax.optimization_barrier((stack, notes, direct[0]))
    turned = call(
        turned_kernel,
        "turned",
        [((width, height), stack.dtype)] * 2,
        [notes, stack],
        [pltpu.VMEM((height, width), jnp.float32)],
        cost=TURNED_COST,
    )
    direct[1], *turned = lax.optimization_barrier((direct[1], *turned))
    far_notes = lax.ppermute(notes, "rows", across)
    relayed = [lax.ppermute(one, "blk", sibling) for one in direct]

    y_near, q_other = call(
        lambda *refs: near_kernel(rounds, sides, *refs),
        "near_products",
        [((height, rank), jnp.float32), ((width, rank), q_own.dtype)],
        [block, beside, *direct[::-1], *relayed[::-1], notes, stack],
        [pltpu.VMEM((width, rank), q_own.dtype)],
        cost=1,
    )
    y, *pieces = call(
        lambda *refs: product_kernel(rounds, sides, *refs),
        "products",
        [((height, rank), jnp.bfloat16)]
        + [((2 * shard, rank), jnp.float32)] * (2 * rounds + 2),
        [y_near, q_other, far_notes, far_tiles, *turned],
        [pltpu.VMEM((height, rank), jnp.float32), pltpu.VMEM((width, rank), jnp.float32)],
    )
    keep, give = pieces[: rounds + 1], pieces[rounds + 1 :]
    given = [lax.ppermute(one, "blk", sibling) for one in give]
    arrived = [
        lax.ppermute(keep[step] + given[step], "blk", to_chips(step)) for step in range(rounds)
    ]
    last = keep[rounds] + given[rounds]
    z_beside = lax.ppermute(last[shard:], "blk", neighbour)
    y, arrived[0] = lax.optimization_barrier((y, arrived[0]))
    (y_owned,) = call(
        lambda *refs: owned_kernel(group, *refs),
        "owned",
        [((height // 2, rank), jnp.bfloat16)],
        [y, notes],
    )
    arrived[1], y_owned = lax.optimization_barrier((arrived[1], y_owned))
    summed = arrived[0]
    for step in range(1, rounds):
        summed = summed + arrived[step]
    z_sibling = lax.ppermute(summed[shard:], "blk", sibling)
    z_share = (summed[:shard] + last[:shard]) + (z_sibling + z_beside)
    return (y_owned[None], z_share[None])


def general(q_panel, tiles, tile_rows, tile_cols, tile_count, owner_map):
    panel_rows = q_panel.shape[1]
    tile_stack = tiles[0, 0]
    tile_total = tile_stack.shape[0]
    tile_size = tile_stack.shape[1]
    group_blocks = owner_map.shape[1]
    class_blocks = panel_rows * lax.axis_size("blk") // tile_size
    column_ids = tile_cols[0, 0, :, 0]
    active = jnp.arange(tile_total, dtype=jnp.int32) < tile_count[0, 0]
    slot_of_tile = owner_map[0][tile_rows[0, 0]]
    slot_hit = slot_of_tile[:, None] == jnp.arange(group_blocks, dtype=jnp.int32)[None, :]
    column_hit = column_ids[:, None] == jnp.arange(class_blocks, dtype=jnp.int32)[None, :]
    placing = (slot_hit[:, :, None] & column_hit[:, None, :] & active[:, None, None]).astype(
        tile_stack.dtype
    )
    local_matrix = jnp.einsum(
        "tsc,tik->sick", placing, tile_stack, preferred_element_type=jnp.float32
    )
    local_matrix = local_matrix.reshape(group_blocks * tile_size, class_blocks * tile_size)
    rows_in = lax.all_gather(q_panel, "blk", axis=1, tiled=True)[0]
    flat_partial = jnp.dot(
        local_matrix, rows_in.astype(jnp.float32), precision=lax.Precision.HIGHEST
    )
    owned = lax.psum_scatter(flat_partial, "rows", scatter_dimension=0, tiled=True)
    y_owned = owned.astype(jnp.bfloat16)
    y_group = lax.all_gather(y_owned, "rows", axis=0, tiled=True)
    column_term = lax.dot_general(
        local_matrix,
        y_group.astype(jnp.float32),
        (((0,), (0,)), ((), ())),
        precision=lax.Precision.HIGHEST,
    )
    z_share = lax.psum_scatter(column_term, "blk", scatter_dimension=0, tiled=True)
    return (y_owned[None], z_share[None])


def solution(mesh):
    placed = (
        P("rows", "blk", None),
        P("blk", "rows", None, None, None),
        P("blk", "rows", None),
        P("blk", "rows", None, None),
        P("blk", "rows"),
        P("blk", None),
    )
    devices = mesh.shape["blk"]
    fits = mesh.shape["rows"] == 2 and devices >= 8 and devices & (devices - 1) == 0
    return jax.shard_map(
        paired if fits else general,
        mesh=mesh,
        in_specs=placed,
        out_specs=(P("blk", "rows", None), P("rows", "blk", None)),
        check_vma=False,
    )
```

time: 38.7 us -> 36.6 us (0.946)
  waiting for transfers between devices: 12.2 us -> 9.15 us
  starting transfers between devices: 18.6 us -> 20.2 us
  local copies, waits for them, and re-layouts: 2.49 us -> 1.39 us
  Pallas kernels: 3.01 us -> 3.52 us
    ppermute x3 -> x7, starting transfers between devices: 2.47 us -> 7.44 us  [the longest x1 3 us: paired(): q_far = lax.ppermute(q_own, 'rows', across)]
    ppermute x3 -> x7, waiting for transfers between devices: 7.57 us -> 3.83 us  [the longest x1 1.44 us: paired(): far_notes = lax.ppermute(notes, 'rows', across)]
    ppermute x4 -> x3, waiting for transfers between devices: 0.03 us -> 2.94 us  [paired(): lax.ppermute(block, 'blk', to_chips(step))]
    ppermute x4 -> x3, starting transfers between devices: 7.11 us -> 5.65 us  [paired(): lax.ppermute(block, 'blk', to_chips(step))]
    ppermute x4 -> x3, starting transfers between devices: 1.79 us -> 0.51 us  [paired(): relayed = [lax.ppermute(one, 'blk', sibling) for one in direct]]
    ppermute x4 -> x3, waiting for transfers between devices: 3.28 us -> 2.14 us  [paired(): lax.ppermute(keep[step] + given[step], 'blk', to_chips(step))]
    ppermute x4 -> x3, waiting for transfers between devices: 1.12 us -> 0.01 us  [paired(): relayed = [lax.ppermute(one, 'blk', sibling) for one in direct]]
    unnamed x10, local copies, waits for them, and re-layouts: 2.49 us -> 1.39 us
  transfers between devices with their start and end apart: 19 -> 20, of which waited for: 10 -> 8; matrix products, arithmetic and copies ran while one was open for 0% -> 0% of each run, Pallas kernels for 5% -> 7%
where the time goes in v4:
time: 36.6 us; the launch traced here: 36.4 us
  starting transfers between devices  20.2 us (55%)
  waiting for transfers between devices  9.15 us (25%)
  Pallas kernels  3.52 us (10%)
  between operations  1.43 us (4%)
  local copies, waits for them, and re-layouts  1.39 us (4%)
  other arithmetic  0.68 us (2%)
    ppermute x3, starting transfers between devices, paired(): lax.ppermute(block, 'blk', to_chips(step))  5.65 us
    ppermute x3, starting transfers between devices, paired(): lax.ppermute(keep[step] + given[step], 'blk', to_chips(step))  5.48 us
    pallas_call x6, Pallas kernels, call(): pl.pallas_call(body, out_shape=[jax.ShapeDtypeStruct(*out) for out in out...  3.52 us
    ppermute x1, starting transfers between devices, paired(): q_far = lax.ppermute(q_own, 'rows', across)  3 us
    ppermute x3, waiting for transfers between devices, paired(): lax.ppermute(block, 'blk', to_chips(step))  2.94 us
    ppermute x3, waiting for transfers between devices, paired(): lax.ppermute(keep[step] + given[step], 'blk', to_chips(step))  2.14 us
    ppermute x1, starting transfers between devices, paired(): beside = lax.ppermute(block, 'blk', neighbour)  1.61 us
    ppermute x1, starting transfers between devices, paired(): far_notes = lax.ppermute(notes, 'rows', across)  1.49 us
  transfers between devices with their start and end apart: 20, of which 8 were waited for; matrix products, arithmetic and copies ran while one was open for 0% of the time, Pallas kernels for 7%

profile of v4, /device:TPU:0, one launch (start us, length us, event | category | flops | bytes accessed | tf_op | source)
XLA Modules:
  0.0 36.4 jit_solution(4295877782194819893)
XLA Ops:
  0.6 3.0 %collective-permute-start = (bf16[32,256]{1,0:T(8,128)(2,1)}, bf16[32,256]{1,0:T(8,128)(2,1)S(1)}, u32[]{:S(2)}, u32[]{:S(2)}) collective-permute-start(bf16[32,256]{1,0:T(8,128)(2,1)} %bitcast.10), channel_id=1, source_target_pairs={{0,1},{1,0},{2,3},{3,2},{4,5},{5,4},{6,7},{7,6},{8,9},{9,8},{10,11... | collective-permute-start | bytes 49160 | tf_op jit(solution)/shard_map/ppermute | solution.py:172
  3.6 0.1 collective-permute-start.10
  4.4 0.6 %copy-done.2 = s32[1,1,20]{2,1,0:T(1,128)S(1)} copy-done((s32[1,1,20]{2,1,0:T(1,128)S(1)}, s32[1,1,20]{2,1,0:T(1,128)}, u32[]{:S(2)}) %copy-start.2) | copy-done | bytes 104
  5.0 0.0 copy-done.3
  5.0 0.0 copy-done.4
  5.1 0.7 %copy-done.1 = bf16[1,32,256]{2,1,0:T(8,128)(2,1)S(1)} copy-done((bf16[1,32,256]{2,1,0:T(8,128)(2,1)S(1)}, bf16[1,32,256]{2,1,0:T(8,128)(2,1)}, u32[]{:S(2)}) %copy-start.1) | copy-done | bytes 16408
  5.8 0.0 collective-permute-done.q_far
  5.8 0.0 copy-start
  5.8 0.1 collective-permute-start.1
  5.9 1.2 %collective-permute-done.1 = bf16[64,256]{1,0:T(8,128)(2,1)S(1)} collective-permute-done((bf16[64,256]{1,0:T(8,128)(2,1)S(1)}, bf16[64,256]{1,0:T(8,128)(2,1)S(1)}, u32[]{:S(2)}, u32[]{:S(2)}) %collective-permute-start.1) | collective-permute-done | bytes 32800 | tf_op jit(solution)/shard_map/ppermute | solution.py:193
  7.1 5.0 %collective-permute-start.5 = (bf16[128,256]{1,0:T(8,128)(2,1)S(1)}, bf16[128,256]{1,0:T(8,128)(2,1)S(1)}, u32[]{:S(2)}, u32[]{:S(2)}) collective-permute-start(bf16[128,256]{1,0:T(8,128)(2,1)S(1)} %pad_maximum_fusion.refs_0_), channel_id=1, source_target_pairs={{0,28},{2,22},{4,24},{6,18},{8,20},{10,30},{12,16},{14,26},{16,12}... | collective-permute-start | bytes 196616 | tf_op jit(solution)/shard_map/ppermute | solution.py:194
  12.1 0.0 collective-permute-start.4
  12.1 0.6 %collective-permute-start.3 = (bf16[128,256]{1,0:T(8,128)(2,1)S(1)}, bf16[128,256]{1,0:T(8,128)(2,1)S(1)}, u32[]{:S(2)}, u32[]{:S(2)}) collective-permute-start(bf16[128,256]{1,0:T(8,128)(2,1)S(1)} %pad_maximum_fusion.refs_0_), channel_id=1, source_target_pairs={{0,16},{2,10},{4,20},{6,14},{8,24},{10,2},{12,28},{14,6},{16,0},{1... | collective-permute-start | bytes 196616 | tf_op jit(solution)/shard_map/ppermute | solution.py:194
  12.7 1.6 %collective-permute-start.2 = (bf16[128,256]{1,0:T(8,128)(2,1)S(1)}, bf16[128,256]{1,0:T(8,128)(2,1)S(1)}, u32[]{:S(2)}, u32[]{:S(2)}) collective-permute-start(bf16[128,256]{1,0:T(8,128)(2,1)S(1)} %pad_maximum_fusion.refs_0_), channel_id=1, source_target_pairs={{0,4},{2,6},{4,0},{6,2},{8,12},{10,14},{12,8},{14,10},{16,20},{18,... | collective-permute-start | bytes 196616 | tf_op jit(solution)/shard_map/ppermute | solution.py:195
  14.4 0.3 collective-permute-done.5.refs_4_
  14.6 0.0 collective-permute-start.8
  14.6 0.7 %turned.1 = (bf16[512,512]{1,0:T(8,128)(2,1)S(1)}, bf16[512,512]{1,0:T(8,128)(2,1)S(1)}) custom-call(s32[8,128]{1,0:T(8,128)S(1)} %get-tuple-element.29.notes.refs_8_.refs_1_, bf16[20,128,128]{2,1,0:T(8,128)(2,1)S(1)} %bitcast.8), custom_call_target="tpu_custom_call" | custom-call | flops 2147483648 | tf_op jit(solution)/shard_map/turned/pallas_call | solution.py:158
  15.3 2.7 %collective-permute-done.4.refs_3_ = bf16[128,256]{1,0:T(8,128)(2,1)S(1)} collective-permute-done((bf16[128,256]{1,0:T(8,128)(2,1)S(1)}, bf16[128,256]{1,0:T(8,128)(2,1)S(1)}, u32[]{:S(2)}, u32[]{:S(2)}) %collective-permute-start.4) | collective-permute-done | bytes 65568 | tf_op jit(solution)/shard_map/ppermute | solution.py:194
  18.0 0.0 collective-permute-done.3.refs_2_
  18.0 0.0 collective-permute-start.6
  18.0 0.5 %collective-permute-start.7 = (bf16[128,256]{1,0:T(8,128)(2,1)S(1)}, bf16[128,256]{1,0:T(8,128)(2,1)S(1)}, u32[]{:S(2)}, u32[]{:S(2)}) collective-permute-start(bf16[128,256]{1,0:T(8,128)(2,1)S(1)} %collective-permute-done.4.refs_3_), channel_id=1, source_target_pairs={{0,2},{2,0},{4,6},{6,4},{8,10},{10,8},{12,14},{14,12},{16,18},{18,... | collective-permute-start | bytes 196616 | tf_op jit(solution)/shard_map/ppermute | solution.py:208
  18.5 0.0 collective-permute-done.2.refs_1_
  18.5 1.5 %collective-permute-start.9 = (s32[8,128]{1,0:T(8,128)S(1)}, s32[8,128]{1,0:T(8,128)S(1)}, u32[]{:S(2)}, u32[]{:S(2)}) collective-permute-start(s32[8,128]{1,0:T(8,128)S(1)} %get-tuple-element.29.notes.refs_8_.refs_1_), channel_id=1, source_target_pairs={{0,1},{1,0},{2,3},{3,2},{4,5},{5,4},{6,7},{7,6},{8,9},{9,8},{10,11... | collective-permute-start | bytes 12296 | tf_op jit(solution)/shard_map/ppermute | solution.py:207
  20.0 0.0 collective-permute-done.8.refs_7_
  20.0 0.0 collective-permute-done.6.refs_5_
  20.0 0.0 collective-permute-done.7.refs_6_
  20.0 0.7 %near_products.1 = (f32[512,256]{1,0:T(8,128)S(1)}, bf16[512,256]{1,0:T(8,128)(2,1)S(1)}) custom-call(bf16[128,256]{1,0:T(8,128)(2,1)S(1)} %pad_maximum_fusion.refs_0_, bf16[128,256]{1,0:T(8,128)(2,1)S(1)} %collective-permute-done.2.refs_1_, bf16[128,256]{1,0:T(8,128)(2,1)S(1)} %collective-permute-done.3.refs_2_, ...), custom_call_target="tpu_custom_call" | custom-call | flops 1 | tf_op jit(solution)/shard_map/near_products/pallas_call | solution.py:158
  20.7 1.4 %collective-permute-done.9.refs_2_ = s32[8,128]{1,0:T(8,128)S(1)} collective-permute-done((s32[8,128]{1,0:T(8,128)S(1)}, s32[8,128]{1,0:T(8,128)S(1)}, u32[]{:S(2)}, u32[]{:S(2)}) %collective-permute-start.9) | collective-permute-done | bytes 4128 | tf_op jit(solution)/shard_map/ppermute | solution.py:207
  22.1 0.0 collective-permute-done.10.refs_3_
  22.1 1.1 %products.1 = (bf16[512,256]{1,0:T(8,128)(2,1)S(1)}, f32[64,256]{1,0:T(8,128)S(1)}, f32[64,256]{1,0:T(8,128)S(1)}, f32[64,256]{1,0:T(8,128)S(1)}, f32[64,256]{1,...) custom-call(f32[512,256]{1,0:T(8,128)S(1)} %get-tuple-element.35.ref, ...), custom_call_target="tpu_custom_call" | custom-call | tf_op jit(solution)/shard_map/products/pallas_call | solution.py:158
  23.3 0.1 collective-permute-start.13
  23.3 0.5 %collective-permute-start.11 = (f32[64,256]{1,0:T(8,128)S(1)}, f32[64,256]{1,0:T(8,128)S(1)}, u32[]{:S(2)}, u32[]{:S(2)}) collective-permute-start(f32[64,256]{1,0:T(8,128)S(1)} %get-tuple-element.40), channel_id=1, source_target_pairs={{0,2},{2,0},{4,6},{6,4},{8,10},{10,8},{12,14},{14,12},{16,18},{18,... | collective-permute-start | bytes 196616 | tf_op jit(solution)/shard_map/ppermute | solution.py:227
  23.8 0.1 collective-permute-start.15
  23.9 0.4 %collective-permute-start.17 = (f32[64,256]{1,0:T(8,128)S(1)}, f32[64,256]{1,0:T(8,128)S(1)}, u32[]{:S(2)}, u32[]{:S(2)}) collective-permute-start(f32[64,256]{1,0:T(8,128)S(1)} %get-tuple-element.51), channel_id=1, source_target_pairs={{0,2},{2,0},{4,6},{6,4},{8,10},{10,8},{12,14},{14,12},{16,18},{18,... | collective-permute-start | bytes 196616 | tf_op jit(solution)/shard_map/ppermute | solution.py:227
  24.3 0.2 collective-permute-done.13
  24.6 3.2 %collective-permute-start.14 = (f32[64,256]{1,0:T(8,128)S(1)}, f32[64,256]{1,0:T(8,128)S(1)}, u32[]{:S(2)}, u32[]{:S(2)}) collective-permute-start(f32[64,256]{1,0:T(8,128)S(1)} %add.28), channel_id=1, source_target_pairs={{0,28},{2,22},{4,24},{6,18},{8,20},{10,30},{12,16},{14,26},{16,12}... | collective-permute-start | bytes 196616 | tf_op jit(solution)/shard_map/ppermute | solution.py:229
  27.8 0.0 collective-permute-done.11
  27.8 0.3 collective-permute-start.12
  28.1 0.0 collective-permute-done.15
  28.1 2.0 %collective-permute-start.16 = (f32[64,256]{1,0:T(8,128)S(1)}, f32[64,256]{1,0:T(8,128)S(1)}, u32[]{:S(2)}, u32[]{:S(2)}) collective-permute-start(f32[64,256]{1,0:T(8,128)S(1)} %add.30), channel_id=1, source_target_pairs={{0,16},{2,10},{4,20},{6,14},{8,24},{10,2},{12,28},{14,6},{16,0},{1... | collective-permute-start | bytes 196616 | tf_op jit(solution)/shard_map/ppermute | solution.py:229
  30.1 0.0 collective-permute-done.17
  30.1 1.1 %collective-permute-start.19 = (f32[32,256]{1,0:T(8,128)S(1)}, f32[32,256]{1,0:T(8,128)S(1)}, u32[]{:S(2)}, u32[]{:S(2)}) collective-permute-start(f32[32,256]{1,0:T(8,128)S(1)} %slice.19), channel_id=1, source_target_pairs={{0,4},{2,6},{4,0},{6,2},{8,12},{10,14},{12,8},{14,10},{16,20},{18,... | collective-permute-start | bytes 98312 | tf_op jit(solution)/shard_map/ppermute | solution.py:232
  31.2 0.4 %collective-permute-done.14 = f32[64,256]{1,0:T(8,128)S(1)} collective-permute-done((f32[64,256]{1,0:T(8,128)S(1)}, f32[64,256]{1,0:T(8,128)S(1)}, u32[]{:S(2)}, u32[]{:S(2)}) %collective-permute-start.14) | collective-permute-done | bytes 65568 | tf_op jit(solution)/shard_map/ppermute | solution.py:229
  31.6 1.0 %owned.1 = bf16[256,256]{1,0:T(8,128)(2,1)} custom-call(bf16[512,256]{1,0:T(8,128)(2,1)S(1)} %get-tuple-element.44.refs_0_, s32[8,128]{1,0:T(8,128)S(1)} %get-tuple-element.29.notes.refs_8_.refs_1_), custom_call_target="tpu_custom_call" | custom-call | tf_op jit(solution)/shard_map/owned/pallas_call | solution.py:158
  32.7 1.8 %collective-permute-done.12 = f32[64,256]{1,0:T(8,128)S(1)} collective-permute-done((f32[64,256]{1,0:T(8,128)S(1)}, f32[64,256]{1,0:T(8,128)S(1)}, u32[]{:S(2)}, u32[]{:S(2)}) %collective-permute-start.12) | collective-permute-done | bytes 65568 | tf_op jit(solution)/shard_map/ppermute | solution.py:229
  34.5 0.1 collective-permute-start.18
  34.5 1.2 %collective-permute-done.18 = f32[32,256]{1,0:T(8,128)S(1)} collective-permute-done((f32[32,256]{1,0:T(8,128)S(1)}, f32[32,256]{1,0:T(8,128)S(1)}, u32[]{:S(2)}, u32[]{:S(2)}) %collective-permute-start.18) | collective-permute-done | bytes 32800 | tf_op jit(solution)/shard_map/ppermute | solution.py:244
  35.7 0.6 %fusion.1 = f32[1,32,256]{2,1,0:T(8,128)} fusion(f32[64,256]{1,0:T(8,128)S(1)} %add.32, f32[64,256]{1,0:T(8,128)S(1)} %add_add_fusion, f32[32,256]{1,0:T(8,128)S(1)} %collective-permute-done.18, f32[32,256]{1,0:T(8,128)S(1)} %collective-permute-done.19), kind=kLoop, calls=%fused_computation.4 | loop fusion | flops 24576 | bytes 163840 | tf_op jit(solution)/shard_map/broadcast_in_dim | solution.py:246
  (17 shorter events, 0.1 us)
Async XLA Ops:
  0.6 5.2 %collective-permute-start = (bf16[32,256]{1,0:T(8,128)(2,1)}, bf16[32,256]{1,0:T(8,128)(2,1)S(1)}, u32[]{:S(2)}, u32[]{:S(2)}) collective-permute-start(bf16[32,256]{1,0:T(8,128)(2,1)} %bitcast.10), channel_id=1, source_target_pairs={{0,1},{1,0},{2,3},{3,2},{4,5},{5,4},{6,7},{7,6},{8,9},{9,8},{10,11... | collective-permute-start | bytes 49160 | tf_op jit(solution)/shard_map/ppermute | solution.py:172
  3.6 18.5 %collective-permute-start.10 = (bf16[20,128,128]{2,1,0:T(8,128)(2,1)}, bf16[20,128,128]{2,1,0:T(8,128)(2,1)S(1)}, u32[]{:S(2)}, u32[]{:S(2)}) collective-permute-start(bf16[20,128,128]{2,1,0:T(8,128)(2,1)} %bitcast.7), channel_id=1, source_target_pairs={{0,1},{1,0},{2,3},{3,2},{4,5},{5,4},{6,7},{7,6},{8,9},{9,8},{10,11... | collective-permute-start | bytes 1966088 | tf_op jit(solution)/shard_map/ppermute | solution.py:173
  4.4 0.7 %copy-start.2 = (s32[1,1,20]{2,1,0:T(1,128)S(1)}, s32[1,1,20]{2,1,0:T(1,128)}, u32[]{:S(2)}) copy-start(s32[1,1,20]{2,1,0:T(1,128)} %param.8) | copy-start | bytes 244
  4.4 0.7 %copy-start.3 = (s32[1,1,20,1]{2,3,1,0:T(1,128)S(1)}, s32[1,1,20,1]{2,3,1,0:T(1,128)}, u32[]{:S(2)}) copy-start(s32[1,1,20,1]{2,3,1,0:T(1,128)} %param.9) | copy-start | bytes 244
  4.4 0.7 %copy-start.4 = (s32[1,4]{1,0:T(1,128)S(1)}, s32[1,4]{1,0:T(1,128)}, u32[]{:S(2)}) copy-start(s32[1,4]{1,0:T(1,128)} %owners.1) | copy-start | bytes 52
  5.1 0.7 %copy-start.1 = (bf16[1,32,256]{2,1,0:T(8,128)(2,1)S(1)}, bf16[1,32,256]{2,1,0:T(8,128)(2,1)}, u32[]{:S(2)}) copy-start(bf16[1,32,256]{2,1,0:T(8,128)(2,1)} %param.6) | copy-start | bytes 49156
  5.8 8.8 %copy-start = (bf16[1,1,20,128,128]{4,3,2,1,0:T(8,128)(2,1)S(1)}, bf16[1,1,20,128,128]{4,3,2,1,0:T(8,128)(2,1)}, u32[]{:S(2)}) copy-start(bf16[1,1,20,128,128]{4,3,2,1,0:T(8,128)(2,1)} %param.7) | copy-start | bytes 1966084
  5.8 1.3 %collective-permute-start.1 = (bf16[64,256]{1,0:T(8,128)(2,1)S(1)}, bf16[64,256]{1,0:T(8,128)(2,1)S(1)}, u32[]{:S(2)}, u32[]{:S(2)}) collective-permute-start(bf16[64,256]{1,0:T(8,128)(2,1)S(1)} %pair.1), channel_id=1, source_target_pairs={{0,2},{2,0},{4,6},{6,4},{8,10},{10,8},{12,14},{14,12},{16,18},{18,... | collective-permute-start | bytes 98312 | tf_op jit(solution)/shard_map/ppermute | solution.py:193
  7.1 7.5 %collective-permute-start.5 = (bf16[128,256]{1,0:T(8,128)(2,1)S(1)}, bf16[128,256]{1,0:T(8,128)(2,1)S(1)}, u32[]{:S(2)}, u32[]{:S(2)}) collective-permute-start(bf16[128,256]{1,0:T(8,128)(2,1)S(1)} %pad_maximum_fusion.refs_0_), channel_id=1, source_target_pairs={{0,28},{2,22},{4,24},{6,18},{8,20},{10,30},{12,16},{14,26},{16,12}... | collective-permute-start | bytes 196616 | tf_op jit(solution)/shard_map/ppermute | solution.py:194
  12.1 5.9 %collective-permute-start.4 = (bf16[128,256]{1,0:T(8,128)(2,1)S(1)}, bf16[128,256]{1,0:T(8,128)(2,1)S(1)}, u32[]{:S(2)}, u32[]{:S(2)}) collective-permute-start(bf16[128,256]{1,0:T(8,128)(2,1)S(1)} %pad_maximum_fusion.refs_0_), channel_id=1, source_target_pairs={{0,12},{2,26},{4,8},{6,30},{8,4},{10,18},{12,0},{14,22},{16,28},{1... | collective-permute-start | bytes 196616 | tf_op jit(solution)/shard_map/ppermute | solution.py:194
  12.1 5.9 %collective-permute-start.3 = (bf16[128,256]{1,0:T(8,128)(2,1)S(1)}, bf16[128,256]{1,0:T(8,128)(2,1)S(1)}, u32[]{:S(2)}, u32[]{:S(2)}) collective-permute-start(bf16[128,256]{1,0:T(8,128)(2,1)S(1)} %pad_maximum_fusion.refs_0_), channel_id=1, source_target_pairs={{0,16},{2,10},{4,20},{6,14},{8,24},{10,2},{12,28},{14,6},{16,0},{1... | collective-permute-start | bytes 196616 | tf_op jit(solution)/shard_map/ppermute | solution.py:194
  12.7 5.8 %collective-permute-start.2 = (bf16[128,256]{1,0:T(8,128)(2,1)S(1)}, bf16[128,256]{1,0:T(8,128)(2,1)S(1)}, u32[]{:S(2)}, u32[]{:S(2)}) collective-permute-start(bf16[128,256]{1,0:T(8,128)(2,1)S(1)} %pad_maximum_fusion.refs_0_), channel_id=1, source_target_pairs={{0,4},{2,6},{4,0},{6,2},{8,12},{10,14},{12,8},{14,10},{16,20},{18,... | collective-permute-start | bytes 196616 | tf_op jit(solution)/shard_map/ppermute | solution.py:195
  14.6 5.4 %collective-permute-start.8 = (bf16[128,256]{1,0:T(8,128)(2,1)S(1)}, bf16[128,256]{1,0:T(8,128)(2,1)S(1)}, u32[]{:S(2)}, u32[]{:S(2)}) collective-permute-start(bf16[128,256]{1,0:T(8,128)(2,1)S(1)} %collective-permute-done.5.refs_4_), channel_id=1, source_target_pairs={{0,2},{2,0},{4,6},{6,4},{8,10},{10,8},{12,14},{14,12},{16,18},{18,... | collective-permute-start | bytes 196616 | tf_op jit(solution)/shard_map/ppermute | solution.py:208
  18.0 2.0 %collective-permute-start.6 = (bf16[128,256]{1,0:T(8,128)(2,1)S(1)}, bf16[128,256]{1,0:T(8,128)(2,1)S(1)}, u32[]{:S(2)}, u32[]{:S(2)}) collective-permute-start(bf16[128,256]{1,0:T(8,128)(2,1)S(1)} %collective-permute-done.3.refs_2_), channel_id=1, source_target_pairs={{0,2},{2,0},{4,6},{6,4},{8,10},{10,8},{12,14},{14,12},{16,18},{18,... | collective-permute-start | bytes 196616 | tf_op jit(solution)/shard_map/ppermute | solution.py:208
  18.0 2.0 %collective-permute-start.7 = (bf16[128,256]{1,0:T(8,128)(2,1)S(1)}, bf16[128,256]{1,0:T(8,128)(2,1)S(1)}, u32[]{:S(2)}, u32[]{:S(2)}) collective-permute-start(bf16[128,256]{1,0:T(8,128)(2,1)S(1)} %collective-permute-done.4.refs_3_), channel_id=1, source_target_pairs={{0,2},{2,0},{4,6},{6,4},{8,10},{10,8},{12,14},{14,12},{16,18},{18,... | collective-permute-start | bytes 196616 | tf_op jit(solution)/shard_map/ppermute | solution.py:208
  18.5 3.6 %collective-permute-start.9 = (s32[8,128]{1,0:T(8,128)S(1)}, s32[8,128]{1,0:T(8,128)S(1)}, u32[]{:S(2)}, u32[]{:S(2)}) collective-permute-start(s32[8,128]{1,0:T(8,128)S(1)} %get-tuple-element.29.notes.refs_8_.refs_1_), channel_id=1, source_target_pairs={{0,1},{1,0},{2,3},{3,2},{4,5},{5,4},{6,7},{7,6},{8,9},{9,8},{10,11... | collective-permute-start | bytes 12296 | tf_op jit(solution)/shard_map/ppermute | solution.py:207
  23.3 1.3 %collective-permute-start.13 = (f32[64,256]{1,0:T(8,128)S(1)}, f32[64,256]{1,0:T(8,128)S(1)}, u32[]{:S(2)}, u32[]{:S(2)}) collective-permute-start(f32[64,256]{1,0:T(8,128)S(1)} %get-tuple-element.43), channel_id=1, source_target_pairs={{0,2},{2,0},{4,6},{6,4},{8,10},{10,8},{12,14},{14,12},{16,18},{18,... | collective-permute-start | bytes 196616 | tf_op jit(solution)/shard_map/ppermute | solution.py:227
  23.3 4.5 %collective-permute-start.11 = (f32[64,256]{1,0:T(8,128)S(1)}, f32[64,256]{1,0:T(8,128)S(1)}, u32[]{:S(2)}, u32[]{:S(2)}) collective-permute-start(f32[64,256]{1,0:T(8,128)S(1)} %get-tuple-element.40), channel_id=1, source_target_pairs={{0,2},{2,0},{4,6},{6,4},{8,10},{10,8},{12,14},{14,12},{16,18},{18,... | collective-permute-start | bytes 196616 | tf_op jit(solution)/shard_map/ppermute | solution.py:227
  23.8 4.3 %collective-permute-start.15 = (f32[64,256]{1,0:T(8,128)S(1)}, f32[64,256]{1,0:T(8,128)S(1)}, u32[]{:S(2)}, u32[]{:S(2)}) collective-permute-start(f32[64,256]{1,0:T(8,128)S(1)} %get-tuple-element.49), channel_id=1, source_target_pairs={{0,2},{2,0},{4,6},{6,4},{8,10},{10,8},{12,14},{14,12},{16,18},{18,... | collective-permute-start | bytes 196616 | tf_op jit(solution)/shard_map/ppermute | solution.py:227
  23.9 6.2 %collective-permute-start.17 = (f32[64,256]{1,0:T(8,128)S(1)}, f32[64,256]{1,0:T(8,128)S(1)}, u32[]{:S(2)}, u32[]{:S(2)}) collective-permute-start(f32[64,256]{1,0:T(8,128)S(1)} %get-tuple-element.51), channel_id=1, source_target_pairs={{0,2},{2,0},{4,6},{6,4},{8,10},{10,8},{12,14},{14,12},{16,18},{18,... | collective-permute-start | bytes 196616 | tf_op jit(solution)/shard_map/ppermute | solution.py:227
  24.6 7.0 %collective-permute-start.14 = (f32[64,256]{1,0:T(8,128)S(1)}, f32[64,256]{1,0:T(8,128)S(1)}, u32[]{:S(2)}, u32[]{:S(2)}) collective-permute-start(f32[64,256]{1,0:T(8,128)S(1)} %add.28), channel_id=1, source_target_pairs={{0,28},{2,22},{4,24},{6,18},{8,20},{10,30},{12,16},{14,26},{16,12}... | collective-permute-start | bytes 196616 | tf_op jit(solution)/shard_map/ppermute | solution.py:229
  27.8 6.6 %collective-permute-start.12 = (f32[64,256]{1,0:T(8,128)S(1)}, f32[64,256]{1,0:T(8,128)S(1)}, u32[]{:S(2)}, u32[]{:S(2)}) collective-permute-start(f32[64,256]{1,0:T(8,128)S(1)} %add.27), channel_id=1, source_target_pairs={{0,12},{2,26},{4,8},{6,30},{8,4},{10,18},{12,0},{14,22},{16,28},{1... | collective-permute-start | bytes 196616 | tf_op jit(solution)/shard_map/ppermute | solution.py:229
  28.1 6.3 %collective-permute-start.16 = (f32[64,256]{1,0:T(8,128)S(1)}, f32[64,256]{1,0:T(8,128)S(1)}, u32[]{:S(2)}, u32[]{:S(2)}) collective-permute-start(f32[64,256]{1,0:T(8,128)S(1)} %add.30), channel_id=1, source_target_pairs={{0,16},{2,10},{4,20},{6,14},{8,24},{10,2},{12,28},{14,6},{16,0},{1... | collective-permute-start | bytes 196616 | tf_op jit(solution)/shard_map/ppermute | solution.py:229
  30.1 4.4 %collective-permute-start.19 = (f32[32,256]{1,0:T(8,128)S(1)}, f32[32,256]{1,0:T(8,128)S(1)}, u32[]{:S(2)}, u32[]{:S(2)}) collective-permute-start(f32[32,256]{1,0:T(8,128)S(1)} %slice.19), channel_id=1, source_target_pairs={{0,4},{2,6},{4,0},{6,2},{8,12},{10,14},{12,8},{14,10},{16,20},{18,... | collective-permute-start | bytes 98312 | tf_op jit(solution)/shard_map/ppermute | solution.py:232
  34.5 1.3 %collective-permute-start.18 = (f32[32,256]{1,0:T(8,128)S(1)}, f32[32,256]{1,0:T(8,128)S(1)}, u32[]{:S(2)}, u32[]{:S(2)}) collective-permute-start(f32[32,256]{1,0:T(8,128)S(1)} %slice.18), channel_id=1, source_target_pairs={{0,2},{2,0},{4,6},{6,4},{8,10},{10,8},{12,14},{14,12},{16,18},{18,... | collective-permute-start | bytes 98312 | tf_op jit(solution)/shard_map/ppermute | solution.py:244

commit v5 on v4

--- a/solution.py
+++ b/solution.py
@@ -7,19 +7,15 @@
 
 
 LANES = 128
+SCALE_ROWS = 16
 VMEM_BYTES = 24 << 20
 PAIR_COST, TURNED_COST = 1 << 35, 1 << 31
 
 
 def sides_of(chips):
-    sides = ([], [])
-    load = [0, 0]
-    for k in sorted(range(2, chips), key=lambda k: -(k // 2 + k % 2)):
-        open_sides = [c for c in range(2) if len(sides[c]) < chips // 2 - 1]
-        c = min(open_sides, key=lambda c: load[c])
-        sides[c].append(k)
-        load[c] += k // 2 + k % 2
-    return sides
+    return tuple(
+        [k for k in reversed(range(2, chips)) if k.bit_count() % 2 == odd] for odd in (1, 0)
+    )
 
 
 def own_place(sides, shard):
@@ -62,6 +58,29 @@
         yield tile, *(
             pl.ds(pl.multiple_of(notes[which, t] * size, size), size) for which in (0, 1)
         )
+
+
+def coded_kernel(ours, given, sent):
+    rows = ours.shape[0]
+    x = ours[...] + given[...]
+    top = jnp.max(jnp.abs(x), axis=0, keepdims=True)
+    power = jnp.ceil(jnp.log2(jnp.maximum(top, 1e-30)))
+    whole = jnp.clip(jnp.round(x * jnp.exp2(15.0 - power)), -32767.0, 32767.0)
+    sent[0:rows, :] = whole.astype(jnp.int32).astype(jnp.int16)
+    power = jnp.broadcast_to(power, (SCALE_ROWS, x.shape[1]))
+    sent[rows:, :] = power.astype(jnp.int32).astype(jnp.int16)
+
+
+def gather_kernel(*refs):
+    *arrived, last, mine, theirs = refs
+    shard = mine.shape[0]
+    total = jnp.concatenate([last[0:shard, :], jnp.zeros_like(mine)], axis=0)
+    for ref in arrived:
+        x = ref[0 : 2 * shard, :].astype(jnp.int32).astype(jnp.float32)
+        power = ref[2 * shard :, :].astype(jnp.int32).astype(jnp.float32)
+        total = total + x * jnp.exp2(power[0:1, :] - 15.0)
+    mine[...] = total[0:shard, :]
+    theirs[...] = total[shard:, :]
 
 
 def add_tiles(total, notes, tiles, q):
@@ -225,9 +244,15 @@
     )
     keep, give = pieces[: rounds + 1], pieces[rounds + 1 :]
     given = [lax.ppermute(one, "blk", sibling) for one in give]
-    arrived = [
-        lax.ppermute(keep[step] + given[step], "blk", to_chips(step)) for step in range(rounds)
-    ]
+    arrived = []
+    for step in range(rounds):
+        (sent,) = call(
+            coded_kernel,
+            "coded",
+            [((2 * shard + SCALE_ROWS, rank), jnp.int16)],
+            [keep[step], given[step]],
+        )
+        arrived.append(lax.ppermute(sent, "blk", to_chips(step)))
     last = keep[rounds] + given[rounds]
     z_beside = lax.ppermute(last[shard:], "blk", neighbour)
     y, arrived[0] = lax.optimization_barrier((y, arrived[0]))
@@ -238,11 +263,13 @@
         [y, notes],
     )
     arrived[1], y_owned = lax.optimization_barrier((arrived[1], y_owned))
-    summed = arrived[0]
-    for step in range(1, rounds):
-        summed = summed + arrived[step]
-    z_sibling = lax.ppermute(summed[shard:], "blk", sibling)
-    z_share = (summed[:shard] + last[:shard]) + (z_sibling + z_beside)
+    z_mine, z_theirs = call(
+        gather_kernel,
+        "gathered",
+        [((shard, rank), jnp.float32)] * 2,
+        [*arrived, last],
+    )
+    z_share = z_mine + (lax.ppermute(z_theirs, "blk", sibling) + z_beside)
     return (y_owned[None], z_share[None])
 
 

time: 36.6 us -> 34.8 us (0.951)
  starting transfers between devices: 20.2 us -> 18.6 us
  waiting for transfers between devices: 9.15 us -> 8.74 us
    ppermute x4, waiting for transfers between devices: 3.33 us -> 1.68 us  [the longest x3 1.06 us: paired(): arrived.append(lax.ppermute(sent, 'blk', to_chips(step)))]
    ppermute x1, starting transfers between devices: 1.61 us -> 0.42 us  [paired(): beside = lax.ppermute(block, 'blk', neighbour)]
    ppermute x3, waiting for transfers between devices: 2.94 us -> 3.6 us  [paired(): lax.ppermute(block, 'blk', to_chips(step))]
    ppermute x4, starting transfers between devices: 5.55 us -> 4.97 us  [the longest x3 4.9 us: paired(): arrived.append(lax.ppermute(sent, 'blk', to_chips(step)))]
    ppermute x1, waiting for transfers between devices: 0.01 us -> 0.57 us  [paired(): z_beside = lax.ppermute(last[shard:], 'blk', neighbour)]
    pallas_call x6 -> x10, Pallas kernels: 3.52 us -> 3.66 us  [call(): pl.pallas_call(body, out_shape=[jax.ShapeDtypeStruct(*out) for out in out...]
  transfers between devices with their start and end apart: 20 -> 20, of which waited for: 8 -> 9; matrix products, arithmetic and copies ran while one was open for 0% -> 0% of each run, Pallas kernels for 7% -> 7%
where the time goes in v5:
time: 34.8 us; the launch traced here: 34.5 us
  starting transfers between devices  18.6 us (53%)
  waiting for transfers between devices  8.74 us (25%)
  Pallas kernels  3.66 us (11%)
  between operations  1.45 us (4%)
  local copies, waits for them, and re-layouts  1.39 us (4%)
  other arithmetic  0.64 us (2%)
    ppermute x3, starting transfers between devices, paired(): lax.ppermute(block, 'blk', to_chips(step))  5.8 us
    ppermute x3, starting transfers between devices, paired(): arrived.append(lax.ppermute(sent, 'blk', to_chips(step)))  4.9 us
    pallas_call x10, Pallas kernels, call(): pl.pallas_call(body, out_shape=[jax.ShapeDtypeStruct(*out) for out in out...  3.66 us
    ppermute x3, waiting for transfers between devices, paired(): lax.ppermute(block, 'blk', to_chips(step))  3.6 us
    ppermute x1, starting transfers between devices, paired(): q_far = lax.ppermute(q_own, 'rows', across)  3 us
    ppermute x1, starting transfers between devices, paired(): far_notes = lax.ppermute(notes, 'rows', across)  1.49 us
    ppermute x1, waiting for transfers between devices, paired(): far_notes = lax.ppermute(notes, 'rows', across)  1.44 us
    unnamed x10, local copies, waits for them, and re-layouts  1.39 us
  transfers between devices with their start and end apart: 20, of which 9 were waited for; matrix products, arithmetic and copies ran while one was open for 0% of the time, Pallas kernels for 7%

profile of v5, /device:TPU:0, one launch (start us, length us, event | category | flops | bytes accessed | tf_op | source)
XLA Modules:
  0.0 34.5 jit_solution(5891213540581939156)
XLA Ops:
  0.6 3.0 %collective-permute-start = (bf16[32,256]{1,0:T(8,128)(2,1)}, bf16[32,256]{1,0:T(8,128)(2,1)S(1)}, u32[]{:S(2)}, u32[]{:S(2)}) collective-permute-start(bf16[32,256]{1,0:T(8,128)(2,1)} %bitcast.10), channel_id=1, source_target_pairs={{0,1},{1,0},{2,3},{3,2},{4,5},{5,4},{6,7},{7,6},{8,9},{9,8},{10,11... | collective-permute-start | bytes 49160 | tf_op jit(solution)/shard_map/ppermute | solution.py:191
  3.6 0.1 collective-permute-start.10
  4.4 0.6 %copy-done.2 = s32[1,1,20]{2,1,0:T(1,128)S(1)} copy-done((s32[1,1,20]{2,1,0:T(1,128)S(1)}, s32[1,1,20]{2,1,0:T(1,128)}, u32[]{:S(2)}) %copy-start.2) | copy-done | bytes 104
  5.0 0.0 copy-done.3
  5.0 0.0 copy-done.4
  5.1 0.7 %copy-done.1 = bf16[1,32,256]{2,1,0:T(8,128)(2,1)S(1)} copy-done((bf16[1,32,256]{2,1,0:T(8,128)(2,1)S(1)}, bf16[1,32,256]{2,1,0:T(8,128)(2,1)}, u32[]{:S(2)}) %copy-start.1) | copy-done | bytes 16408
  5.8 0.0 collective-permute-done.q_far
  5.8 0.0 copy-start
  5.8 0.1 collective-permute-start.1
  5.9 1.2 %collective-permute-done.1 = bf16[64,256]{1,0:T(8,128)(2,1)S(1)} collective-permute-done((bf16[64,256]{1,0:T(8,128)(2,1)S(1)}, bf16[64,256]{1,0:T(8,128)(2,1)S(1)}, u32[]{:S(2)}, u32[]{:S(2)}) %collective-permute-start.1) | collective-permute-done | bytes 32800 | tf_op jit(solution)/shard_map/ppermute | solution.py:212
  7.1 5.0 %collective-permute-start.5 = (bf16[128,256]{1,0:T(8,128)(2,1)S(1)}, bf16[128,256]{1,0:T(8,128)(2,1)S(1)}, u32[]{:S(2)}, u32[]{:S(2)}) collective-permute-start(bf16[128,256]{1,0:T(8,128)(2,1)S(1)} %pad_maximum_fusion.refs_0_), channel_id=1, source_target_pairs={{0,28},{2,26},{4,24},{6,30},{8,20},{10,18},{12,16},{14,22},{16,12}... | collective-permute-start | bytes 196616 | tf_op jit(solution)/shard_map/ppermute | solution.py:213
  12.1 0.0 collective-permute-start.4
  12.1 0.8 %collective-permute-start.3 = (bf16[128,256]{1,0:T(8,128)(2,1)S(1)}, bf16[128,256]{1,0:T(8,128)(2,1)S(1)}, u32[]{:S(2)}, u32[]{:S(2)}) collective-permute-start(bf16[128,256]{1,0:T(8,128)(2,1)S(1)} %pad_maximum_fusion.refs_0_), channel_id=1, source_target_pairs={{0,8},{2,14},{4,12},{6,10},{8,0},{10,6},{12,4},{14,2},{16,24},{18,... | collective-permute-start | bytes 196616 | tf_op jit(solution)/shard_map/ppermute | solution.py:213
  12.9 0.4 %collective-permute-start.2 = (bf16[128,256]{1,0:T(8,128)(2,1)S(1)}, bf16[128,256]{1,0:T(8,128)(2,1)S(1)}, u32[]{:S(2)}, u32[]{:S(2)}) collective-permute-start(bf16[128,256]{1,0:T(8,128)(2,1)S(1)} %pad_maximum_fusion.refs_0_), channel_id=1, source_target_pairs={{0,4},{2,6},{4,0},{6,2},{8,12},{10,14},{12,8},{14,10},{16,20},{18,... | collective-permute-start | bytes 196616 | tf_op jit(solution)/shard_map/ppermute | solution.py:214
  13.3 1.5 %collective-permute-done.5.refs_4_ = bf16[128,256]{1,0:T(8,128)(2,1)S(1)} collective-permute-done((bf16[128,256]{1,0:T(8,128)(2,1)S(1)}, bf16[128,256]{1,0:T(8,128)(2,1)S(1)}, u32[]{:S(2)}, u32[]{:S(2)}) %collective-permute-start.5) | collective-permute-done | bytes 65568 | tf_op jit(solution)/shard_map/ppermute | solution.py:213
  14.8 0.0 collective-permute-start.8
  14.8 0.7 %turned.1 = (bf16[512,512]{1,0:T(8,128)(2,1)S(1)}, bf16[512,512]{1,0:T(8,128)(2,1)S(1)}) custom-call(s32[8,128]{1,0:T(8,128)S(1)} %get-tuple-element.31.notes.refs_8_.refs_1_, bf16[20,128,128]{2,1,0:T(8,128)(2,1)S(1)} %bitcast.8), custom_call_target="tpu_custom_call" | custom-call | flops 2147483648 | tf_op jit(solution)/shard_map/turned/pallas_call | solution.py:177
  15.5 2.1 %collective-permute-done.4.refs_3_ = bf16[128,256]{1,0:T(8,128)(2,1)S(1)} collective-permute-done((bf16[128,256]{1,0:T(8,128)(2,1)S(1)}, bf16[128,256]{1,0:T(8,128)(2,1)S(1)}, u32[]{:S(2)}, u32[]{:S(2)}) %collective-permute-start.4) | collective-permute-done | bytes 65568 | tf_op jit(solution)/shard_map/ppermute | solution.py:213
  17.6 0.0 collective-permute-done.3.refs_2_
  17.6 0.0 collective-permute-start.6
  17.6 0.5 %collective-permute-start.7 = (bf16[128,256]{1,0:T(8,128)(2,1)S(1)}, bf16[128,256]{1,0:T(8,128)(2,1)S(1)}, u32[]{:S(2)}, u32[]{:S(2)}) collective-permute-start(bf16[128,256]{1,0:T(8,128)(2,1)S(1)} %collective-permute-done.4.refs_3_), channel_id=1, source_target_pairs={{0,2},{2,0},{4,6},{6,4},{8,10},{10,8},{12,14},{14,12},{16,18},{18,... | collective-permute-start | bytes 196616 | tf_op jit(solution)/shard_map/ppermute | solution.py:227
  18.1 0.0 collective-permute-done.2.refs_1_
  18.1 1.5 %collective-permute-start.9 = (s32[8,128]{1,0:T(8,128)S(1)}, s32[8,128]{1,0:T(8,128)S(1)}, u32[]{:S(2)}, u32[]{:S(2)}) collective-permute-start(s32[8,128]{1,0:T(8,128)S(1)} %get-tuple-element.31.notes.refs_8_.refs_1_), channel_id=1, source_target_pairs={{0,1},{1,0},{2,3},{3,2},{4,5},{5,4},{6,7},{7,6},{8,9},{9,8},{10,11... | collective-permute-start | bytes 12296 | tf_op jit(solution)/shard_map/ppermute | solution.py:226
  19.6 0.0 collective-permute-done.8.refs_7_
  19.6 0.0 collective-permute-done.6.refs_5_
  19.6 0.0 collective-permute-done.7.refs_6_
  19.6 0.7 %near_products.1 = (f32[512,256]{1,0:T(8,128)S(1)}, bf16[512,256]{1,0:T(8,128)(2,1)S(1)}) custom-call(bf16[128,256]{1,0:T(8,128)(2,1)S(1)} %pad_maximum_fusion.refs_0_, bf16[128,256]{1,0:T(8,128)(2,1)S(1)} %collective-permute-done.2.refs_1_, bf16[128,256]{1,0:T(8,128)(2,1)S(1)} %collective-permute-done.3.refs_2_, ...), custom_call_target="tpu_custom_call" | custom-call | flops 1 | tf_op jit(solution)/shard_map/near_products/pallas_call | solution.py:177
  20.3 1.4 %collective-permute-done.9.refs_2_ = s32[8,128]{1,0:T(8,128)S(1)} collective-permute-done((s32[8,128]{1,0:T(8,128)S(1)}, s32[8,128]{1,0:T(8,128)S(1)}, u32[]{:S(2)}, u32[]{:S(2)}) %collective-permute-start.9) | collective-permute-done | bytes 4128 | tf_op jit(solution)/shard_map/ppermute | solution.py:226
  21.7 0.0 collective-permute-done.10.refs_3_
  21.7 1.1 %products.1 = (bf16[512,256]{1,0:T(8,128)(2,1)S(1)}, f32[64,256]{1,0:T(8,128)S(1)}, f32[64,256]{1,0:T(8,128)S(1)}, f32[64,256]{1,0:T(8,128)S(1)}, f32[64,256]{1,...) custom-call(f32[512,256]{1,0:T(8,128)S(1)} %get-tuple-element.37.ref, ...), custom_call_target="tpu_custom_call" | custom-call | tf_op jit(solution)/shard_map/products/pallas_call | solution.py:177
  22.9 0.1 collective-permute-start.13
  23.0 0.5 %collective-permute-start.11 = (f32[64,256]{1,0:T(8,128)S(1)}, f32[64,256]{1,0:T(8,128)S(1)}, u32[]{:S(2)}, u32[]{:S(2)}) collective-permute-start(f32[64,256]{1,0:T(8,128)S(1)} %get-tuple-element.42), channel_id=1, source_target_pairs={{0,2},{2,0},{4,6},{6,4},{8,10},{10,8},{12,14},{14,12},{16,18},{18,... | collective-permute-start | bytes 196616 | tf_op jit(solution)/shard_map/ppermute | solution.py:246
  23.4 0.1 collective-permute-start.15
  23.5 0.4 %collective-permute-start.17 = (f32[64,256]{1,0:T(8,128)S(1)}, f32[64,256]{1,0:T(8,128)S(1)}, u32[]{:S(2)}, u32[]{:S(2)}) collective-permute-start(f32[64,256]{1,0:T(8,128)S(1)} %get-tuple-element.53), channel_id=1, source_target_pairs={{0,2},{2,0},{4,6},{6,4},{8,10},{10,8},{12,14},{14,12},{16,18},{18,... | collective-permute-start | bytes 196616 | tf_op jit(solution)/shard_map/ppermute | solution.py:246
  24.0 0.2 collective-permute-done.13.given
  24.2 3.3 %collective-permute-start.14 = (s16[80,256]{1,0:T(8,128)(2,1)S(1)}, s16[80,256]{1,0:T(8,128)(2,1)S(1)}, u32[]{:S(2)}, u32[]{:S(2)}) collective-permute-start(s16[80,256]{1,0:T(8,128)(2,1)S(1)} %coded.4), channel_id=1, source_target_pairs={{0,28},{2,26},{4,24},{6,30},{8,20},{10,18},{12,16},{14,22},{16,12}... | collective-permute-start | bytes 122888 | tf_op jit(solution)/shard_map/ppermute | solution.py:255
  27.6 0.1 collective-permute-start.12
  27.7 0.0 collective-permute-done.15.given
  27.7 1.5 %collective-permute-start.16 = (s16[80,256]{1,0:T(8,128)(2,1)S(1)}, s16[80,256]{1,0:T(8,128)(2,1)S(1)}, u32[]{:S(2)}, u32[]{:S(2)}) collective-permute-start(s16[80,256]{1,0:T(8,128)(2,1)S(1)} %coded.5), channel_id=1, source_target_pairs={{0,8},{2,14},{4,12},{6,10},{8,0},{10,6},{12,4},{14,2},{16,24},{18,... | collective-permute-start | bytes 122888 | tf_op jit(solution)/shard_map/ppermute | solution.py:255
  29.2 0.0 collective-permute-done.17
  29.3 1.2 %collective-permute-start.19 = (f32[32,256]{1,0:T(8,128)S(1)}, f32[32,256]{1,0:T(8,128)S(1)}, u32[]{:S(2)}, u32[]{:S(2)}) collective-permute-start(f32[32,256]{1,0:T(8,128)S(1)} %slice.4), channel_id=1, source_target_pairs={{0,4},{2,6},{4,0},{6,2},{8,12},{10,14},{12,8},{14,10},{16,20},{18,... | collective-permute-start | bytes 98312 | tf_op jit(solution)/shard_map/ppermute | solution.py:257
  30.5 0.9 %collective-permute-done.14.refs_0_ = s16[80,256]{1,0:T(8,128)(2,1)S(1)} collective-permute-done((s16[80,256]{1,0:T(8,128)(2,1)S(1)}, s16[80,256]{1,0:T(8,128)(2,1)S(1)}, u32[]{:S(2)}, u32[]{:S(2)}) %collective-permute-start.14) | collective-permute-done | bytes 40992 | tf_op jit(solution)/shard_map/ppermute | solution.py:255
  31.3 1.0 %owned.1 = bf16[256,256]{1,0:T(8,128)(2,1)} custom-call(bf16[512,256]{1,0:T(8,128)(2,1)S(1)} %get-tuple-element.46.refs_0_, s32[8,128]{1,0:T(8,128)S(1)} %get-tuple-element.31.notes.refs_8_.refs_1_), custom_call_target="tpu_custom_call" | custom-call | tf_op jit(solution)/shard_map/owned/pallas_call | solution.py:177
  32.4 0.2 collective-permute-done.12.refs_1_
  32.6 0.1 collective-permute-start.18
  32.7 0.6 %collective-permute-done.19 = f32[32,256]{1,0:T(8,128)S(1)} collective-permute-done((f32[32,256]{1,0:T(8,128)S(1)}, f32[32,256]{1,0:T(8,128)S(1)}, u32[]{:S(2)}, u32[]{:S(2)}) %collective-permute-start.19) | collective-permute-done | bytes 32800 | tf_op jit(solution)/shard_map/ppermute | solution.py:257
  33.2 0.6 %collective-permute-done.18 = f32[32,256]{1,0:T(8,128)S(1)} collective-permute-done((f32[32,256]{1,0:T(8,128)S(1)}, f32[32,256]{1,0:T(8,128)S(1)}, u32[]{:S(2)}, u32[]{:S(2)}) %collective-permute-start.18) | collective-permute-done | bytes 32800 | tf_op jit(solution)/shard_map/ppermute | solution.py:272
  33.9 0.6 %add_bitcast_fusion = f32[1,32,256]{2,1,0:T(8,128)} fusion(f32[32,256]{1,0:T(8,128)S(1)} %get-tuple-element.54, f32[32,256]{1,0:T(8,128)S(1)} %collective-permute-done.18, f32[32,256]{1,0:T(8,128)S(1)} %collective-permute-done.19), kind=kLoop, calls=%fused_computation.1 | loop fusion | flops 16384 | bytes 131072 | tf_op jit(solution)/shard_map/broadcast_in_dim | solution.py:273
  (16 shorter events, 0.2 us)
Async XLA Ops:
  0.6 5.2 %collective-permute-start = (bf16[32,256]{1,0:T(8,128)(2,1)}, bf16[32,256]{1,0:T(8,128)(2,1)S(1)}, u32[]{:S(2)}, u32[]{:S(2)}) collective-permute-start(bf16[32,256]{1,0:T(8,128)(2,1)} %bitcast.10), channel_id=1, source_target_pairs={{0,1},{1,0},{2,3},{3,2},{4,5},{5,4},{6,7},{7,6},{8,9},{9,8},{10,11... | collective-permute-start | bytes 49160 | tf_op jit(solution)/shard_map/ppermute | solution.py:191
  3.6 18.1 %collective-permute-start.10 = (bf16[20,128,128]{2,1,0:T(8,128)(2,1)}, bf16[20,128,128]{2,1,0:T(8,128)(2,1)S(1)}, u32[]{:S(2)}, u32[]{:S(2)}) collective-permute-start(bf16[20,128,128]{2,1,0:T(8,128)(2,1)} %bitcast.7), channel_id=1, source_target_pairs={{0,1},{1,0},{2,3},{3,2},{4,5},{5,4},{6,7},{7,6},{8,9},{9,8},{10,11... | collective-permute-start | bytes 1966088 | tf_op jit(solution)/shard_map/ppermute | solution.py:192
  4.4 0.7 %copy-start.2 = (s32[1,1,20]{2,1,0:T(1,128)S(1)}, s32[1,1,20]{2,1,0:T(1,128)}, u32[]{:S(2)}) copy-start(s32[1,1,20]{2,1,0:T(1,128)} %param.8) | copy-start | bytes 244
  4.4 0.7 %copy-start.3 = (s32[1,1,20,1]{2,3,1,0:T(1,128)S(1)}, s32[1,1,20,1]{2,3,1,0:T(1,128)}, u32[]{:S(2)}) copy-start(s32[1,1,20,1]{2,3,1,0:T(1,128)} %param.9) | copy-start | bytes 244
  4.4 0.7 %copy-start.4 = (s32[1,4]{1,0:T(1,128)S(1)}, s32[1,4]{1,0:T(1,128)}, u32[]{:S(2)}) copy-start(s32[1,4]{1,0:T(1,128)} %owners.1) | copy-start | bytes 52
  5.1 0.7 %copy-start.1 = (bf16[1,32,256]{2,1,0:T(8,128)(2,1)S(1)}, bf16[1,32,256]{2,1,0:T(8,128)(2,1)}, u32[]{:S(2)}) copy-start(bf16[1,32,256]{2,1,0:T(8,128)(2,1)} %param.6) | copy-start | bytes 49156
  5.8 9.0 %copy-start = (bf16[1,1,20,128,128]{4,3,2,1,0:T(8,128)(2,1)S(1)}, bf16[1,1,20,128,128]{4,3,2,1,0:T(8,128)(2,1)}, u32[]{:S(2)}) copy-start(bf16[1,1,20,128,128]{4,3,2,1,0:T(8,128)(2,1)} %param.7) | copy-start | bytes 1966084
  5.8 1.3 %collective-permute-start.1 = (bf16[64,256]{1,0:T(8,128)(2,1)S(1)}, bf16[64,256]{1,0:T(8,128)(2,1)S(1)}, u32[]{:S(2)}, u32[]{:S(2)}) collective-permute-start(bf16[64,256]{1,0:T(8,128)(2,1)S(1)} %pair.1), channel_id=1, source_target_pairs={{0,2},{2,0},{4,6},{6,4},{8,10},{10,8},{12,14},{14,12},{16,18},{18,... | collective-permute-start | bytes 98312 | tf_op jit(solution)/shard_map/ppermute | solution.py:212
  7.1 7.7 %collective-permute-start.5 = (bf16[128,256]{1,0:T(8,128)(2,1)S(1)}, bf16[128,256]{1,0:T(8,128)(2,1)S(1)}, u32[]{:S(2)}, u32[]{:S(2)}) collective-permute-start(bf16[128,256]{1,0:T(8,128)(2,1)S(1)} %pad_maximum_fusion.refs_0_), channel_id=1, source_target_pairs={{0,28},{2,26},{4,24},{6,30},{8,20},{10,18},{12,16},{14,22},{16,12}... | collective-permute-start | bytes 196616 | tf_op jit(solution)/shard_map/ppermute | solution.py:213
  12.1 5.5 %collective-permute-start.4 = (bf16[128,256]{1,0:T(8,128)(2,1)S(1)}, bf16[128,256]{1,0:T(8,128)(2,1)S(1)}, u32[]{:S(2)}, u32[]{:S(2)}) collective-permute-start(bf16[128,256]{1,0:T(8,128)(2,1)S(1)} %pad_maximum_fusion.refs_0_), channel_id=1, source_target_pairs={{0,16},{2,22},{4,20},{6,18},{8,24},{10,30},{12,28},{14,26},{16,0},... | collective-permute-start | bytes 196616 | tf_op jit(solution)/shard_map/ppermute | solution.py:213
  12.1 5.5 %collective-permute-start.3 = (bf16[128,256]{1,0:T(8,128)(2,1)S(1)}, bf16[128,256]{1,0:T(8,128)(2,1)S(1)}, u32[]{:S(2)}, u32[]{:S(2)}) collective-permute-start(bf16[128,256]{1,0:T(8,128)(2,1)S(1)} %pad_maximum_fusion.refs_0_), channel_id=1, source_target_pairs={{0,8},{2,14},{4,12},{6,10},{8,0},{10,6},{12,4},{14,2},{16,24},{18,... | collective-permute-start | bytes 196616 | tf_op jit(solution)/shard_map/ppermute | solution.py:213
  12.9 5.2 %collective-permute-start.2 = (bf16[128,256]{1,0:T(8,128)(2,1)S(1)}, bf16[128,256]{1,0:T(8,128)(2,1)S(1)}, u32[]{:S(2)}, u32[]{:S(2)}) collective-permute-start(bf16[128,256]{1,0:T(8,128)(2,1)S(1)} %pad_maximum_fusion.refs_0_), channel_id=1, source_target_pairs={{0,4},{2,6},{4,0},{6,2},{8,12},{10,14},{12,8},{14,10},{16,20},{18,... | collective-permute-start | bytes 196616 | tf_op jit(solution)/shard_map/ppermute | solution.py:214
  14.8 4.8 %collective-permute-start.8 = (bf16[128,256]{1,0:T(8,128)(2,1)S(1)}, bf16[128,256]{1,0:T(8,128)(2,1)S(1)}, u32[]{:S(2)}, u32[]{:S(2)}) collective-permute-start(bf16[128,256]{1,0:T(8,128)(2,1)S(1)} %collective-permute-done.5.refs_4_), channel_id=1, source_target_pairs={{0,2},{2,0},{4,6},{6,4},{8,10},{10,8},{12,14},{14,12},{16,18},{18,... | collective-permute-start | bytes 196616 | tf_op jit(solution)/shard_map/ppermute | solution.py:227
  17.6 2.0 %collective-permute-start.6 = (bf16[128,256]{1,0:T(8,128)(2,1)S(1)}, bf16[128,256]{1,0:T(8,128)(2,1)S(1)}, u32[]{:S(2)}, u32[]{:S(2)}) collective-permute-start(bf16[128,256]{1,0:T(8,128)(2,1)S(1)} %collective-permute-done.3.refs_2_), channel_id=1, source_target_pairs={{0,2},{2,0},{4,6},{6,4},{8,10},{10,8},{12,14},{14,12},{16,18},{18,... | collective-permute-start | bytes 196616 | tf_op jit(solution)/shard_map/ppermute | solution.py:227
  17.6 2.0 %collective-permute-start.7 = (bf16[128,256]{1,0:T(8,128)(2,1)S(1)}, bf16[128,256]{1,0:T(8,128)(2,1)S(1)}, u32[]{:S(2)}, u32[]{:S(2)}) collective-permute-start(bf16[128,256]{1,0:T(8,128)(2,1)S(1)} %collective-permute-done.4.refs_3_), channel_id=1, source_target_pairs={{0,2},{2,0},{4,6},{6,4},{8,10},{10,8},{12,14},{14,12},{16,18},{18,... | collective-permute-start | bytes 196616 | tf_op jit(solution)/shard_map/ppermute | solution.py:227
  18.1 3.6 %collective-permute-start.9 = (s32[8,128]{1,0:T(8,128)S(1)}, s32[8,128]{1,0:T(8,128)S(1)}, u32[]{:S(2)}, u32[]{:S(2)}) collective-permute-start(s32[8,128]{1,0:T(8,128)S(1)} %get-tuple-element.31.notes.refs_8_.refs_1_), channel_id=1, source_target_pairs={{0,1},{1,0},{2,3},{3,2},{4,5},{5,4},{6,7},{7,6},{8,9},{9,8},{10,11... | collective-permute-start | bytes 12296 | tf_op jit(solution)/shard_map/ppermute | solution.py:226
  22.9 1.3 %collective-permute-start.13 = (f32[64,256]{1,0:T(8,128)S(1)}, f32[64,256]{1,0:T(8,128)S(1)}, u32[]{:S(2)}, u32[]{:S(2)}) collective-permute-start(f32[64,256]{1,0:T(8,128)S(1)} %get-tuple-element.45), channel_id=1, source_target_pairs={{0,2},{2,0},{4,6},{6,4},{8,10},{10,8},{12,14},{14,12},{16,18},{18,... | collective-permute-start | bytes 196616 | tf_op jit(solution)/shard_map/ppermute | solution.py:246
  23.0 4.6 %collective-permute-start.11 = (f32[64,256]{1,0:T(8,128)S(1)}, f32[64,256]{1,0:T(8,128)S(1)}, u32[]{:S(2)}, u32[]{:S(2)}) collective-permute-start(f32[64,256]{1,0:T(8,128)S(1)} %get-tuple-element.42), channel_id=1, source_target_pairs={{0,2},{2,0},{4,6},{6,4},{8,10},{10,8},{12,14},{14,12},{16,18},{18,... | collective-permute-start | bytes 196616 | tf_op jit(solution)/shard_map/ppermute | solution.py:246
  23.4 4.2 %collective-permute-start.15 = (f32[64,256]{1,0:T(8,128)S(1)}, f32[64,256]{1,0:T(8,128)S(1)}, u32[]{:S(2)}, u32[]{:S(2)}) collective-permute-start(f32[64,256]{1,0:T(8,128)S(1)} %get-tuple-element.51), channel_id=1, source_target_pairs={{0,2},{2,0},{4,6},{6,4},{8,10},{10,8},{12,14},{14,12},{16,18},{18,... | collective-permute-start | bytes 196616 | tf_op jit(solution)/shard_map/ppermute | solution.py:246
  23.5 5.7 %collective-permute-start.17 = (f32[64,256]{1,0:T(8,128)S(1)}, f32[64,256]{1,0:T(8,128)S(1)}, u32[]{:S(2)}, u32[]{:S(2)}) collective-permute-start(f32[64,256]{1,0:T(8,128)S(1)} %get-tuple-element.53), channel_id=1, source_target_pairs={{0,2},{2,0},{4,6},{6,4},{8,10},{10,8},{12,14},{14,12},{16,18},{18,... | collective-permute-start | bytes 196616 | tf_op jit(solution)/shard_map/ppermute | solution.py:246
  24.2 7.1 %collective-permute-start.14 = (s16[80,256]{1,0:T(8,128)(2,1)S(1)}, s16[80,256]{1,0:T(8,128)(2,1)S(1)}, u32[]{:S(2)}, u32[]{:S(2)}) collective-permute-start(s16[80,256]{1,0:T(8,128)(2,1)S(1)} %coded.4), channel_id=1, source_target_pairs={{0,28},{2,26},{4,24},{6,30},{8,20},{10,18},{12,16},{14,22},{16,12}... | collective-permute-start | bytes 122888 | tf_op jit(solution)/shard_map/ppermute | solution.py:255
  27.6 5.0 %collective-permute-start.12 = (s16[80,256]{1,0:T(8,128)(2,1)S(1)}, s16[80,256]{1,0:T(8,128)(2,1)S(1)}, u32[]{:S(2)}, u32[]{:S(2)}) collective-permute-start(s16[80,256]{1,0:T(8,128)(2,1)S(1)} %coded.3), channel_id=1, source_target_pairs={{0,16},{2,22},{4,20},{6,18},{8,24},{10,30},{12,28},{14,26},{16,0},... | collective-permute-start | bytes 122888 | tf_op jit(solution)/shard_map/ppermute | solution.py:255
  27.7 4.8 %collective-permute-start.16 = (s16[80,256]{1,0:T(8,128)(2,1)S(1)}, s16[80,256]{1,0:T(8,128)(2,1)S(1)}, u32[]{:S(2)}, u32[]{:S(2)}) collective-permute-start(s16[80,256]{1,0:T(8,128)(2,1)S(1)} %coded.5), channel_id=1, source_target_pairs={{0,8},{2,14},{4,12},{6,10},{8,0},{10,6},{12,4},{14,2},{16,24},{18,... | collective-permute-start | bytes 122888 | tf_op jit(solution)/shard_map/ppermute | solution.py:255
  29.3 4.0 %collective-permute-start.19 = (f32[32,256]{1,0:T(8,128)S(1)}, f32[32,256]{1,0:T(8,128)S(1)}, u32[]{:S(2)}, u32[]{:S(2)}) collective-permute-start(f32[32,256]{1,0:T(8,128)S(1)} %slice.4), channel_id=1, source_target_pairs={{0,4},{2,6},{4,0},{6,2},{8,12},{10,14},{12,8},{14,10},{16,20},{18,... | collective-permute-start | bytes 98312 | tf_op jit(solution)/shard_map/ppermute | solution.py:257
  32.6 1.3 %collective-permute-start.18 = (f32[32,256]{1,0:T(8,128)S(1)}, f32[32,256]{1,0:T(8,128)S(1)}, u32[]{:S(2)}, u32[]{:S(2)}) collective-permute-start(f32[32,256]{1,0:T(8,128)S(1)} %get-tuple-element.55), channel_id=1, source_target_pairs={{0,2},{2,0},{4,6},{6,4},{8,10},{10,8},{12,14},{14,12},{16,18},{18,... | collective-permute-start | bytes 98312 | tf_op jit(solution)/shard_map/ppermute | solution.py:272

commit v6 on v5

--- a/solution.py
+++ b/solution.py
@@ -222,7 +222,6 @@
         [pltpu.VMEM((height, width), jnp.float32)],
         cost=TURNED_COST,
     )
-    direct[1], *turned = lax.optimization_barrier((direct[1], *turned))
     far_notes = lax.ppermute(notes, "rows", across)
     relayed = [lax.ppermute(one, "blk", sibling) for one in direct]
 

time: 34.8 us -> 34.6 us (level)
    ppermute x3, waiting for transfers between devices: 1.06 us -> 2.47 us  [paired(): arrived.append(lax.ppermute(sent, 'blk', to_chips(step)))]
    ppermute x1, waiting for transfers between devices: 1.44 us -> 0.09 us  [paired(): far_notes = lax.ppermute(notes, 'rows', across)]
    ppermute x3, waiting for transfers between devices: 3.6 us -> 2.78 us  [paired(): lax.ppermute(block, 'blk', to_chips(step))]
    ppermute x1, starting transfers between devices: 1.2 us -> 0.47 us  [paired(): z_beside = lax.ppermute(last[shard:], 'blk', neighbour)]
    ppermute x3, starting transfers between devices: 4.9 us -> 5.62 us  [paired(): arrived.append(lax.ppermute(sent, 'blk', to_chips(step)))]
    ppermute x1, waiting for transfers between devices: 0.57 us -> 0.01 us  [paired(): z_beside = lax.ppermute(last[shard:], 'blk', neighbour)]
    ppermute x1, waiting for transfers between devices: 0.62 us -> 1.18 us  [paired(): z_share = z_mine + (lax.ppermute(z_theirs, 'blk', sibling) + z_beside)]
    ppermute x3, waiting for transfers between devices: 0.01 us -> 0.49 us  [paired(): relayed = [lax.ppermute(one, 'blk', sibling) for one in direct]]
  transfers between devices with their start and end apart: 20 -> 20, of which waited for: 9 -> 10; matrix products, arithmetic and copies ran while one was open for 0% -> 0% of each run, Pallas kernels for 7% -> 7%
where the time goes in v6:
time: 34.6 us; the launch traced here: 34.3 us
  starting transfers between devices  18.7 us (54%)
  waiting for transfers between devices  8.45 us (24%)
  Pallas kernels  3.66 us (11%)
  between operations  1.45 us (4%)
  local copies, waits for them, and re-layouts  1.39 us (4%)
  other arithmetic  0.64 us (2%)
    ppermute x3, starting transfers between devices, paired(): lax.ppermute(block, 'blk', to_chips(step))  5.8 us
    ppermute x3, starting transfers between devices, paired(): arrived.append(lax.ppermute(sent, 'blk', to_chips(step)))  5.62 us
    pallas_call x10, Pallas kernels, call(): pl.pallas_call(body, out_shape=[jax.ShapeDtypeStruct(*out) for out in out...  3.66 us
    ppermute x1, starting transfers between devices, paired(): q_far = lax.ppermute(q_own, 'rows', across)  3 us
    ppermute x3, waiting for transfers between devices, paired(): lax.ppermute(block, 'blk', to_chips(step))  2.78 us
    ppermute x3, waiting for transfers between devices, paired(): arrived.append(lax.ppermute(sent, 'blk', to_chips(step)))  2.47 us
    ppermute x1, starting transfers between devices, paired(): far_notes = lax.ppermute(notes, 'rows', across)  1.52 us
    unnamed x10, local copies, waits for them, and re-layouts  1.39 us
  transfers between devices with their start and end apart: 20, of which 10 were waited for; matrix products, arithmetic and copies ran while one was open for 0% of the time, Pallas kernels for 7%

profile of v6, /device:TPU:0, one launch (start us, length us, event | category | flops | bytes accessed | tf_op | source)
XLA Modules:
  0.0 34.3 jit_solution(7858954999794882217)
XLA Ops:
  0.6 3.0 %collective-permute-start = (bf16[32,256]{1,0:T(8,128)(2,1)}, bf16[32,256]{1,0:T(8,128)(2,1)S(1)}, u32[]{:S(2)}, u32[]{:S(2)}) collective-permute-start(bf16[32,256]{1,0:T(8,128)(2,1)} %bitcast.10), channel_id=1, source_target_pairs={{0,1},{1,0},{2,3},{3,2},{4,5},{5,4},{6,7},{7,6},{8,9},{9,8},{10,11... | collective-permute-start | bytes 49160 | tf_op jit(solution)/shard_map/ppermute | solution.py:191
  3.6 0.1 collective-permute-start.10
  4.4 0.6 %copy-done.2 = s32[1,1,20]{2,1,0:T(1,128)S(1)} copy-done((s32[1,1,20]{2,1,0:T(1,128)S(1)}, s32[1,1,20]{2,1,0:T(1,128)}, u32[]{:S(2)}) %copy-start.2) | copy-done | bytes 104
  5.0 0.0 copy-done.3
  5.0 0.0 copy-done.4
  5.1 0.7 %copy-done.1 = bf16[1,32,256]{2,1,0:T(8,128)(2,1)S(1)} copy-done((bf16[1,32,256]{2,1,0:T(8,128)(2,1)S(1)}, bf16[1,32,256]{2,1,0:T(8,128)(2,1)}, u32[]{:S(2)}) %copy-start.1) | copy-done | bytes 16408
  5.8 0.0 collective-permute-done.q_far
  5.8 0.0 copy-start
  5.8 0.1 collective-permute-start.1
  5.9 1.2 %collective-permute-done.1 = bf16[64,256]{1,0:T(8,128)(2,1)S(1)} collective-permute-done((bf16[64,256]{1,0:T(8,128)(2,1)S(1)}, bf16[64,256]{1,0:T(8,128)(2,1)S(1)}, u32[]{:S(2)}, u32[]{:S(2)}) %collective-permute-start.1) | collective-permute-done | bytes 32800 | tf_op jit(solution)/shard_map/ppermute | solution.py:212
  7.1 5.0 %collective-permute-start.5 = (bf16[128,256]{1,0:T(8,128)(2,1)S(1)}, bf16[128,256]{1,0:T(8,128)(2,1)S(1)}, u32[]{:S(2)}, u32[]{:S(2)}) collective-permute-start(bf16[128,256]{1,0:T(8,128)(2,1)S(1)} %pad_maximum_fusion.refs_0_), channel_id=1, source_target_pairs={{0,28},{2,26},{4,24},{6,30},{8,20},{10,18},{12,16},{14,22},{16,12}... | collective-permute-start | bytes 196616 | tf_op jit(solution)/shard_map/ppermute | solution.py:213
  12.1 0.0 collective-permute-start.4
  12.1 0.8 %collective-permute-start.3 = (bf16[128,256]{1,0:T(8,128)(2,1)S(1)}, bf16[128,256]{1,0:T(8,128)(2,1)S(1)}, u32[]{:S(2)}, u32[]{:S(2)}) collective-permute-start(bf16[128,256]{1,0:T(8,128)(2,1)S(1)} %pad_maximum_fusion.refs_0_), channel_id=1, source_target_pairs={{0,8},{2,14},{4,12},{6,10},{8,0},{10,6},{12,4},{14,2},{16,24},{18,... | collective-permute-start | bytes 196616 | tf_op jit(solution)/shard_map/ppermute | solution.py:213
  12.9 0.4 %collective-permute-start.2 = (bf16[128,256]{1,0:T(8,128)(2,1)S(1)}, bf16[128,256]{1,0:T(8,128)(2,1)S(1)}, u32[]{:S(2)}, u32[]{:S(2)}) collective-permute-start(bf16[128,256]{1,0:T(8,128)(2,1)S(1)} %pad_maximum_fusion.refs_0_), channel_id=1, source_target_pairs={{0,4},{2,6},{4,0},{6,2},{8,12},{10,14},{12,8},{14,10},{16,20},{18,... | collective-permute-start | bytes 196616 | tf_op jit(solution)/shard_map/ppermute | solution.py:214
  13.3 1.5 %collective-permute-done.5.refs_4_ = bf16[128,256]{1,0:T(8,128)(2,1)S(1)} collective-permute-done((bf16[128,256]{1,0:T(8,128)(2,1)S(1)}, bf16[128,256]{1,0:T(8,128)(2,1)S(1)}, u32[]{:S(2)}, u32[]{:S(2)}) %collective-permute-start.5) | collective-permute-done | bytes 65568 | tf_op jit(solution)/shard_map/ppermute | solution.py:213
  14.8 1.5 %collective-permute-start.9 = (s32[8,128]{1,0:T(8,128)S(1)}, s32[8,128]{1,0:T(8,128)S(1)}, u32[]{:S(2)}, u32[]{:S(2)}) collective-permute-start(s32[8,128]{1,0:T(8,128)S(1)} %get-tuple-element.29.refs_8_.notes.refs_1_), channel_id=1, source_target_pairs={{0,1},{1,0},{2,3},{3,2},{4,5},{5,4},{6,7},{7,6},{8,9},{9,8},{10,11... | collective-permute-start | bytes 12296 | tf_op jit(solution)/shard_map/ppermute | solution.py:225
  16.3 1.3 %collective-permute-done.4.refs_3_ = bf16[128,256]{1,0:T(8,128)(2,1)S(1)} collective-permute-done((bf16[128,256]{1,0:T(8,128)(2,1)S(1)}, bf16[128,256]{1,0:T(8,128)(2,1)S(1)}, u32[]{:S(2)}, u32[]{:S(2)}) %collective-permute-start.4) | collective-permute-done | bytes 65568 | tf_op jit(solution)/shard_map/ppermute | solution.py:213
  17.6 0.0 collective-permute-start.8
  17.6 0.0 collective-permute-done.3.refs_2_
  17.6 0.5 %collective-permute-start.7 = (bf16[128,256]{1,0:T(8,128)(2,1)S(1)}, bf16[128,256]{1,0:T(8,128)(2,1)S(1)}, u32[]{:S(2)}, u32[]{:S(2)}) collective-permute-start(bf16[128,256]{1,0:T(8,128)(2,1)S(1)} %collective-permute-done.4.refs_3_), channel_id=1, source_target_pairs={{0,2},{2,0},{4,6},{6,4},{8,10},{10,8},{12,14},{14,12},{16,18},{18,... | collective-permute-start | bytes 196616 | tf_op jit(solution)/shard_map/ppermute | solution.py:226
  18.1 0.0 collective-permute-done.2.refs_1_
  18.1 0.1 collective-permute-start.6
  18.2 0.7 %turned.1 = (bf16[512,512]{1,0:T(8,128)(2,1)S(1)}, bf16[512,512]{1,0:T(8,128)(2,1)S(1)}) custom-call(s32[8,128]{1,0:T(8,128)S(1)} %get-tuple-element.29.refs_8_.notes.refs_1_, bf16[20,128,128]{2,1,0:T(8,128)(2,1)S(1)} %bitcast.8), custom_call_target="tpu_custom_call" | custom-call | flops 2147483648 | tf_op jit(solution)/shard_map/turned/pallas_call | solution.py:177
  18.9 0.0 collective-permute-done.8.refs_7_
  18.9 0.1 collective-permute-done.7.refs_6_
  19.0 0.4 %collective-permute-done.6.refs_5_ = bf16[128,256]{1,0:T(8,128)(2,1)S(1)} collective-permute-done((bf16[128,256]{1,0:T(8,128)(2,1)S(1)}, bf16[128,256]{1,0:T(8,128)(2,1)S(1)}, u32[]{:S(2)}, u32[]{:S(2)}) %collective-permute-start.6) | collective-permute-done | bytes 65568 | tf_op jit(solution)/shard_map/ppermute | solution.py:226
  19.4 0.7 %near_products.1 = (f32[512,256]{1,0:T(8,128)S(1)}, bf16[512,256]{1,0:T(8,128)(2,1)S(1)}) custom-call(bf16[128,256]{1,0:T(8,128)(2,1)S(1)} %pad_maximum_fusion.refs_0_, bf16[128,256]{1,0:T(8,128)(2,1)S(1)} %collective-permute-done.2.refs_1_, bf16[128,256]{1,0:T(8,128)(2,1)S(1)} %collective-permute-done.3.refs_2_, ...), custom_call_target="tpu_custom_call" | custom-call | flops 1 | tf_op jit(solution)/shard_map/near_products/pallas_call | solution.py:177
  20.0 0.1 collective-permute-done.9.refs_2_
  20.1 0.0 collective-permute-done.10.refs_3_
  20.1 1.1 %products.1 = (bf16[512,256]{1,0:T(8,128)(2,1)S(1)}, f32[64,256]{1,0:T(8,128)S(1)}, f32[64,256]{1,0:T(8,128)S(1)}, f32[64,256]{1,0:T(8,128)S(1)}, f32[64,256]{1,...) custom-call(f32[512,256]{1,0:T(8,128)S(1)} %get-tuple-element.31.ref, ...), custom_call_target="tpu_custom_call" | custom-call | tf_op jit(solution)/shard_map/products/pallas_call | solution.py:177
  21.3 0.2 collective-permute-start.13
  21.4 0.4 %collective-permute-start.11 = (f32[64,256]{1,0:T(8,128)S(1)}, f32[64,256]{1,0:T(8,128)S(1)}, u32[]{:S(2)}, u32[]{:S(2)}) collective-permute-start(f32[64,256]{1,0:T(8,128)S(1)} %get-tuple-element.36), channel_id=1, source_target_pairs={{0,2},{2,0},{4,6},{6,4},{8,10},{10,8},{12,14},{14,12},{16,18},{18,... | collective-permute-start | bytes 196616 | tf_op jit(solution)/shard_map/ppermute | solution.py:245
  21.8 0.1 collective-permute-start.15
  21.9 0.4 %collective-permute-start.17 = (f32[64,256]{1,0:T(8,128)S(1)}, f32[64,256]{1,0:T(8,128)S(1)}, u32[]{:S(2)}, u32[]{:S(2)}) collective-permute-start(f32[64,256]{1,0:T(8,128)S(1)} %get-tuple-element.47), channel_id=1, source_target_pairs={{0,2},{2,0},{4,6},{6,4},{8,10},{10,8},{12,14},{14,12},{16,18},{18,... | collective-permute-start | bytes 196616 | tf_op jit(solution)/shard_map/ppermute | solution.py:245
  22.4 0.2 collective-permute-done.13.given
  22.6 4.7 %collective-permute-start.14 = (s16[80,256]{1,0:T(8,128)(2,1)S(1)}, s16[80,256]{1,0:T(8,128)(2,1)S(1)}, u32[]{:S(2)}, u32[]{:S(2)}) collective-permute-start(s16[80,256]{1,0:T(8,128)(2,1)S(1)} %coded.4), channel_id=1, source_target_pairs={{0,28},{2,26},{4,24},{6,30},{8,20},{10,18},{12,16},{14,22},{16,12}... | collective-permute-start | bytes 122888 | tf_op jit(solution)/shard_map/ppermute | solution.py:254
  27.4 0.0 collective-permute-done.11.given
  27.4 0.1 collective-permute-start.12
  27.5 0.8 %collective-permute-start.16 = (s16[80,256]{1,0:T(8,128)(2,1)S(1)}, s16[80,256]{1,0:T(8,128)(2,1)S(1)}, u32[]{:S(2)}, u32[]{:S(2)}) collective-permute-start(s16[80,256]{1,0:T(8,128)(2,1)S(1)} %coded.5), channel_id=1, source_target_pairs={{0,8},{2,14},{4,12},{6,10},{8,0},{10,6},{12,4},{14,2},{16,24},{18,... | collective-permute-start | bytes 122888 | tf_op jit(solution)/shard_map/ppermute | solution.py:254
  28.4 0.0 collective-permute-done.17
  28.4 0.5 %collective-permute-start.19 = (f32[32,256]{1,0:T(8,128)S(1)}, f32[32,256]{1,0:T(8,128)S(1)}, u32[]{:S(2)}, u32[]{:S(2)}) collective-permute-start(f32[32,256]{1,0:T(8,128)S(1)} %slice.4), channel_id=1, source_target_pairs={{0,4},{2,6},{4,0},{6,2},{8,12},{10,14},{12,8},{14,10},{16,20},{18,... | collective-permute-start | bytes 98312 | tf_op jit(solution)/shard_map/ppermute | solution.py:256
  28.9 0.5 %collective-permute-done.14.refs_0_ = s16[80,256]{1,0:T(8,128)(2,1)S(1)} collective-permute-done((s16[80,256]{1,0:T(8,128)(2,1)S(1)}, s16[80,256]{1,0:T(8,128)(2,1)S(1)}, u32[]{:S(2)}, u32[]{:S(2)}) %collective-permute-start.14) | collective-permute-done | bytes 40992 | tf_op jit(solution)/shard_map/ppermute | solution.py:254
  29.4 1.0 %owned.1 = bf16[256,256]{1,0:T(8,128)(2,1)} custom-call(bf16[512,256]{1,0:T(8,128)(2,1)S(1)} %get-tuple-element.40.refs_0_, s32[8,128]{1,0:T(8,128)S(1)} %get-tuple-element.29.refs_8_.notes.refs_1_), custom_call_target="tpu_custom_call" | custom-call | tf_op jit(solution)/shard_map/owned/pallas_call | solution.py:177
  30.4 1.9 %collective-permute-done.12.refs_1_ = s16[80,256]{1,0:T(8,128)(2,1)S(1)} collective-permute-done((s16[80,256]{1,0:T(8,128)(2,1)S(1)}, s16[80,256]{1,0:T(8,128)(2,1)S(1)}, u32[]{:S(2)}, u32[]{:S(2)}) %collective-permute-start.12) | collective-permute-done | bytes 40992 | tf_op jit(solution)/shard_map/ppermute | solution.py:254
  32.4 0.1 collective-permute-start.18
  32.5 0.0 collective-permute-done.19
  32.5 1.2 %collective-permute-done.18 = f32[32,256]{1,0:T(8,128)S(1)} collective-permute-done((f32[32,256]{1,0:T(8,128)S(1)}, f32[32,256]{1,0:T(8,128)S(1)}, u32[]{:S(2)}, u32[]{:S(2)}) %collective-permute-start.18) | collective-permute-done | bytes 32800 | tf_op jit(solution)/shard_map/ppermute | solution.py:271
  33.7 0.6 %add_bitcast_fusion = f32[1,32,256]{2,1,0:T(8,128)} fusion(f32[32,256]{1,0:T(8,128)S(1)} %get-tuple-element.48, f32[32,256]{1,0:T(8,128)S(1)} %collective-permute-done.18, f32[32,256]{1,0:T(8,128)S(1)} %collective-permute-done.19), kind=kLoop, calls=%fused_computation.1 | loop fusion | flops 16384 | bytes 131072 | tf_op jit(solution)/shard_map/broadcast_in_dim | solution.py:272
  (16 shorter events, 0.2 us)
Async XLA Ops:
  0.6 5.2 %collective-permute-start = (bf16[32,256]{1,0:T(8,128)(2,1)}, bf16[32,256]{1,0:T(8,128)(2,1)S(1)}, u32[]{:S(2)}, u32[]{:S(2)}) collective-permute-start(bf16[32,256]{1,0:T(8,128)(2,1)} %bitcast.10), channel_id=1, source_target_pairs={{0,1},{1,0},{2,3},{3,2},{4,5},{5,4},{6,7},{7,6},{8,9},{9,8},{10,11... | collective-permute-start | bytes 49160 | tf_op jit(solution)/shard_map/ppermute | solution.py:191
  3.6 16.5 %collective-permute-start.10 = (bf16[20,128,128]{2,1,0:T(8,128)(2,1)}, bf16[20,128,128]{2,1,0:T(8,128)(2,1)S(1)}, u32[]{:S(2)}, u32[]{:S(2)}) collective-permute-start(bf16[20,128,128]{2,1,0:T(8,128)(2,1)} %bitcast.7), channel_id=1, source_target_pairs={{0,1},{1,0},{2,3},{3,2},{4,5},{5,4},{6,7},{7,6},{8,9},{9,8},{10,11... | collective-permute-start | bytes 1966088 | tf_op jit(solution)/shard_map/ppermute | solution.py:192
  4.4 0.7 %copy-start.2 = (s32[1,1,20]{2,1,0:T(1,128)S(1)}, s32[1,1,20]{2,1,0:T(1,128)}, u32[]{:S(2)}) copy-start(s32[1,1,20]{2,1,0:T(1,128)} %param.8) | copy-start | bytes 244
  4.4 0.7 %copy-start.3 = (s32[1,1,20,1]{2,3,1,0:T(1,128)S(1)}, s32[1,1,20,1]{2,3,1,0:T(1,128)}, u32[]{:S(2)}) copy-start(s32[1,1,20,1]{2,3,1,0:T(1,128)} %param.9) | copy-start | bytes 244
  4.4 0.7 %copy-start.4 = (s32[1,4]{1,0:T(1,128)S(1)}, s32[1,4]{1,0:T(1,128)}, u32[]{:S(2)}) copy-start(s32[1,4]{1,0:T(1,128)} %owners.1) | copy-start | bytes 52
  5.1 0.7 %copy-start.1 = (bf16[1,32,256]{2,1,0:T(8,128)(2,1)S(1)}, bf16[1,32,256]{2,1,0:T(8,128)(2,1)}, u32[]{:S(2)}) copy-start(bf16[1,32,256]{2,1,0:T(8,128)(2,1)} %param.6) | copy-start | bytes 49156
  5.8 12.4 %copy-start = (bf16[1,1,20,128,128]{4,3,2,1,0:T(8,128)(2,1)S(1)}, bf16[1,1,20,128,128]{4,3,2,1,0:T(8,128)(2,1)}, u32[]{:S(2)}) copy-start(bf16[1,1,20,128,128]{4,3,2,1,0:T(8,128)(2,1)} %param.7) | copy-start | bytes 1966084
  5.8 1.3 %collective-permute-start.1 = (bf16[64,256]{1,0:T(8,128)(2,1)S(1)}, bf16[64,256]{1,0:T(8,128)(2,1)S(1)}, u32[]{:S(2)}, u32[]{:S(2)}) collective-permute-start(bf16[64,256]{1,0:T(8,128)(2,1)S(1)} %pair.1), channel_id=1, source_target_pairs={{0,2},{2,0},{4,6},{6,4},{8,10},{10,8},{12,14},{14,12},{16,18},{18,... | collective-permute-start | bytes 98312 | tf_op jit(solution)/shard_map/ppermute | solution.py:212
  7.1 7.7 %collective-permute-start.5 = (bf16[128,256]{1,0:T(8,128)(2,1)S(1)}, bf16[128,256]{1,0:T(8,128)(2,1)S(1)}, u32[]{:S(2)}, u32[]{:S(2)}) collective-permute-start(bf16[128,256]{1,0:T(8,128)(2,1)S(1)} %pad_maximum_fusion.refs_0_), channel_id=1, source_target_pairs={{0,28},{2,26},{4,24},{6,30},{8,20},{10,18},{12,16},{14,22},{16,12}... | collective-permute-start | bytes 196616 | tf_op jit(solution)/shard_map/ppermute | solution.py:213
  12.1 5.5 %collective-permute-start.4 = (bf16[128,256]{1,0:T(8,128)(2,1)S(1)}, bf16[128,256]{1,0:T(8,128)(2,1)S(1)}, u32[]{:S(2)}, u32[]{:S(2)}) collective-permute-start(bf16[128,256]{1,0:T(8,128)(2,1)S(1)} %pad_maximum_fusion.refs_0_), channel_id=1, source_target_pairs={{0,16},{2,22},{4,20},{6,18},{8,24},{10,30},{12,28},{14,26},{16,0},... | collective-permute-start | bytes 196616 | tf_op jit(solution)/shard_map/ppermute | solution.py:213
  12.1 5.5 %collective-permute-start.3 = (bf16[128,256]{1,0:T(8,128)(2,1)S(1)}, bf16[128,256]{1,0:T(8,128)(2,1)S(1)}, u32[]{:S(2)}, u32[]{:S(2)}) collective-permute-start(bf16[128,256]{1,0:T(8,128)(2,1)S(1)} %pad_maximum_fusion.refs_0_), channel_id=1, source_target_pairs={{0,8},{2,14},{4,12},{6,10},{8,0},{10,6},{12,4},{14,2},{16,24},{18,... | collective-permute-start | bytes 196616 | tf_op jit(solution)/shard_map/ppermute | solution.py:213
  12.9 5.2 %collective-permute-start.2 = (bf16[128,256]{1,0:T(8,128)(2,1)S(1)}, bf16[128,256]{1,0:T(8,128)(2,1)S(1)}, u32[]{:S(2)}, u32[]{:S(2)}) collective-permute-start(bf16[128,256]{1,0:T(8,128)(2,1)S(1)} %pad_maximum_fusion.refs_0_), channel_id=1, source_target_pairs={{0,4},{2,6},{4,0},{6,2},{8,12},{10,14},{12,8},{14,10},{16,20},{18,... | collective-permute-start | bytes 196616 | tf_op jit(solution)/shard_map/ppermute | solution.py:214
  14.8 5.3 %collective-permute-start.9 = (s32[8,128]{1,0:T(8,128)S(1)}, s32[8,128]{1,0:T(8,128)S(1)}, u32[]{:S(2)}, u32[]{:S(2)}) collective-permute-start(s32[8,128]{1,0:T(8,128)S(1)} %get-tuple-element.29.refs_8_.notes.refs_1_), channel_id=1, source_target_pairs={{0,1},{1,0},{2,3},{3,2},{4,5},{5,4},{6,7},{7,6},{8,9},{9,8},{10,11... | collective-permute-start | bytes 12296 | tf_op jit(solution)/shard_map/ppermute | solution.py:225
  17.6 1.3 %collective-permute-start.8 = (bf16[128,256]{1,0:T(8,128)(2,1)S(1)}, bf16[128,256]{1,0:T(8,128)(2,1)S(1)}, u32[]{:S(2)}, u32[]{:S(2)}) collective-permute-start(bf16[128,256]{1,0:T(8,128)(2,1)S(1)} %collective-permute-done.5.refs_4_), channel_id=1, source_target_pairs={{0,2},{2,0},{4,6},{6,4},{8,10},{10,8},{12,14},{14,12},{16,18},{18,... | collective-permute-start | bytes 196616 | tf_op jit(solution)/shard_map/ppermute | solution.py:226
  17.6 1.4 %collective-permute-start.7 = (bf16[128,256]{1,0:T(8,128)(2,1)S(1)}, bf16[128,256]{1,0:T(8,128)(2,1)S(1)}, u32[]{:S(2)}, u32[]{:S(2)}) collective-permute-start(bf16[128,256]{1,0:T(8,128)(2,1)S(1)} %collective-permute-done.4.refs_3_), channel_id=1, source_target_pairs={{0,2},{2,0},{4,6},{6,4},{8,10},{10,8},{12,14},{14,12},{16,18},{18,... | collective-permute-start | bytes 196616 | tf_op jit(solution)/shard_map/ppermute | solution.py:226
  18.1 1.3 %collective-permute-start.6 = (bf16[128,256]{1,0:T(8,128)(2,1)S(1)}, bf16[128,256]{1,0:T(8,128)(2,1)S(1)}, u32[]{:S(2)}, u32[]{:S(2)}) collective-permute-start(bf16[128,256]{1,0:T(8,128)(2,1)S(1)} %collective-permute-done.3.refs_2_), channel_id=1, source_target_pairs={{0,2},{2,0},{4,6},{6,4},{8,10},{10,8},{12,14},{14,12},{16,18},{18,... | collective-permute-start | bytes 196616 | tf_op jit(solution)/shard_map/ppermute | solution.py:226
  21.3 1.3 %collective-permute-start.13 = (f32[64,256]{1,0:T(8,128)S(1)}, f32[64,256]{1,0:T(8,128)S(1)}, u32[]{:S(2)}, u32[]{:S(2)}) collective-permute-start(f32[64,256]{1,0:T(8,128)S(1)} %get-tuple-element.39), channel_id=1, source_target_pairs={{0,2},{2,0},{4,6},{6,4},{8,10},{10,8},{12,14},{14,12},{16,18},{18,... | collective-permute-start | bytes 196616 | tf_op jit(solution)/shard_map/ppermute | solution.py:245
  21.4 5.9 %collective-permute-start.11 = (f32[64,256]{1,0:T(8,128)S(1)}, f32[64,256]{1,0:T(8,128)S(1)}, u32[]{:S(2)}, u32[]{:S(2)}) collective-permute-start(f32[64,256]{1,0:T(8,128)S(1)} %get-tuple-element.36), channel_id=1, source_target_pairs={{0,2},{2,0},{4,6},{6,4},{8,10},{10,8},{12,14},{14,12},{16,18},{18,... | collective-permute-start | bytes 196616 | tf_op jit(solution)/shard_map/ppermute | solution.py:245
  21.8 5.6 %collective-permute-start.15 = (f32[64,256]{1,0:T(8,128)S(1)}, f32[64,256]{1,0:T(8,128)S(1)}, u32[]{:S(2)}, u32[]{:S(2)}) collective-permute-start(f32[64,256]{1,0:T(8,128)S(1)} %get-tuple-element.45), channel_id=1, source_target_pairs={{0,2},{2,0},{4,6},{6,4},{8,10},{10,8},{12,14},{14,12},{16,18},{18,... | collective-permute-start | bytes 196616 | tf_op jit(solution)/shard_map/ppermute | solution.py:245
  21.9 6.4 %collective-permute-start.17 = (f32[64,256]{1,0:T(8,128)S(1)}, f32[64,256]{1,0:T(8,128)S(1)}, u32[]{:S(2)}, u32[]{:S(2)}) collective-permute-start(f32[64,256]{1,0:T(8,128)S(1)} %get-tuple-element.47), channel_id=1, source_target_pairs={{0,2},{2,0},{4,6},{6,4},{8,10},{10,8},{12,14},{14,12},{16,18},{18,... | collective-permute-start | bytes 196616 | tf_op jit(solution)/shard_map/ppermute | solution.py:245
  22.6 6.8 %collective-permute-start.14 = (s16[80,256]{1,0:T(8,128)(2,1)S(1)}, s16[80,256]{1,0:T(8,128)(2,1)S(1)}, u32[]{:S(2)}, u32[]{:S(2)}) collective-permute-start(s16[80,256]{1,0:T(8,128)(2,1)S(1)} %coded.4), channel_id=1, source_target_pairs={{0,28},{2,26},{4,24},{6,30},{8,20},{10,18},{12,16},{14,22},{16,12}... | collective-permute-start | bytes 122888 | tf_op jit(solution)/shard_map/ppermute | solution.py:254
  27.4 5.0 %collective-permute-start.12 = (s16[80,256]{1,0:T(8,128)(2,1)S(1)}, s16[80,256]{1,0:T(8,128)(2,1)S(1)}, u32[]{:S(2)}, u32[]{:S(2)}) collective-permute-start(s16[80,256]{1,0:T(8,128)(2,1)S(1)} %coded.3), channel_id=1, source_target_pairs={{0,16},{2,22},{4,20},{6,18},{8,24},{10,30},{12,28},{14,26},{16,0},... | collective-permute-start | bytes 122888 | tf_op jit(solution)/shard_map/ppermute | solution.py:254
  27.5 4.8 %collective-permute-start.16 = (s16[80,256]{1,0:T(8,128)(2,1)S(1)}, s16[80,256]{1,0:T(8,128)(2,1)S(1)}, u32[]{:S(2)}, u32[]{:S(2)}) collective-permute-start(s16[80,256]{1,0:T(8,128)(2,1)S(1)} %coded.5), channel_id=1, source_target_pairs={{0,8},{2,14},{4,12},{6,10},{8,0},{10,6},{12,4},{14,2},{16,24},{18,... | collective-permute-start | bytes 122888 | tf_op jit(solution)/shard_map/ppermute | solution.py:254
  28.4 4.1 %collective-permute-start.19 = (f32[32,256]{1,0:T(8,128)S(1)}, f32[32,256]{1,0:T(8,128)S(1)}, u32[]{:S(2)}, u32[]{:S(2)}) collective-permute-start(f32[32,256]{1,0:T(8,128)S(1)} %slice.4), channel_id=1, source_target_pairs={{0,4},{2,6},{4,0},{6,2},{8,12},{10,14},{12,8},{14,10},{16,20},{18,... | collective-permute-start | bytes 98312 | tf_op jit(solution)/shard_map/ppermute | solution.py:256
  32.4 1.3 %collective-permute-start.18 = (f32[32,256]{1,0:T(8,128)S(1)}, f32[32,256]{1,0:T(8,128)S(1)}, u32[]{:S(2)}, u32[]{:S(2)}) collective-permute-start(f32[32,256]{1,0:T(8,128)S(1)} %get-tuple-element.49), channel_id=1, source_target_pairs={{0,2},{2,0},{4,6},{6,4},{8,10},{10,8},{12,14},{14,12},{16,18},{18,... | collective-permute-start | bytes 98312 | tf_op jit(solution)/shard_map/ppermute | solution.py:271

commit v7 on v6

--- a/solution.py
+++ b/solution.py
@@ -60,15 +60,24 @@
         )
 
 
-def coded_kernel(ours, given, sent):
-    rows = ours.shape[0]
-    x = ours[...] + given[...]
+def coded_kernel(step, sides, z, given, sent):
+    rows = given.shape[0]
+    core, _, rows_of = own_place(sides, rows // 2)
+    ours = [z[rows_of(step, core, owner), :] for owner in (core, 1 - core)]
+    x = jnp.concatenate(ours, axis=0) + given[...]
     top = jnp.max(jnp.abs(x), axis=0, keepdims=True)
     power = jnp.ceil(jnp.log2(jnp.maximum(top, 1e-30)))
     whole = jnp.clip(jnp.round(x * jnp.exp2(15.0 - power)), -32767.0, 32767.0)
     sent[0:rows, :] = whole.astype(jnp.int32).astype(jnp.int16)
     power = jnp.broadcast_to(power, (SCALE_ROWS, x.shape[1]))
     sent[rows:, :] = power.astype(jnp.int32).astype(jnp.int16)
+
+
+def last_kernel(sides, z, given, last):
+    shard = last.shape[0] // 2
+    core, rows_at, _ = own_place(sides, shard)
+    last[0:shard, :] = z[rows_at(0, core), :] + given[0:shard, :]
+    last[shard:, :] = z[rows_at(1, core), :] + given[shard:, :]
 
 
 def gather_kernel(*refs):
@@ -121,21 +130,19 @@
 
 def product_kernel(rounds, sides, *refs):
     y_near, q_far, far_notes, far_tiles, high, low, y = refs[:7]
-    keep, give = refs[7 : 8 + rounds], refs[8 + rounds : 9 + 2 * rounds]
-    total, z = refs[9 + 2 * rounds :]
+    z, *give, total = refs[7:]
     total[...] = y_near[...]
     add_tiles(total, far_notes, far_tiles, q_far)
     y[...] = total[...].astype(y.dtype)
     z[...] = dot(high[...], y[...]) + dot(low[...], y[...])
-    shard = keep[0].shape[0] // 2
+    shard = give[0].shape[0] // 2
     core, rows_at, rows_of = own_place(sides, shard)
+    side = 1 - core
     for step in range(rounds):
-        for ref, side in ((keep[step], core), (give[step], 1 - core)):
-            ref[0:shard, :] = z[rows_of(step, side, side), :]
-            ref[shard : 2 * shard, :] = z[rows_of(step, side, 1 - side), :]
-    for ref, side in ((keep[rounds], core), (give[rounds], 1 - core)):
-        ref[0:shard, :] = z[rows_at(0, side), :]
-        ref[shard : 2 * shard, :] = z[rows_at(1, side), :]
+        give[step][0:shard, :] = z[rows_of(step, side, side), :]
+        give[step][shard : 2 * shard, :] = z[rows_of(step, side, core), :]
+    give[rounds][0:shard, :] = z[rows_at(0, side), :]
+    give[rounds][shard : 2 * shard, :] = z[rows_at(1, side), :]
 
 
 def owned_kernel(group, y, notes, y_out):
@@ -213,7 +220,7 @@
     direct = [lax.ppermute(block, "blk", to_chips(step)) for step in range(rounds)]
     beside = lax.ppermute(block, "blk", neighbour)
 
-    stack, notes, direct[0] = lax.optimization_barrier((stack, notes, direct[0]))
+    stack, direct[0] = lax.optimization_barrier((stack, direct[0]))
     turned = call(
         turned_kernel,
         "turned",
@@ -233,26 +240,30 @@
         [pltpu.VMEM((width, rank), q_own.dtype)],
         cost=1,
     )
-    y, *pieces = call(
+    y, z, *give = call(
         lambda *refs: product_kernel(rounds, sides, *refs),
         "products",
-        [((height, rank), jnp.bfloat16)]
-        + [((2 * shard, rank), jnp.float32)] * (2 * rounds + 2),
+        [((height, rank), jnp.bfloat16), ((width, rank), jnp.float32)]
+        + [((2 * shard, rank), jnp.float32)] * (rounds + 1),
         [y_near, q_other, far_notes, far_tiles, *turned],
-        [pltpu.VMEM((height, rank), jnp.float32), pltpu.VMEM((width, rank), jnp.float32)],
-    )
-    keep, give = pieces[: rounds + 1], pieces[rounds + 1 :]
+        [pltpu.VMEM((height, rank), jnp.float32)],
+    )
     given = [lax.ppermute(one, "blk", sibling) for one in give]
     arrived = []
     for step in range(rounds):
         (sent,) = call(
-            coded_kernel,
+            lambda *refs, step=step: coded_kernel(step, sides, *refs),
             "coded",
             [((2 * shard + SCALE_ROWS, rank), jnp.int16)],
-            [keep[step], given[step]],
+            [z, given[step]],
         )
         arrived.append(lax.ppermute(sent, "blk", to_chips(step)))
-    last = keep[rounds] + given[rounds]
+    (last,) = call(
+        lambda *refs: last_kernel(sides, *refs),
+        "last",
+        [((2 * shard, rank), jnp.float32)],
+        [z, given[rounds]],
+    )
     z_beside = lax.ppermute(last[shard:], "blk", neighbour)
     y, arrived[0] = lax.optimization_barrier((y, arrived[0]))
     (y_owned,) = call(

time: 34.6 us -> 34.6 us (level)
    pallas_call x10 -> x11, Pallas kernels: 3.66 us -> 3.66 us  [call(): pl.pallas_call(body, out_shape=[jax.ShapeDtypeStruct(*out) for out in out...]
where the time goes in v7:
time: 34.6 us; the launch traced here: 34.3 us
  starting transfers between devices  18.7 us (54%)
  waiting for transfers between devices  8.45 us (24%)
  Pallas kernels  3.66 us (11%)
  between operations  1.45 us (4%)
  local copies, waits for them, and re-layouts  1.39 us (4%)
  other arithmetic  0.63 us (2%)
    ppermute x3, starting transfers between devices, paired(): lax.ppermute(block, 'blk', to_chips(step))  5.8 us
    ppermute x3, starting transfers between devices, paired(): arrived.append(lax.ppermute(sent, 'blk', to_chips(step)))  5.61 us
    pallas_call x11, Pallas kernels, call(): pl.pallas_call(body, out_shape=[jax.ShapeDtypeStruct(*out) for out in out...  3.66 us
    ppermute x1, starting transfers between devices, paired(): q_far = lax.ppermute(q_own, 'rows', across)  3 us
    ppermute x3, waiting for transfers between devices, paired(): lax.ppermute(block, 'blk', to_chips(step))  2.78 us
    ppermute x3, waiting for transfers between devices, paired(): arrived.append(lax.ppermute(sent, 'blk', to_chips(step)))  2.47 us
    ppermute x1, starting transfers between devices, paired(): far_notes = lax.ppermute(notes, 'rows', across)  1.52 us
    unnamed x10, local copies, waits for them, and re-layouts  1.39 us
  transfers between devices with their start and end apart: 20, of which 10 were waited for; matrix products, arithmetic and copies ran while one was open for 0% of the time, Pallas kernels for 7%

profile of v7, /device:TPU:0, one launch (start us, length us, event | category | flops | bytes accessed | tf_op | source)
XLA Modules:
  0.0 34.3 jit_solution(8537481331547521443)
XLA Ops:
  0.6 3.0 %collective-permute-start = (bf16[32,256]{1,0:T(8,128)(2,1)}, bf16[32,256]{1,0:T(8,128)(2,1)S(1)}, u32[]{:S(2)}, u32[]{:S(2)}) collective-permute-start(bf16[32,256]{1,0:T(8,128)(2,1)} %bitcast.10), channel_id=1, source_target_pairs={{0,1},{1,0},{2,3},{3,2},{4,5},{5,4},{6,7},{7,6},{8,9},{9,8},{10,11... | collective-permute-start | bytes 49160 | tf_op jit(solution)/shard_map/ppermute | solution.py:198
  3.6 0.1 collective-permute-start.10
  4.4 0.6 %copy-done.2 = s32[1,1,20]{2,1,0:T(1,128)S(1)} copy-done((s32[1,1,20]{2,1,0:T(1,128)S(1)}, s32[1,1,20]{2,1,0:T(1,128)}, u32[]{:S(2)}) %copy-start.2) | copy-done | bytes 104
  5.0 0.0 copy-done.3
  5.0 0.0 copy-done.4
  5.1 0.7 %copy-done.1 = bf16[1,32,256]{2,1,0:T(8,128)(2,1)S(1)} copy-done((bf16[1,32,256]{2,1,0:T(8,128)(2,1)S(1)}, bf16[1,32,256]{2,1,0:T(8,128)(2,1)}, u32[]{:S(2)}) %copy-start.1) | copy-done | bytes 16408
  5.8 0.0 collective-permute-done.q_far
  5.8 0.0 copy-start
  5.8 0.1 collective-permute-start.1
  5.9 1.2 %collective-permute-done.1 = bf16[64,256]{1,0:T(8,128)(2,1)S(1)} collective-permute-done((bf16[64,256]{1,0:T(8,128)(2,1)S(1)}, bf16[64,256]{1,0:T(8,128)(2,1)S(1)}, u32[]{:S(2)}, u32[]{:S(2)}) %collective-permute-start.1) | collective-permute-done | bytes 32800 | tf_op jit(solution)/shard_map/ppermute | solution.py:219
  7.1 5.0 %collective-permute-start.5 = (bf16[128,256]{1,0:T(8,128)(2,1)S(1)}, bf16[128,256]{1,0:T(8,128)(2,1)S(1)}, u32[]{:S(2)}, u32[]{:S(2)}) collective-permute-start(bf16[128,256]{1,0:T(8,128)(2,1)S(1)} %pad_maximum_fusion.refs_0_), channel_id=1, source_target_pairs={{0,28},{2,26},{4,24},{6,30},{8,20},{10,18},{12,16},{14,22},{16,12}... | collective-permute-start | bytes 196616 | tf_op jit(solution)/shard_map/ppermute | solution.py:220
  12.1 0.0 collective-permute-start.4
  12.1 0.8 %collective-permute-start.3 = (bf16[128,256]{1,0:T(8,128)(2,1)S(1)}, bf16[128,256]{1,0:T(8,128)(2,1)S(1)}, u32[]{:S(2)}, u32[]{:S(2)}) collective-permute-start(bf16[128,256]{1,0:T(8,128)(2,1)S(1)} %pad_maximum_fusion.refs_0_), channel_id=1, source_target_pairs={{0,8},{2,14},{4,12},{6,10},{8,0},{10,6},{12,4},{14,2},{16,24},{18,... | collective-permute-start | bytes 196616 | tf_op jit(solution)/shard_map/ppermute | solution.py:220
  12.9 0.4 %collective-permute-start.2 = (bf16[128,256]{1,0:T(8,128)(2,1)S(1)}, bf16[128,256]{1,0:T(8,128)(2,1)S(1)}, u32[]{:S(2)}, u32[]{:S(2)}) collective-permute-start(bf16[128,256]{1,0:T(8,128)(2,1)S(1)} %pad_maximum_fusion.refs_0_), channel_id=1, source_target_pairs={{0,4},{2,6},{4,0},{6,2},{8,12},{10,14},{12,8},{14,10},{16,20},{18,... | collective-permute-start | bytes 196616 | tf_op jit(solution)/shard_map/ppermute | solution.py:221
  13.3 1.5 %collective-permute-done.5.refs_4_ = bf16[128,256]{1,0:T(8,128)(2,1)S(1)} collective-permute-done((bf16[128,256]{1,0:T(8,128)(2,1)S(1)}, bf16[128,256]{1,0:T(8,128)(2,1)S(1)}, u32[]{:S(2)}, u32[]{:S(2)}) %collective-permute-start.5) | collective-permute-done | bytes 65568 | tf_op jit(solution)/shard_map/ppermute | solution.py:220
  14.8 1.5 %collective-permute-start.9 = (s32[8,128]{1,0:T(8,128)S(1)}, s32[8,128]{1,0:T(8,128)S(1)}, u32[]{:S(2)}, u32[]{:S(2)}) collective-permute-start(s32[8,128]{1,0:T(8,128)S(1)} %get-tuple-element.24.refs_8_.notes.refs_1_), channel_id=1, source_target_pairs={{0,1},{1,0},{2,3},{3,2},{4,5},{5,4},{6,7},{7,6},{8,9},{9,8},{10,11... | collective-permute-start | bytes 12296 | tf_op jit(solution)/shard_map/ppermute | solution.py:232
  16.3 1.3 %collective-permute-done.4.refs_3_ = bf16[128,256]{1,0:T(8,128)(2,1)S(1)} collective-permute-done((bf16[128,256]{1,0:T(8,128)(2,1)S(1)}, bf16[128,256]{1,0:T(8,128)(2,1)S(1)}, u32[]{:S(2)}, u32[]{:S(2)}) %collective-permute-start.4) | collective-permute-done | bytes 65568 | tf_op jit(solution)/shard_map/ppermute | solution.py:220
  17.6 0.0 collective-permute-start.8
  17.6 0.0 collective-permute-done.3.refs_2_
  17.6 0.5 %collective-permute-start.7 = (bf16[128,256]{1,0:T(8,128)(2,1)S(1)}, bf16[128,256]{1,0:T(8,128)(2,1)S(1)}, u32[]{:S(2)}, u32[]{:S(2)}) collective-permute-start(bf16[128,256]{1,0:T(8,128)(2,1)S(1)} %collective-permute-done.4.refs_3_), channel_id=1, source_target_pairs={{0,2},{2,0},{4,6},{6,4},{8,10},{10,8},{12,14},{14,12},{16,18},{18,... | collective-permute-start | bytes 196616 | tf_op jit(solution)/shard_map/ppermute | solution.py:233
  18.1 0.0 collective-permute-done.2.refs_1_
  18.1 0.1 collective-permute-start.6
  18.2 0.7 %turned.1 = (bf16[512,512]{1,0:T(8,128)(2,1)S(1)}, bf16[512,512]{1,0:T(8,128)(2,1)S(1)}) custom-call(s32[8,128]{1,0:T(8,128)S(1)} %get-tuple-element.24.refs_8_.notes.refs_1_, bf16[20,128,128]{2,1,0:T(8,128)(2,1)S(1)} %bitcast.8), custom_call_target="tpu_custom_call" | custom-call | flops 2147483648 | tf_op jit(solution)/shard_map/turned/pallas_call | solution.py:184
  18.9 0.0 collective-permute-done.8.refs_7_
  18.9 0.1 collective-permute-done.7.refs_6_
  19.0 0.4 %collective-permute-done.6.refs_5_ = bf16[128,256]{1,0:T(8,128)(2,1)S(1)} collective-permute-done((bf16[128,256]{1,0:T(8,128)(2,1)S(1)}, bf16[128,256]{1,0:T(8,128)(2,1)S(1)}, u32[]{:S(2)}, u32[]{:S(2)}) %collective-permute-start.6) | collective-permute-done | bytes 65568 | tf_op jit(solution)/shard_map/ppermute | solution.py:233
  19.4 0.7 %near_products.1 = (f32[512,256]{1,0:T(8,128)S(1)}, bf16[512,256]{1,0:T(8,128)(2,1)S(1)}) custom-call(bf16[128,256]{1,0:T(8,128)(2,1)S(1)} %pad_maximum_fusion.refs_0_, bf16[128,256]{1,0:T(8,128)(2,1)S(1)} %collective-permute-done.2.refs_1_, bf16[128,256]{1,0:T(8,128)(2,1)S(1)} %collective-permute-done.3.refs_2_, ...), custom_call_target="tpu_custom_call" | custom-call | flops 1 | tf_op jit(solution)/shard_map/near_products/pallas_call | solution.py:184
  20.0 0.1 collective-permute-done.9.refs_2_
  20.1 0.0 collective-permute-done.10.refs_3_
  20.1 1.1 %products.1 = (bf16[512,256]{1,0:T(8,128)(2,1)S(1)}, f32[512,256]{1,0:T(8,128)S(1)}, f32[64,256]{1,0:T(8,128)S(1)}, f32[64,256]{1,0:T(8,128)S(1)}, f32[64,256]{1,0:T(8,128)S(1)}, /*index=5*/f32[64,256]{1,0:T(8,128)S(1)}) custom-call(f32[512,256]{1,0:T(8,128)S(1)} %get-tuple-element.26.refs_0_, bf16[512,256]{1,0:T(8,128)(2,1)S(1)} %get-tuple-element.27.refs_1_, ...), custom_call_target="tpu_custom_call" | custom-call | tf_op jit(solution)/shard_map/products/pallas_call | solution.py:184
  21.3 0.2 collective-permute-start.13
  21.4 0.4 %collective-permute-start.11 = (f32[64,256]{1,0:T(8,128)S(1)}, f32[64,256]{1,0:T(8,128)S(1)}, u32[]{:S(2)}, u32[]{:S(2)}) collective-permute-start(f32[64,256]{1,0:T(8,128)S(1)} %get-tuple-element.31), channel_id=1, source_target_pairs={{0,2},{2,0},{4,6},{6,4},{8,10},{10,8},{12,14},{14,12},{16,18},{18,... | collective-permute-start | bytes 196616 | tf_op jit(solution)/shard_map/ppermute | solution.py:251
  21.8 0.1 collective-permute-start.15
  21.9 0.4 %collective-permute-start.17 = (f32[64,256]{1,0:T(8,128)S(1)}, f32[64,256]{1,0:T(8,128)S(1)}, u32[]{:S(2)}, u32[]{:S(2)}) collective-permute-start(f32[64,256]{1,0:T(8,128)S(1)} %get-tuple-element.39), channel_id=1, source_target_pairs={{0,2},{2,0},{4,6},{6,4},{8,10},{10,8},{12,14},{14,12},{16,18},{18,... | collective-permute-start | bytes 196616 | tf_op jit(solution)/shard_map/ppermute | solution.py:251
  22.3 0.2 collective-permute-done.13.refs_1_
  22.6 4.7 %collective-permute-start.14 = (s16[80,256]{1,0:T(8,128)(2,1)S(1)}, s16[80,256]{1,0:T(8,128)(2,1)S(1)}, u32[]{:S(2)}, u32[]{:S(2)}) collective-permute-start(s16[80,256]{1,0:T(8,128)(2,1)S(1)} %coded.4), channel_id=1, source_target_pairs={{0,28},{2,26},{4,24},{6,30},{8,20},{10,18},{12,16},{14,22},{16,12}... | collective-permute-start | bytes 122888 | tf_op jit(solution)/shard_map/ppermute | solution.py:260
  27.3 0.0 collective-permute-done.11.refs_1_
  27.4 0.1 collective-permute-start.12
  27.5 0.8 %collective-permute-start.16 = (s16[80,256]{1,0:T(8,128)(2,1)S(1)}, s16[80,256]{1,0:T(8,128)(2,1)S(1)}, u32[]{:S(2)}, u32[]{:S(2)}) collective-permute-start(s16[80,256]{1,0:T(8,128)(2,1)S(1)} %coded.5), channel_id=1, source_target_pairs={{0,8},{2,14},{4,12},{6,10},{8,0},{10,6},{12,4},{14,2},{16,24},{18,... | collective-permute-start | bytes 122888 | tf_op jit(solution)/shard_map/ppermute | solution.py:260
  28.3 0.0 collective-permute-done.17.refs_1_
  28.4 0.5 %collective-permute-start.19 = (f32[32,256]{1,0:T(8,128)S(1)}, f32[32,256]{1,0:T(8,128)S(1)}, u32[]{:S(2)}, u32[]{:S(2)}) collective-permute-start(f32[32,256]{1,0:T(8,128)S(1)} %slice.4), channel_id=1, source_target_pairs={{0,4},{2,6},{4,0},{6,2},{8,12},{10,14},{12,8},{14,10},{16,20},{18,... | collective-permute-start | bytes 98312 | tf_op jit(solution)/shard_map/ppermute | solution.py:267
  28.8 0.5 %collective-permute-done.14.refs_0_ = s16[80,256]{1,0:T(8,128)(2,1)S(1)} collective-permute-done((s16[80,256]{1,0:T(8,128)(2,1)S(1)}, s16[80,256]{1,0:T(8,128)(2,1)S(1)}, u32[]{:S(2)}, u32[]{:S(2)}) %collective-permute-start.14) | collective-permute-done | bytes 40992 | tf_op jit(solution)/shard_map/ppermute | solution.py:260
  29.4 1.0 %owned.1 = bf16[256,256]{1,0:T(8,128)(2,1)} custom-call(bf16[512,256]{1,0:T(8,128)(2,1)S(1)} %get-tuple-element.34.refs_0_, s32[8,128]{1,0:T(8,128)S(1)} %get-tuple-element.24.refs_8_.notes.refs_1_), custom_call_target="tpu_custom_call" | custom-call | tf_op jit(solution)/shard_map/owned/pallas_call | solution.py:184
  30.4 1.9 %collective-permute-done.12.refs_1_ = s16[80,256]{1,0:T(8,128)(2,1)S(1)} collective-permute-done((s16[80,256]{1,0:T(8,128)(2,1)S(1)}, s16[80,256]{1,0:T(8,128)(2,1)S(1)}, u32[]{:S(2)}, u32[]{:S(2)}) %collective-permute-start.12) | collective-permute-done | bytes 40992 | tf_op jit(solution)/shard_map/ppermute | solution.py:260
  32.3 0.0 collective-permute-done.16.refs_2_
  32.4 0.1 collective-permute-start.18
  32.5 1.2 %collective-permute-done.18 = f32[32,256]{1,0:T(8,128)S(1)} collective-permute-done((f32[32,256]{1,0:T(8,128)S(1)}, f32[32,256]{1,0:T(8,128)S(1)}, u32[]{:S(2)}, u32[]{:S(2)}) %collective-permute-start.18) | collective-permute-done | bytes 32800 | tf_op jit(solution)/shard_map/ppermute | solution.py:282
  33.7 0.6 %add_bitcast_fusion = f32[1,32,256]{2,1,0:T(8,128)} fusion(f32[32,256]{1,0:T(8,128)S(1)} %get-tuple-element.40, f32[32,256]{1,0:T(8,128)S(1)} %collective-permute-done.18, f32[32,256]{1,0:T(8,128)S(1)} %collective-permute-done.19), kind=kLoop, calls=%fused_computation.1 | loop fusion | flops 16384 | bytes 131072 | tf_op jit(solution)/shard_map/broadcast_in_dim | solution.py:283
  (16 shorter events, 0.2 us)
Async XLA Ops:
  0.6 5.2 %collective-permute-start = (bf16[32,256]{1,0:T(8,128)(2,1)}, bf16[32,256]{1,0:T(8,128)(2,1)S(1)}, u32[]{:S(2)}, u32[]{:S(2)}) collective-permute-start(bf16[32,256]{1,0:T(8,128)(2,1)} %bitcast.10), channel_id=1, source_target_pairs={{0,1},{1,0},{2,3},{3,2},{4,5},{5,4},{6,7},{7,6},{8,9},{9,8},{10,11... | collective-permute-start | bytes 49160 | tf_op jit(solution)/shard_map/ppermute | solution.py:198
  3.6 16.5 %collective-permute-start.10 = (bf16[20,128,128]{2,1,0:T(8,128)(2,1)}, bf16[20,128,128]{2,1,0:T(8,128)(2,1)S(1)}, u32[]{:S(2)}, u32[]{:S(2)}) collective-permute-start(bf16[20,128,128]{2,1,0:T(8,128)(2,1)} %bitcast.7), channel_id=1, source_target_pairs={{0,1},{1,0},{2,3},{3,2},{4,5},{5,4},{6,7},{7,6},{8,9},{9,8},{10,11... | collective-permute-start | bytes 1966088 | tf_op jit(solution)/shard_map/ppermute | solution.py:199
  4.4 0.7 %copy-start.2 = (s32[1,1,20]{2,1,0:T(1,128)S(1)}, s32[1,1,20]{2,1,0:T(1,128)}, u32[]{:S(2)}) copy-start(s32[1,1,20]{2,1,0:T(1,128)} %param.8) | copy-start | bytes 244
  4.4 0.7 %copy-start.3 = (s32[1,1,20,1]{2,3,1,0:T(1,128)S(1)}, s32[1,1,20,1]{2,3,1,0:T(1,128)}, u32[]{:S(2)}) copy-start(s32[1,1,20,1]{2,3,1,0:T(1,128)} %param.9) | copy-start | bytes 244
  4.4 0.7 %copy-start.4 = (s32[1,4]{1,0:T(1,128)S(1)}, s32[1,4]{1,0:T(1,128)}, u32[]{:S(2)}) copy-start(s32[1,4]{1,0:T(1,128)} %owners.1) | copy-start | bytes 52
  5.1 0.7 %copy-start.1 = (bf16[1,32,256]{2,1,0:T(8,128)(2,1)S(1)}, bf16[1,32,256]{2,1,0:T(8,128)(2,1)}, u32[]{:S(2)}) copy-start(bf16[1,32,256]{2,1,0:T(8,128)(2,1)} %param.6) | copy-start | bytes 49156
  5.8 12.4 %copy-start = (bf16[1,1,20,128,128]{4,3,2,1,0:T(8,128)(2,1)S(1)}, bf16[1,1,20,128,128]{4,3,2,1,0:T(8,128)(2,1)}, u32[]{:S(2)}) copy-start(bf16[1,1,20,128,128]{4,3,2,1,0:T(8,128)(2,1)} %param.7) | copy-start | bytes 1966084
  5.8 1.3 %collective-permute-start.1 = (bf16[64,256]{1,0:T(8,128)(2,1)S(1)}, bf16[64,256]{1,0:T(8,128)(2,1)S(1)}, u32[]{:S(2)}, u32[]{:S(2)}) collective-permute-start(bf16[64,256]{1,0:T(8,128)(2,1)S(1)} %pair.1), channel_id=1, source_target_pairs={{0,2},{2,0},{4,6},{6,4},{8,10},{10,8},{12,14},{14,12},{16,18},{18,... | collective-permute-start | bytes 98312 | tf_op jit(solution)/shard_map/ppermute | solution.py:219
  7.1 7.7 %collective-permute-start.5 = (bf16[128,256]{1,0:T(8,128)(2,1)S(1)}, bf16[128,256]{1,0:T(8,128)(2,1)S(1)}, u32[]{:S(2)}, u32[]{:S(2)}) collective-permute-start(bf16[128,256]{1,0:T(8,128)(2,1)S(1)} %pad_maximum_fusion.refs_0_), channel_id=1, source_target_pairs={{0,28},{2,26},{4,24},{6,30},{8,20},{10,18},{12,16},{14,22},{16,12}... | collective-permute-start | bytes 196616 | tf_op jit(solution)/shard_map/ppermute | solution.py:220
  12.1 5.5 %collective-permute-start.4 = (bf16[128,256]{1,0:T(8,128)(2,1)S(1)}, bf16[128,256]{1,0:T(8,128)(2,1)S(1)}, u32[]{:S(2)}, u32[]{:S(2)}) collective-permute-start(bf16[128,256]{1,0:T(8,128)(2,1)S(1)} %pad_maximum_fusion.refs_0_), channel_id=1, source_target_pairs={{0,16},{2,22},{4,20},{6,18},{8,24},{10,30},{12,28},{14,26},{16,0},... | collective-permute-start | bytes 196616 | tf_op jit(solution)/shard_map/ppermute | solution.py:220
  12.1 5.5 %collective-permute-start.3 = (bf16[128,256]{1,0:T(8,128)(2,1)S(1)}, bf16[128,256]{1,0:T(8,128)(2,1)S(1)}, u32[]{:S(2)}, u32[]{:S(2)}) collective-permute-start(bf16[128,256]{1,0:T(8,128)(2,1)S(1)} %pad_maximum_fusion.refs_0_), channel_id=1, source_target_pairs={{0,8},{2,14},{4,12},{6,10},{8,0},{10,6},{12,4},{14,2},{16,24},{18,... | collective-permute-start | bytes 196616 | tf_op jit(solution)/shard_map/ppermute | solution.py:220
  12.9 5.2 %collective-permute-start.2 = (bf16[128,256]{1,0:T(8,128)(2,1)S(1)}, bf16[128,256]{1,0:T(8,128)(2,1)S(1)}, u32[]{:S(2)}, u32[]{:S(2)}) collective-permute-start(bf16[128,256]{1,0:T(8,128)(2,1)S(1)} %pad_maximum_fusion.refs_0_), channel_id=1, source_target_pairs={{0,4},{2,6},{4,0},{6,2},{8,12},{10,14},{12,8},{14,10},{16,20},{18,... | collective-permute-start | bytes 196616 | tf_op jit(solution)/shard_map/ppermute | solution.py:221
  14.8 5.3 %collective-permute-start.9 = (s32[8,128]{1,0:T(8,128)S(1)}, s32[8,128]{1,0:T(8,128)S(1)}, u32[]{:S(2)}, u32[]{:S(2)}) collective-permute-start(s32[8,128]{1,0:T(8,128)S(1)} %get-tuple-element.24.refs_8_.notes.refs_1_), channel_id=1, source_target_pairs={{0,1},{1,0},{2,3},{3,2},{4,5},{5,4},{6,7},{7,6},{8,9},{9,8},{10,11... | collective-permute-start | bytes 12296 | tf_op jit(solution)/shard_map/ppermute | solution.py:232
  17.6 1.3 %collective-permute-start.8 = (bf16[128,256]{1,0:T(8,128)(2,1)S(1)}, bf16[128,256]{1,0:T(8,128)(2,1)S(1)}, u32[]{:S(2)}, u32[]{:S(2)}) collective-permute-start(bf16[128,256]{1,0:T(8,128)(2,1)S(1)} %collective-permute-done.5.refs_4_), channel_id=1, source_target_pairs={{0,2},{2,0},{4,6},{6,4},{8,10},{10,8},{12,14},{14,12},{16,18},{18,... | collective-permute-start | bytes 196616 | tf_op jit(solution)/shard_map/ppermute | solution.py:233
  17.6 1.4 %collective-permute-start.7 = (bf16[128,256]{1,0:T(8,128)(2,1)S(1)}, bf16[128,256]{1,0:T(8,128)(2,1)S(1)}, u32[]{:S(2)}, u32[]{:S(2)}) collective-permute-start(bf16[128,256]{1,0:T(8,128)(2,1)S(1)} %collective-permute-done.4.refs_3_), channel_id=1, source_target_pairs={{0,2},{2,0},{4,6},{6,4},{8,10},{10,8},{12,14},{14,12},{16,18},{18,... | collective-permute-start | bytes 196616 | tf_op jit(solution)/shard_map/ppermute | solution.py:233
  18.1 1.3 %collective-permute-start.6 = (bf16[128,256]{1,0:T(8,128)(2,1)S(1)}, bf16[128,256]{1,0:T(8,128)(2,1)S(1)}, u32[]{:S(2)}, u32[]{:S(2)}) collective-permute-start(bf16[128,256]{1,0:T(8,128)(2,1)S(1)} %collective-permute-done.3.refs_2_), channel_id=1, source_target_pairs={{0,2},{2,0},{4,6},{6,4},{8,10},{10,8},{12,14},{14,12},{16,18},{18,... | collective-permute-start | bytes 196616 | tf_op jit(solution)/shard_map/ppermute | solution.py:233
  21.3 1.3 %collective-permute-start.13 = (f32[64,256]{1,0:T(8,128)S(1)}, f32[64,256]{1,0:T(8,128)S(1)}, u32[]{:S(2)}, u32[]{:S(2)}) collective-permute-start(f32[64,256]{1,0:T(8,128)S(1)} %get-tuple-element.33), channel_id=1, source_target_pairs={{0,2},{2,0},{4,6},{6,4},{8,10},{10,8},{12,14},{14,12},{16,18},{18,... | collective-permute-start | bytes 196616 | tf_op jit(solution)/shard_map/ppermute | solution.py:251
  21.4 5.9 %collective-permute-start.11 = (f32[64,256]{1,0:T(8,128)S(1)}, f32[64,256]{1,0:T(8,128)S(1)}, u32[]{:S(2)}, u32[]{:S(2)}) collective-permute-start(f32[64,256]{1,0:T(8,128)S(1)} %get-tuple-element.31), channel_id=1, source_target_pairs={{0,2},{2,0},{4,6},{6,4},{8,10},{10,8},{12,14},{14,12},{16,18},{18,... | collective-permute-start | bytes 196616 | tf_op jit(solution)/shard_map/ppermute | solution.py:251
  21.8 5.6 %collective-permute-start.15 = (f32[64,256]{1,0:T(8,128)S(1)}, f32[64,256]{1,0:T(8,128)S(1)}, u32[]{:S(2)}, u32[]{:S(2)}) collective-permute-start(f32[64,256]{1,0:T(8,128)S(1)} %get-tuple-element.38), channel_id=1, source_target_pairs={{0,2},{2,0},{4,6},{6,4},{8,10},{10,8},{12,14},{14,12},{16,18},{18,... | collective-permute-start | bytes 196616 | tf_op jit(solution)/shard_map/ppermute | solution.py:251
  21.9 6.4 %collective-permute-start.17 = (f32[64,256]{1,0:T(8,128)S(1)}, f32[64,256]{1,0:T(8,128)S(1)}, u32[]{:S(2)}, u32[]{:S(2)}) collective-permute-start(f32[64,256]{1,0:T(8,128)S(1)} %get-tuple-element.39), channel_id=1, source_target_pairs={{0,2},{2,0},{4,6},{6,4},{8,10},{10,8},{12,14},{14,12},{16,18},{18,... | collective-permute-start | bytes 196616 | tf_op jit(solution)/shard_map/ppermute | solution.py:251
  22.6 6.8 %collective-permute-start.14 = (s16[80,256]{1,0:T(8,128)(2,1)S(1)}, s16[80,256]{1,0:T(8,128)(2,1)S(1)}, u32[]{:S(2)}, u32[]{:S(2)}) collective-permute-start(s16[80,256]{1,0:T(8,128)(2,1)S(1)} %coded.4), channel_id=1, source_target_pairs={{0,28},{2,26},{4,24},{6,30},{8,20},{10,18},{12,16},{14,22},{16,12}... | collective-permute-start | bytes 122888 | tf_op jit(solution)/shard_map/ppermute | solution.py:260
  27.4 5.0 %collective-permute-start.12 = (s16[80,256]{1,0:T(8,128)(2,1)S(1)}, s16[80,256]{1,0:T(8,128)(2,1)S(1)}, u32[]{:S(2)}, u32[]{:S(2)}) collective-permute-start(s16[80,256]{1,0:T(8,128)(2,1)S(1)} %coded.3), channel_id=1, source_target_pairs={{0,16},{2,22},{4,20},{6,18},{8,24},{10,30},{12,28},{14,26},{16,0},... | collective-permute-start | bytes 122888 | tf_op jit(solution)/shard_map/ppermute | solution.py:260
  27.5 4.8 %collective-permute-start.16 = (s16[80,256]{1,0:T(8,128)(2,1)S(1)}, s16[80,256]{1,0:T(8,128)(2,1)S(1)}, u32[]{:S(2)}, u32[]{:S(2)}) collective-permute-start(s16[80,256]{1,0:T(8,128)(2,1)S(1)} %coded.5), channel_id=1, source_target_pairs={{0,8},{2,14},{4,12},{6,10},{8,0},{10,6},{12,4},{14,2},{16,24},{18,... | collective-permute-start | bytes 122888 | tf_op jit(solution)/shard_map/ppermute | solution.py:260
  28.4 4.1 %collective-permute-start.19 = (f32[32,256]{1,0:T(8,128)S(1)}, f32[32,256]{1,0:T(8,128)S(1)}, u32[]{:S(2)}, u32[]{:S(2)}) collective-permute-start(f32[32,256]{1,0:T(8,128)S(1)} %slice.4), channel_id=1, source_target_pairs={{0,4},{2,6},{4,0},{6,2},{8,12},{10,14},{12,8},{14,10},{16,20},{18,... | collective-permute-start | bytes 98312 | tf_op jit(solution)/shard_map/ppermute | solution.py:267
  32.4 1.3 %collective-permute-start.18 = (f32[32,256]{1,0:T(8,128)S(1)}, f32[32,256]{1,0:T(8,128)S(1)}, u32[]{:S(2)}, u32[]{:S(2)}) collective-permute-start(f32[32,256]{1,0:T(8,128)S(1)} %get-tuple-element.41), channel_id=1, source_target_pairs={{0,2},{2,0},{4,6},{6,4},{8,10},{10,8},{12,14},{14,12},{16,18},{18,... | collective-permute-start | bytes 98312 | tf_op jit(solution)/shard_map/ppermute | solution.py:282

commit v8 on v6

--- a/solution.py
+++ b/solution.py
@@ -7,6 +7,7 @@
 
 
 LANES = 128
+NEXT = 2
 SCALE_ROWS = 16
 VMEM_BYTES = 24 << 20
 PAIR_COST, TURNED_COST = 1 << 35, 1 << 31
@@ -14,7 +15,8 @@
 
 def sides_of(chips):
     return tuple(
-        [k for k in reversed(range(2, chips)) if k.bit_count() % 2 == odd] for odd in (1, 0)
+        [k for k in reversed(range(1, chips)) if k != NEXT and k.bit_count() % 2 == odd]
+        for odd in (1, 0)
     )
 
 
@@ -101,7 +103,7 @@
             q_near[at, :] = ref[low : low + shard, :]
             q_far[at, :] = ref[low + shard : low + 2 * shard, :]
 
-    for ref, offset in ((block, 0), (beside, 1)):
+    for ref, offset in ((block, 0), (beside, NEXT)):
         put(ref, rows_at(offset, core), rows_at(offset, 1 - core))
     for step in range(rounds):
         for ref, side in ((direct[step], core), (relayed[step], 1 - core)):
@@ -135,7 +137,7 @@
             ref[shard : 2 * shard, :] = z[rows_of(step, side, 1 - side), :]
     for ref, side in ((keep[rounds], core), (give[rounds], 1 - core)):
         ref[0:shard, :] = z[rows_at(0, side), :]
-        ref[shard : 2 * shard, :] = z[rows_at(1, side), :]
+        ref[shard : 2 * shard, :] = z[rows_at(NEXT, side), :]
 
 
 def owned_kernel(group, y, notes, y_out):
@@ -163,7 +165,7 @@
     height = group * size
     across = [(0, 1), (1, 0)]
     sibling = [(i, i ^ 1) for i in range(devices)]
-    neighbour = [(i, i ^ 2) for i in range(devices)]
+    neighbour = [(i, i ^ (2 * NEXT)) for i in range(devices)]
     vmem = pl.BlockSpec(memory_space=pltpu.VMEM)
 
     def to_chips(step):

time: 34.6 us -> 34.6 us (level)
  transfers between devices with their start and end apart: 20 -> 20, of which waited for: 10 -> 9; matrix products, arithmetic and copies ran while one was open for 0% -> 0% of each run, Pallas kernels for 7% -> 7%
where the time goes in v8:
time: 34.6 us; the launch traced here: 34.4 us
  starting transfers between devices  18.7 us (54%)
  waiting for transfers between devices  8.49 us (25%)
  Pallas kernels  3.66 us (11%)
  between operations  1.46 us (4%)
  local copies, waits for them, and re-layouts  1.39 us (4%)
  other arithmetic  0.64 us (2%)
    ppermute x3, starting transfers between devices, paired(): lax.ppermute(block, 'blk', to_chips(step))  5.52 us
    ppermute x3, starting transfers between devices, paired(): arrived.append(lax.ppermute(sent, 'blk', to_chips(step)))  5.34 us
    pallas_call x10, Pallas kernels, call(): pl.pallas_call(body, out_shape=[jax.ShapeDtypeStruct(*out) for out in out...  3.66 us
    ppermute x1, starting transfers between devices, paired(): q_far = lax.ppermute(q_own, 'rows', across)  3 us
    ppermute x3, waiting for transfers between devices, paired(): lax.ppermute(block, 'blk', to_chips(step))  2.87 us
    ppermute x3, waiting for transfers between devices, paired(): arrived.append(lax.ppermute(sent, 'blk', to_chips(step)))  2.49 us
    ppermute x1, starting transfers between devices, paired(): far_notes = lax.ppermute(notes, 'rows', across)  1.52 us
    unnamed x10, local copies, waits for them, and re-layouts  1.39 us
  transfers between devices with their start and end apart: 20, of which 9 were waited for; matrix products, arithmetic and copies ran while one was open for 0% of the time, Pallas kernels for 7%

profile of v8, /device:TPU:0, one launch (start us, length us, event | category | flops | bytes accessed | tf_op | source)
XLA Modules:
  0.0 34.4 jit_solution(14023526611869919890)
XLA Ops:
  0.6 3.0 %collective-permute-start = (bf16[32,256]{1,0:T(8,128)(2,1)}, bf16[32,256]{1,0:T(8,128)(2,1)S(1)}, u32[]{:S(2)}, u32[]{:S(2)}) collective-permute-start(bf16[32,256]{1,0:T(8,128)(2,1)} %bitcast.10), channel_id=1, source_target_pairs={{0,1},{1,0},{2,3},{3,2},{4,5},{5,4},{6,7},{7,6},{8,9},{9,8},{10,11... | collective-permute-start | bytes 49160 | tf_op jit(solution)/shard_map/ppermute | solution.py:193
  3.6 0.1 collective-permute-start.10
  4.4 0.6 %copy-done.2 = s32[1,1,20]{2,1,0:T(1,128)S(1)} copy-done((s32[1,1,20]{2,1,0:T(1,128)S(1)}, s32[1,1,20]{2,1,0:T(1,128)}, u32[]{:S(2)}) %copy-start.2) | copy-done | bytes 104
  5.0 0.0 copy-done.3
  5.0 0.0 copy-done.4
  5.1 0.7 %copy-done.1 = bf16[1,32,256]{2,1,0:T(8,128)(2,1)S(1)} copy-done((bf16[1,32,256]{2,1,0:T(8,128)(2,1)S(1)}, bf16[1,32,256]{2,1,0:T(8,128)(2,1)}, u32[]{:S(2)}) %copy-start.1) | copy-done | bytes 16408
  5.8 0.0 collective-permute-done.q_far
  5.8 0.0 copy-start
  5.8 0.1 collective-permute-start.1
  5.9 1.2 %collective-permute-done.1 = bf16[64,256]{1,0:T(8,128)(2,1)S(1)} collective-permute-done((bf16[64,256]{1,0:T(8,128)(2,1)S(1)}, bf16[64,256]{1,0:T(8,128)(2,1)S(1)}, u32[]{:S(2)}, u32[]{:S(2)}) %collective-permute-start.1) | collective-permute-done | bytes 32800 | tf_op jit(solution)/shard_map/ppermute | solution.py:214
  7.1 5.0 %collective-permute-start.5 = (bf16[128,256]{1,0:T(8,128)(2,1)S(1)}, bf16[128,256]{1,0:T(8,128)(2,1)S(1)}, u32[]{:S(2)}, u32[]{:S(2)}) collective-permute-start(bf16[128,256]{1,0:T(8,128)(2,1)S(1)} %pad_maximum_fusion.refs_0_), channel_id=1, source_target_pairs={{0,28},{2,26},{4,24},{6,30},{8,20},{10,18},{12,16},{14,22},{16,12}... | collective-permute-start | bytes 196616 | tf_op jit(solution)/shard_map/ppermute | solution.py:215
  12.1 0.0 collective-permute-start.4
  12.1 0.5 %collective-permute-start.3 = (bf16[128,256]{1,0:T(8,128)(2,1)S(1)}, bf16[128,256]{1,0:T(8,128)(2,1)S(1)}, u32[]{:S(2)}, u32[]{:S(2)}) collective-permute-start(bf16[128,256]{1,0:T(8,128)(2,1)S(1)} %pad_maximum_fusion.refs_0_), channel_id=1, source_target_pairs={{0,4},{2,14},{4,0},{6,10},{8,12},{10,6},{12,8},{14,2},{16,20},{18,... | collective-permute-start | bytes 196616 | tf_op jit(solution)/shard_map/ppermute | solution.py:215
  12.6 0.7 %collective-permute-start.2 = (bf16[128,256]{1,0:T(8,128)(2,1)S(1)}, bf16[128,256]{1,0:T(8,128)(2,1)S(1)}, u32[]{:S(2)}, u32[]{:S(2)}) collective-permute-start(bf16[128,256]{1,0:T(8,128)(2,1)S(1)} %pad_maximum_fusion.refs_0_), channel_id=1, source_target_pairs={{0,8},{2,10},{4,12},{6,14},{8,0},{10,2},{12,4},{14,6},{16,24},{18,... | collective-permute-start | bytes 196616 | tf_op jit(solution)/shard_map/ppermute | solution.py:216
  13.3 1.5 %collective-permute-done.5.refs_4_ = bf16[128,256]{1,0:T(8,128)(2,1)S(1)} collective-permute-done((bf16[128,256]{1,0:T(8,128)(2,1)S(1)}, bf16[128,256]{1,0:T(8,128)(2,1)S(1)}, u32[]{:S(2)}, u32[]{:S(2)}) %collective-permute-start.5) | collective-permute-done | bytes 65568 | tf_op jit(solution)/shard_map/ppermute | solution.py:215
  14.8 1.5 %collective-permute-start.9 = (s32[8,128]{1,0:T(8,128)S(1)}, s32[8,128]{1,0:T(8,128)S(1)}, u32[]{:S(2)}, u32[]{:S(2)}) collective-permute-start(s32[8,128]{1,0:T(8,128)S(1)} %get-tuple-element.29.refs_8_.notes.refs_1_), channel_id=1, source_target_pairs={{0,1},{1,0},{2,3},{3,2},{4,5},{5,4},{6,7},{7,6},{8,9},{9,8},{10,11... | collective-permute-start | bytes 12296 | tf_op jit(solution)/shard_map/ppermute | solution.py:227
  16.3 1.4 %collective-permute-done.4.refs_3_ = bf16[128,256]{1,0:T(8,128)(2,1)S(1)} collective-permute-done((bf16[128,256]{1,0:T(8,128)(2,1)S(1)}, bf16[128,256]{1,0:T(8,128)(2,1)S(1)}, u32[]{:S(2)}, u32[]{:S(2)}) %collective-permute-start.4) | collective-permute-done | bytes 65568 | tf_op jit(solution)/shard_map/ppermute | solution.py:215
  17.7 0.0 collective-permute-start.8
  17.7 0.0 collective-permute-done.3.refs_2_
  17.7 0.5 %collective-permute-start.7 = (bf16[128,256]{1,0:T(8,128)(2,1)S(1)}, bf16[128,256]{1,0:T(8,128)(2,1)S(1)}, u32[]{:S(2)}, u32[]{:S(2)}) collective-permute-start(bf16[128,256]{1,0:T(8,128)(2,1)S(1)} %collective-permute-done.4.refs_3_), channel_id=1, source_target_pairs={{0,2},{2,0},{4,6},{6,4},{8,10},{10,8},{12,14},{14,12},{16,18},{18,... | collective-permute-start | bytes 196616 | tf_op jit(solution)/shard_map/ppermute | solution.py:228
  18.2 0.0 collective-permute-done.2.refs_1_
  18.2 0.1 collective-permute-start.6
  18.3 0.7 %turned.1 = (bf16[512,512]{1,0:T(8,128)(2,1)S(1)}, bf16[512,512]{1,0:T(8,128)(2,1)S(1)}) custom-call(s32[8,128]{1,0:T(8,128)S(1)} %get-tuple-element.29.refs_8_.notes.refs_1_, bf16[20,128,128]{2,1,0:T(8,128)(2,1)S(1)} %bitcast.8), custom_call_target="tpu_custom_call" | custom-call | flops 2147483648 | tf_op jit(solution)/shard_map/turned/pallas_call | solution.py:179
  19.0 0.0 collective-permute-done.8.refs_7_
  19.0 0.1 collective-permute-done.7.refs_6_
  19.1 0.4 %collective-permute-done.6.refs_5_ = bf16[128,256]{1,0:T(8,128)(2,1)S(1)} collective-permute-done((bf16[128,256]{1,0:T(8,128)(2,1)S(1)}, bf16[128,256]{1,0:T(8,128)(2,1)S(1)}, u32[]{:S(2)}, u32[]{:S(2)}) %collective-permute-start.6) | collective-permute-done | bytes 65568 | tf_op jit(solution)/shard_map/ppermute | solution.py:228
  19.5 0.7 %near_products.1 = (f32[512,256]{1,0:T(8,128)S(1)}, bf16[512,256]{1,0:T(8,128)(2,1)S(1)}) custom-call(bf16[128,256]{1,0:T(8,128)(2,1)S(1)} %pad_maximum_fusion.refs_0_, bf16[128,256]{1,0:T(8,128)(2,1)S(1)} %collective-permute-done.2.refs_1_, bf16[128,256]{1,0:T(8,128)(2,1)S(1)} %collective-permute-done.3.refs_2_, ...), custom_call_target="tpu_custom_call" | custom-call | flops 1 | tf_op jit(solution)/shard_map/near_products/pallas_call | solution.py:179
  20.1 0.0 collective-permute-done.9.refs_2_
  20.1 0.0 collective-permute-done.10.refs_3_
  20.1 1.1 %products.1 = (bf16[512,256]{1,0:T(8,128)(2,1)S(1)}, f32[64,256]{1,0:T(8,128)S(1)}, f32[64,256]{1,0:T(8,128)S(1)}, f32[64,256]{1,0:T(8,128)S(1)}, f32[64,256]{1,...) custom-call(f32[512,256]{1,0:T(8,128)S(1)} %get-tuple-element.31.ref, ...), custom_call_target="tpu_custom_call" | custom-call | tf_op jit(solution)/shard_map/products/pallas_call | solution.py:179
  21.3 0.2 collective-permute-start.13
  21.5 0.4 %collective-permute-start.11 = (f32[64,256]{1,0:T(8,128)S(1)}, f32[64,256]{1,0:T(8,128)S(1)}, u32[]{:S(2)}, u32[]{:S(2)}) collective-permute-start(f32[64,256]{1,0:T(8,128)S(1)} %get-tuple-element.36), channel_id=1, source_target_pairs={{0,2},{2,0},{4,6},{6,4},{8,10},{10,8},{12,14},{14,12},{16,18},{18,... | collective-permute-start | bytes 196616 | tf_op jit(solution)/shard_map/ppermute | solution.py:247
  21.9 0.2 collective-permute-start.15
  22.0 0.4 %collective-permute-start.17 = (f32[64,256]{1,0:T(8,128)S(1)}, f32[64,256]{1,0:T(8,128)S(1)}, u32[]{:S(2)}, u32[]{:S(2)}) collective-permute-start(f32[64,256]{1,0:T(8,128)S(1)} %get-tuple-element.47), channel_id=1, source_target_pairs={{0,2},{2,0},{4,6},{6,4},{8,10},{10,8},{12,14},{14,12},{16,18},{18,... | collective-permute-start | bytes 196616 | tf_op jit(solution)/shard_map/ppermute | solution.py:247
  22.4 0.2 collective-permute-done.13.given
  22.7 4.7 %collective-permute-start.14 = (s16[80,256]{1,0:T(8,128)(2,1)S(1)}, s16[80,256]{1,0:T(8,128)(2,1)S(1)}, u32[]{:S(2)}, u32[]{:S(2)}) collective-permute-start(s16[80,256]{1,0:T(8,128)(2,1)S(1)} %coded.4), channel_id=1, source_target_pairs={{0,28},{2,26},{4,24},{6,30},{8,20},{10,18},{12,16},{14,22},{16,12}... | collective-permute-start | bytes 122888 | tf_op jit(solution)/shard_map/ppermute | solution.py:256
  27.4 0.1 collective-permute-start.12
  27.5 0.0 collective-permute-done.15.given
  27.5 0.6 %collective-permute-start.16 = (s16[80,256]{1,0:T(8,128)(2,1)S(1)}, s16[80,256]{1,0:T(8,128)(2,1)S(1)}, u32[]{:S(2)}, u32[]{:S(2)}) collective-permute-start(s16[80,256]{1,0:T(8,128)(2,1)S(1)} %coded.5), channel_id=1, source_target_pairs={{0,4},{2,14},{4,0},{6,10},{8,12},{10,6},{12,8},{14,2},{16,20},{18,... | collective-permute-start | bytes 122888 | tf_op jit(solution)/shard_map/ppermute | solution.py:256
  28.1 0.0 collective-permute-done.17
  28.1 0.8 %collective-permute-start.19 = (f32[32,256]{1,0:T(8,128)S(1)}, f32[32,256]{1,0:T(8,128)S(1)}, u32[]{:S(2)}, u32[]{:S(2)}) collective-permute-start(f32[32,256]{1,0:T(8,128)S(1)} %slice.4), channel_id=1, source_target_pairs={{0,8},{2,10},{4,12},{6,14},{8,0},{10,2},{12,4},{14,6},{16,24},{18,... | collective-permute-start | bytes 98312 | tf_op jit(solution)/shard_map/ppermute | solution.py:258
  28.9 0.5 %collective-permute-done.14.refs_0_ = s16[80,256]{1,0:T(8,128)(2,1)S(1)} collective-permute-done((s16[80,256]{1,0:T(8,128)(2,1)S(1)}, s16[80,256]{1,0:T(8,128)(2,1)S(1)}, u32[]{:S(2)}, u32[]{:S(2)}) %collective-permute-start.14) | collective-permute-done | bytes 40992 | tf_op jit(solution)/shard_map/ppermute | solution.py:256
  29.4 1.0 %owned.1 = bf16[256,256]{1,0:T(8,128)(2,1)} custom-call(bf16[512,256]{1,0:T(8,128)(2,1)S(1)} %get-tuple-element.40.refs_0_, s32[8,128]{1,0:T(8,128)S(1)} %get-tuple-element.29.refs_8_.notes.refs_1_), custom_call_target="tpu_custom_call" | custom-call | tf_op jit(solution)/shard_map/owned/pallas_call | solution.py:179
  30.5 2.0 %collective-permute-done.12.refs_1_ = s16[80,256]{1,0:T(8,128)(2,1)S(1)} collective-permute-done((s16[80,256]{1,0:T(8,128)(2,1)S(1)}, s16[80,256]{1,0:T(8,128)(2,1)S(1)}, u32[]{:S(2)}, u32[]{:S(2)}) %collective-permute-start.12) | collective-permute-done | bytes 40992 | tf_op jit(solution)/shard_map/ppermute | solution.py:256
  32.5 0.1 collective-permute-start.18
  32.5 0.0 collective-permute-done.19
  32.6 1.2 %collective-permute-done.18 = f32[32,256]{1,0:T(8,128)S(1)} collective-permute-done((f32[32,256]{1,0:T(8,128)S(1)}, f32[32,256]{1,0:T(8,128)S(1)}, u32[]{:S(2)}, u32[]{:S(2)}) %collective-permute-start.18) | collective-permute-done | bytes 32800 | tf_op jit(solution)/shard_map/ppermute | solution.py:273
  33.7 0.6 %add_bitcast_fusion = f32[1,32,256]{2,1,0:T(8,128)} fusion(f32[32,256]{1,0:T(8,128)S(1)} %get-tuple-element.48, f32[32,256]{1,0:T(8,128)S(1)} %collective-permute-done.18, f32[32,256]{1,0:T(8,128)S(1)} %collective-permute-done.19), kind=kLoop, calls=%fused_computation.1 | loop fusion | flops 16384 | bytes 131072 | tf_op jit(solution)/shard_map/broadcast_in_dim | solution.py:274
  (16 shorter events, 0.2 us)
Async XLA Ops:
  0.6 5.2 %collective-permute-start = (bf16[32,256]{1,0:T(8,128)(2,1)}, bf16[32,256]{1,0:T(8,128)(2,1)S(1)}, u32[]{:S(2)}, u32[]{:S(2)}) collective-permute-start(bf16[32,256]{1,0:T(8,128)(2,1)} %bitcast.10), channel_id=1, source_target_pairs={{0,1},{1,0},{2,3},{3,2},{4,5},{5,4},{6,7},{7,6},{8,9},{9,8},{10,11... | collective-permute-start | bytes 49160 | tf_op jit(solution)/shard_map/ppermute | solution.py:193
  3.6 16.5 %collective-permute-start.10 = (bf16[20,128,128]{2,1,0:T(8,128)(2,1)}, bf16[20,128,128]{2,1,0:T(8,128)(2,1)S(1)}, u32[]{:S(2)}, u32[]{:S(2)}) collective-permute-start(bf16[20,128,128]{2,1,0:T(8,128)(2,1)} %bitcast.7), channel_id=1, source_target_pairs={{0,1},{1,0},{2,3},{3,2},{4,5},{5,4},{6,7},{7,6},{8,9},{9,8},{10,11... | collective-permute-start | bytes 1966088 | tf_op jit(solution)/shard_map/ppermute | solution.py:194
  4.4 0.7 %copy-start.2 = (s32[1,1,20]{2,1,0:T(1,128)S(1)}, s32[1,1,20]{2,1,0:T(1,128)}, u32[]{:S(2)}) copy-start(s32[1,1,20]{2,1,0:T(1,128)} %param.8) | copy-start | bytes 244
  4.4 0.7 %copy-start.3 = (s32[1,1,20,1]{2,3,1,0:T(1,128)S(1)}, s32[1,1,20,1]{2,3,1,0:T(1,128)}, u32[]{:S(2)}) copy-start(s32[1,1,20,1]{2,3,1,0:T(1,128)} %param.9) | copy-start | bytes 244
  4.4 0.7 %copy-start.4 = (s32[1,4]{1,0:T(1,128)S(1)}, s32[1,4]{1,0:T(1,128)}, u32[]{:S(2)}) copy-start(s32[1,4]{1,0:T(1,128)} %owners.1) | copy-start | bytes 52
  5.1 0.7 %copy-start.1 = (bf16[1,32,256]{2,1,0:T(8,128)(2,1)S(1)}, bf16[1,32,256]{2,1,0:T(8,128)(2,1)}, u32[]{:S(2)}) copy-start(bf16[1,32,256]{2,1,0:T(8,128)(2,1)} %param.6) | copy-start | bytes 49156
  5.8 12.5 %copy-start = (bf16[1,1,20,128,128]{4,3,2,1,0:T(8,128)(2,1)S(1)}, bf16[1,1,20,128,128]{4,3,2,1,0:T(8,128)(2,1)}, u32[]{:S(2)}) copy-start(bf16[1,1,20,128,128]{4,3,2,1,0:T(8,128)(2,1)} %param.7) | copy-start | bytes 1966084
  5.8 1.3 %collective-permute-start.1 = (bf16[64,256]{1,0:T(8,128)(2,1)S(1)}, bf16[64,256]{1,0:T(8,128)(2,1)S(1)}, u32[]{:S(2)}, u32[]{:S(2)}) collective-permute-start(bf16[64,256]{1,0:T(8,128)(2,1)S(1)} %pair.1), channel_id=1, source_target_pairs={{0,2},{2,0},{4,6},{6,4},{8,10},{10,8},{12,14},{14,12},{16,18},{18,... | collective-permute-start | bytes 98312 | tf_op jit(solution)/shard_map/ppermute | solution.py:214
  7.1 7.7 %collective-permute-start.5 = (bf16[128,256]{1,0:T(8,128)(2,1)S(1)}, bf16[128,256]{1,0:T(8,128)(2,1)S(1)}, u32[]{:S(2)}, u32[]{:S(2)}) collective-permute-start(bf16[128,256]{1,0:T(8,128)(2,1)S(1)} %pad_maximum_fusion.refs_0_), channel_id=1, source_target_pairs={{0,28},{2,26},{4,24},{6,30},{8,20},{10,18},{12,16},{14,22},{16,12}... | collective-permute-start | bytes 196616 | tf_op jit(solution)/shard_map/ppermute | solution.py:215
  12.1 5.6 %collective-permute-start.4 = (bf16[128,256]{1,0:T(8,128)(2,1)S(1)}, bf16[128,256]{1,0:T(8,128)(2,1)S(1)}, u32[]{:S(2)}, u32[]{:S(2)}) collective-permute-start(bf16[128,256]{1,0:T(8,128)(2,1)S(1)} %pad_maximum_fusion.refs_0_), channel_id=1, source_target_pairs={{0,16},{2,22},{4,20},{6,18},{8,24},{10,30},{12,28},{14,26},{16,0},... | collective-permute-start | bytes 196616 | tf_op jit(solution)/shard_map/ppermute | solution.py:215
  12.1 5.6 %collective-permute-start.3 = (bf16[128,256]{1,0:T(8,128)(2,1)S(1)}, bf16[128,256]{1,0:T(8,128)(2,1)S(1)}, u32[]{:S(2)}, u32[]{:S(2)}) collective-permute-start(bf16[128,256]{1,0:T(8,128)(2,1)S(1)} %pad_maximum_fusion.refs_0_), channel_id=1, source_target_pairs={{0,4},{2,14},{4,0},{6,10},{8,12},{10,6},{12,8},{14,2},{16,20},{18,... | collective-permute-start | bytes 196616 | tf_op jit(solution)/shard_map/ppermute | solution.py:215
  12.6 5.6 %collective-permute-start.2 = (bf16[128,256]{1,0:T(8,128)(2,1)S(1)}, bf16[128,256]{1,0:T(8,128)(2,1)S(1)}, u32[]{:S(2)}, u32[]{:S(2)}) collective-permute-start(bf16[128,256]{1,0:T(8,128)(2,1)S(1)} %pad_maximum_fusion.refs_0_), channel_id=1, source_target_pairs={{0,8},{2,10},{4,12},{6,14},{8,0},{10,2},{12,4},{14,6},{16,24},{18,... | collective-permute-start | bytes 196616 | tf_op jit(solution)/shard_map/ppermute | solution.py:216
  14.8 5.3 %collective-permute-start.9 = (s32[8,128]{1,0:T(8,128)S(1)}, s32[8,128]{1,0:T(8,128)S(1)}, u32[]{:S(2)}, u32[]{:S(2)}) collective-permute-start(s32[8,128]{1,0:T(8,128)S(1)} %get-tuple-element.29.refs_8_.notes.refs_1_), channel_id=1, source_target_pairs={{0,1},{1,0},{2,3},{3,2},{4,5},{5,4},{6,7},{7,6},{8,9},{9,8},{10,11... | collective-permute-start | bytes 12296 | tf_op jit(solution)/shard_map/ppermute | solution.py:227
  17.7 1.3 %collective-permute-start.8 = (bf16[128,256]{1,0:T(8,128)(2,1)S(1)}, bf16[128,256]{1,0:T(8,128)(2,1)S(1)}, u32[]{:S(2)}, u32[]{:S(2)}) collective-permute-start(bf16[128,256]{1,0:T(8,128)(2,1)S(1)} %collective-permute-done.5.refs_4_), channel_id=1, source_target_pairs={{0,2},{2,0},{4,6},{6,4},{8,10},{10,8},{12,14},{14,12},{16,18},{18,... | collective-permute-start | bytes 196616 | tf_op jit(solution)/shard_map/ppermute | solution.py:228
  17.7 1.4 %collective-permute-start.7 = (bf16[128,256]{1,0:T(8,128)(2,1)S(1)}, bf16[128,256]{1,0:T(8,128)(2,1)S(1)}, u32[]{:S(2)}, u32[]{:S(2)}) collective-permute-start(bf16[128,256]{1,0:T(8,128)(2,1)S(1)} %collective-permute-done.4.refs_3_), channel_id=1, source_target_pairs={{0,2},{2,0},{4,6},{6,4},{8,10},{10,8},{12,14},{14,12},{16,18},{18,... | collective-permute-start | bytes 196616 | tf_op jit(solution)/shard_map/ppermute | solution.py:228
  18.2 1.3 %collective-permute-start.6 = (bf16[128,256]{1,0:T(8,128)(2,1)S(1)}, bf16[128,256]{1,0:T(8,128)(2,1)S(1)}, u32[]{:S(2)}, u32[]{:S(2)}) collective-permute-start(bf16[128,256]{1,0:T(8,128)(2,1)S(1)} %collective-permute-done.3.refs_2_), channel_id=1, source_target_pairs={{0,2},{2,0},{4,6},{6,4},{8,10},{10,8},{12,14},{14,12},{16,18},{18,... | collective-permute-start | bytes 196616 | tf_op jit(solution)/shard_map/ppermute | solution.py:228
  21.3 1.3 %collective-permute-start.13 = (f32[64,256]{1,0:T(8,128)S(1)}, f32[64,256]{1,0:T(8,128)S(1)}, u32[]{:S(2)}, u32[]{:S(2)}) collective-permute-start(f32[64,256]{1,0:T(8,128)S(1)} %get-tuple-element.39), channel_id=1, source_target_pairs={{0,2},{2,0},{4,6},{6,4},{8,10},{10,8},{12,14},{14,12},{16,18},{18,... | collective-permute-start | bytes 196616 | tf_op jit(solution)/shard_map/ppermute | solution.py:247
  21.5 5.8 %collective-permute-start.11 = (f32[64,256]{1,0:T(8,128)S(1)}, f32[64,256]{1,0:T(8,128)S(1)}, u32[]{:S(2)}, u32[]{:S(2)}) collective-permute-start(f32[64,256]{1,0:T(8,128)S(1)} %get-tuple-element.36), channel_id=1, source_target_pairs={{0,2},{2,0},{4,6},{6,4},{8,10},{10,8},{12,14},{14,12},{16,18},{18,... | collective-permute-start | bytes 196616 | tf_op jit(solution)/shard_map/ppermute | solution.py:247
  21.9 5.6 %collective-permute-start.15 = (f32[64,256]{1,0:T(8,128)S(1)}, f32[64,256]{1,0:T(8,128)S(1)}, u32[]{:S(2)}, u32[]{:S(2)}) collective-permute-start(f32[64,256]{1,0:T(8,128)S(1)} %get-tuple-element.45), channel_id=1, source_target_pairs={{0,2},{2,0},{4,6},{6,4},{8,10},{10,8},{12,14},{14,12},{16,18},{18,... | collective-permute-start | bytes 196616 | tf_op jit(solution)/shard_map/ppermute | solution.py:247
  22.0 6.1 %collective-permute-start.17 = (f32[64,256]{1,0:T(8,128)S(1)}, f32[64,256]{1,0:T(8,128)S(1)}, u32[]{:S(2)}, u32[]{:S(2)}) collective-permute-start(f32[64,256]{1,0:T(8,128)S(1)} %get-tuple-element.47), channel_id=1, source_target_pairs={{0,2},{2,0},{4,6},{6,4},{8,10},{10,8},{12,14},{14,12},{16,18},{18,... | collective-permute-start | bytes 196616 | tf_op jit(solution)/shard_map/ppermute | solution.py:247
  22.7 6.8 %collective-permute-start.14 = (s16[80,256]{1,0:T(8,128)(2,1)S(1)}, s16[80,256]{1,0:T(8,128)(2,1)S(1)}, u32[]{:S(2)}, u32[]{:S(2)}) collective-permute-start(s16[80,256]{1,0:T(8,128)(2,1)S(1)} %coded.4), channel_id=1, source_target_pairs={{0,28},{2,26},{4,24},{6,30},{8,20},{10,18},{12,16},{14,22},{16,12}... | collective-permute-start | bytes 122888 | tf_op jit(solution)/shard_map/ppermute | solution.py:256
  27.4 5.0 %collective-permute-start.12 = (s16[80,256]{1,0:T(8,128)(2,1)S(1)}, s16[80,256]{1,0:T(8,128)(2,1)S(1)}, u32[]{:S(2)}, u32[]{:S(2)}) collective-permute-start(s16[80,256]{1,0:T(8,128)(2,1)S(1)} %coded.3), channel_id=1, source_target_pairs={{0,16},{2,22},{4,20},{6,18},{8,24},{10,30},{12,28},{14,26},{16,0},... | collective-permute-start | bytes 122888 | tf_op jit(solution)/shard_map/ppermute | solution.py:256
  27.5 4.9 %collective-permute-start.16 = (s16[80,256]{1,0:T(8,128)(2,1)S(1)}, s16[80,256]{1,0:T(8,128)(2,1)S(1)}, u32[]{:S(2)}, u32[]{:S(2)}) collective-permute-start(s16[80,256]{1,0:T(8,128)(2,1)S(1)} %coded.5), channel_id=1, source_target_pairs={{0,4},{2,14},{4,0},{6,10},{8,12},{10,6},{12,8},{14,2},{16,20},{18,... | collective-permute-start | bytes 122888 | tf_op jit(solution)/shard_map/ppermute | solution.py:256
  28.1 4.4 %collective-permute-start.19 = (f32[32,256]{1,0:T(8,128)S(1)}, f32[32,256]{1,0:T(8,128)S(1)}, u32[]{:S(2)}, u32[]{:S(2)}) collective-permute-start(f32[32,256]{1,0:T(8,128)S(1)} %slice.4), channel_id=1, source_target_pairs={{0,8},{2,10},{4,12},{6,14},{8,0},{10,2},{12,4},{14,6},{16,24},{18,... | collective-permute-start | bytes 98312 | tf_op jit(solution)/shard_map/ppermute | solution.py:258
  32.5 1.3 %collective-permute-start.18 = (f32[32,256]{1,0:T(8,128)S(1)}, f32[32,256]{1,0:T(8,128)S(1)}, u32[]{:S(2)}, u32[]{:S(2)}) collective-permute-start(f32[32,256]{1,0:T(8,128)S(1)} %get-tuple-element.49), channel_id=1, source_target_pairs={{0,2},{2,0},{4,6},{6,4},{8,10},{10,8},{12,14},{14,12},{16,18},{18,... | collective-permute-start | bytes 98312 | tf_op jit(solution)/shard_map/ppermute | solution.py:273
